TPU v7x, 32 devices: a whole 2x2x4 slice. The times are simulated.
32 devices in a mesh: seq: 2 (over x), batch: 16 (over z, y, core).
Axes of the slice: x: 2, y: 2, z: 4, core: 2. Of those that a mesh axis runs over, the one named last changes fastest.
Arguments:
- tokens: bfloat16 [32, 2048, 1024], P('batch', 'seq'), may hold values from -6 to 6
- cotangent: bfloat16 [32, 2048, 1024], P('batch', 'seq'), may hold values from -6 to 6
- lengths: int32 [32], P('batch'), may hold values from 256 to 2048, as said below
- routed: int32 [32, 256], P('batch'), may hold values from -1 to 2047, as said below
- w_qkv: bfloat16 [1024, 3072], P(('seq', 'batch')), may hold values from -0.1875 to 0.1875
- w_out: bfloat16 [1024, 1024], P(('seq', 'batch')), may hold values from -0.75 to 0.75
- w_up: bfloat16 [1024, 4096], P(('seq', 'batch')), may hold values from -0.1875 to 0.1875
- w_down: bfloat16 [4096, 1024], P(('seq', 'batch')), may hold values from -0.09375 to 0.09375
- gain_attn: bfloat16 [1024], P(('seq', 'batch')), may hold values from 0.099609375 to 1.8984375
- gain_mlp: bfloat16 [1024], P(('seq', 'batch')), may hold values from 0.099609375 to 1.8984375
- router: bfloat16 [1024], P(('seq', 'batch')), may hold values from -0.1875 to 0.1875
Outputs:
- output: bfloat16 [32, 2048, 1024], P('batch', 'seq')
- input_grad: bfloat16 [32, 2048, 1024], P('batch', 'seq')
- grad_qkv: float32 [1024, 3072], P(('seq', 'batch'))
- grad_out: float32 [1024, 1024], P(('seq', 'batch'))
- grad_up: float32 [1024, 4096], P(('seq', 'batch'))
- grad_down: float32 [4096, 1024], P(('seq', 'batch'))
- grad_gain_attn: float32 [1024], P(('seq', 'batch'))
- grad_gain_mlp: float32 [1024], P(('seq', 'batch'))
- grad_router: float32 [1024], P(('seq', 'batch'))
Inputs may be any that keep to these rules, and one draw needn't show every extreme that they name: `lengths`: multiples of 8; in every run of 2 slots along the first dimension one slot has length 2048. `routed`: for a slot of length n, entries 0 to n // 8 - 1 are distinct positions below n in rising order; the others are -1.
All inputs are finite; a program needn't handle non-finite values.
Results may differ from a plain program's by a relative error of at most 0.014.
Values may be sent and summed in bfloat16 or wider, within the bound.
A program may use at most 192 MiB of HBM per device.

v0:
```python
import jax
import jax.numpy as jnp
from jax import lax
from jax.sharding import PartitionSpec as P

HEAD_DIM = 64


epsilon = 1e-05
highest = lax.Precision.HIGHEST


def norm_apply(values_in, gain_vec):
    return (
        values_in
        * lax.rsqrt(jnp.mean(values_in * values_in, axis=-1, keepdims=True) + epsilon)
        * gain_vec
    )


def gelu_tanh(values_in):
    return jax.nn.gelu(values_in, approximate=True)


def per_device(
    tokens, cotangent, lengths, routed, w_qkv, w_out, w_up, w_down, gain_attn, gain_mlp, router
):
    slot_count, local_len, model_width = tokens.shape
    capacity = routed.shape[1]
    seq_devices = lax.axis_size("seq")
    own_count = capacity // seq_devices
    head_count = model_width // HEAD_DIM
    row_count = own_count * slot_count
    score_scale = HEAD_DIM ** (-0.5)
    f32 = jnp.float32
    bf16 = jnp.bfloat16
    gathered = (
        lax.all_gather(w_qkv, ("seq", "batch"), axis=0, tiled=True),
        lax.all_gather(w_out, ("seq", "batch"), axis=0, tiled=True),
        lax.all_gather(w_up, ("seq", "batch"), axis=0, tiled=True),
        lax.all_gather(w_down, ("seq", "batch"), axis=0, tiled=True),
        lax.all_gather(gain_attn, ("seq", "batch"), axis=0, tiled=True),
        lax.all_gather(gain_mlp, ("seq", "batch"), axis=0, tiled=True),
        lax.all_gather(router, ("seq", "batch"), axis=0, tiled=True),
    )
    full_qkv, full_out, full_up, full_down, full_ga, full_gm, full_router = gathered
    gain_one = full_ga.astype(f32)
    gain_two = full_gm.astype(f32)
    router_vec = full_router.astype(f32)
    counts = lengths // 8
    seq_place = lax.axis_index("seq")
    positions = seq_place * local_len + jnp.arange(local_len, dtype=jnp.int32)
    rank_all = jnp.arange(capacity, dtype=jnp.int32)
    live_all = rank_all[None, :] < counts[:, None]
    chooser = ((routed[:, :, None] == positions[None, None, :]) & live_all[:, :, None]).astype(bf16)
    pick_in = jnp.einsum("scp,spd->csd", chooser, tokens, preferred_element_type=f32)
    pick_cot = jnp.einsum("scp,spd->csd", chooser, cotangent, preferred_element_type=f32)
    picked, picked_cot = (
        lax.psum_scatter(
            pick_in.astype(jnp.bfloat16), "seq", scatter_dimension=0, tiled=True
        ).astype(jnp.float32),
        lax.psum_scatter(
            pick_cot.astype(jnp.bfloat16), "seq", scatter_dimension=0, tiled=True
        ).astype(jnp.float32),
    )
    own_rank = seq_place * own_count + jnp.arange(own_count, dtype=jnp.int32)
    live_own = own_rank[:, None] < counts[None, :]
    live_mask = live_own.reshape(row_count, 1).astype(f32)
    routed_in = picked.reshape(row_count, model_width)
    normed_one = norm_apply(routed_in, gain_one).astype(bf16)
    joined = jnp.dot(normed_one, full_qkv, preferred_element_type=f32).astype(bf16)
    query_rows = joined[:, :model_width].reshape(own_count, slot_count, head_count, HEAD_DIM)
    key_own = joined[:, model_width : 2 * model_width].reshape(own_count, slot_count, model_width)
    value_own = joined[:, 2 * model_width :].reshape(own_count, slot_count, model_width)
    key_every, value_every = (
        lax.all_gather(key_own, "seq", axis=0, tiled=True),
        lax.all_gather(value_own, "seq", axis=0, tiled=True),
    )
    key_rows = key_every.reshape(capacity, slot_count, head_count, HEAD_DIM)
    value_rows = value_every.reshape(capacity, slot_count, head_count, HEAD_DIM)
    scores = (
        jnp.einsum("qsha,ksha->shqk", query_rows, key_rows, preferred_element_type=f32)
        * score_scale
    )
    causal = rank_all[None, :] <= own_rank[:, None]
    allowed = causal[None, :, :] & (rank_all[None, None, :] < counts[:, None, None])
    scores = jnp.where(allowed[:, None], scores, -1000000000.0)
    row_max = jnp.max(scores, axis=-1, keepdims=True)
    weights_f = jnp.exp(scores - row_max)
    row_total = jnp.sum(weights_f, axis=-1, keepdims=True)
    weights_low = weights_f.astype(bf16)
    mixture = jnp.einsum("shqk,ksha->qsha", weights_low, value_rows, preferred_element_type=f32)
    mixture = mixture / jnp.transpose(row_total, (2, 0, 1, 3))
    attended = mixture.reshape(row_count, model_width).astype(bf16)
    branch_a = jnp.dot(attended, full_out, preferred_element_type=f32)
    hidden = routed_in + branch_a
    normed_two = norm_apply(hidden, gain_two).astype(bf16)
    up_proj = jnp.dot(normed_two, full_up, preferred_element_type=f32)
    activated = gelu_tanh(up_proj).astype(bf16)
    branch_m = jnp.dot(activated, full_down, preferred_element_type=f32)
    gate_prob = jax.nn.sigmoid(jnp.dot(routed_in, router_vec, precision=highest))
    branch = branch_a + branch_m
    update = (
        (gate_prob[:, None] * branch * live_mask)
        .astype(bf16)
        .reshape(own_count, slot_count, model_width)
    )
    update_every = lax.all_gather(update, "seq", axis=0, tiled=True)
    output = (
        tokens.astype(f32)
        + jnp.einsum("scp,csd->spd", chooser, update_every, preferred_element_type=f32)
    ).astype(bf16)
    cot_rows = picked_cot.reshape(row_count, model_width)
    grad_gate = jnp.sum(cot_rows * branch, axis=-1)
    grad_logit = grad_gate * gate_prob * (1.0 - gate_prob)
    grad_branch = gate_prob[:, None] * cot_rows
    grad_m = grad_branch.astype(bf16)
    grad_act = jnp.einsum("rd,fd->rf", grad_m, full_down, preferred_element_type=f32)
    unused_up, gelu_pull = jax.vjp(gelu_tanh, up_proj)
    grad_u = gelu_pull(grad_act)[0].astype(bf16)
    grad_n2 = jnp.einsum("rf,df->rd", grad_u, full_up, preferred_element_type=f32)
    unused_two, norm_pull_two = jax.vjp(norm_apply, hidden, gain_two)
    grad_hidden, grad_gm = norm_pull_two(grad_n2)
    grad_a = (grad_branch + grad_hidden).astype(bf16)
    grad_att = jnp.einsum("rd,ed->re", grad_a, full_out, preferred_element_type=f32).astype(bf16)
    grad_att4 = grad_att.reshape(own_count, slot_count, head_count, HEAD_DIM)
    delta_rows = jnp.sum(grad_att4.astype(f32) * mixture, axis=-1)
    delta = jnp.transpose(delta_rows, (1, 2, 0))[..., None]
    grad_p = jnp.einsum("qsha,ksha->shqk", grad_att4, value_rows, preferred_element_type=f32)
    probs = weights_f / row_total
    grad_s = (probs * (grad_p - delta)).astype(bf16)
    grad_q = (
        jnp.einsum("shqk,ksha->qsha", grad_s, key_rows, preferred_element_type=f32) * score_scale
    )
    grad_k = (
        jnp.einsum("shqk,qsha->ksha", grad_s, query_rows, preferred_element_type=f32) * score_scale
    )
    scaled_low = weights_low.astype(f32) / row_total
    grad_v = jnp.einsum("shqk,qsha->ksha", scaled_low, grad_att4.astype(f32), precision=highest)
    grad_k_own, grad_v_own = (
        lax.psum_scatter(
            grad_k.reshape(capacity, slot_count, model_width).astype(jnp.bfloat16),
            "seq",
            scatter_dimension=0,
            tiled=True,
        ).astype(jnp.float32),
        lax.psum_scatter(
            grad_v.reshape(capacity, slot_count, model_width).astype(jnp.bfloat16),
            "seq",
            scatter_dimension=0,
            tiled=True,
        ).astype(jnp.float32),
    )
    grad_joined = jnp.concatenate(
        [
            grad_q.reshape(row_count, model_width),
            grad_k_own.reshape(row_count, model_width),
            grad_v_own.reshape(row_count, model_width),
        ],
        axis=-1,
    ).astype(bf16)
    grad_n1 = jnp.einsum("re,de->rd", grad_joined, full_qkv, preferred_element_type=f32)
    unused_one, norm_pull_one = jax.vjp(norm_apply, routed_in, gain_one)
    grad_x1, grad_ga = norm_pull_one(grad_n1)
    grad_router = jnp.sum(routed_in * grad_logit[:, None], axis=0)
    grad_rows = (grad_hidden + grad_x1 + grad_logit[:, None] * router_vec[None, :]).astype(bf16)
    grad_rows = grad_rows.reshape(own_count, slot_count, model_width)
    grad_every = lax.all_gather(grad_rows, "seq", axis=0, tiled=True)
    input_grad = (
        cotangent.astype(f32)
        + jnp.einsum("scp,csd->spd", chooser, grad_every, preferred_element_type=f32)
    ).astype(bf16)
    part_qkv = jnp.einsum("rd,re->de", normed_one, grad_joined, preferred_element_type=f32)
    part_out = jnp.einsum("re,rd->ed", attended, grad_a, preferred_element_type=f32)
    part_up = jnp.einsum("rd,rf->df", normed_two, grad_u, preferred_element_type=f32)
    wide_sum = lax.psum_scatter(
        jnp.concatenate([part_qkv, part_out, part_up], axis=1),
        ("seq", "batch"),
        scatter_dimension=0,
        tiled=True,
    )
    down_sum = lax.psum_scatter(
        jnp.einsum("rf,rd->fd", activated, grad_m, preferred_element_type=f32),
        ("seq", "batch"),
        scatter_dimension=0,
        tiled=True,
    )
    small_ga, small_gm, small_router = (
        lax.psum_scatter(grad_ga, ("seq", "batch"), scatter_dimension=0, tiled=True),
        lax.psum_scatter(grad_gm, ("seq", "batch"), scatter_dimension=0, tiled=True),
        lax.psum_scatter(grad_router, ("seq", "batch"), scatter_dimension=0, tiled=True),
    )
    grad_qkv = wide_sum[:, : 3 * model_width]
    grad_out = wide_sum[:, 3 * model_width : 4 * model_width]
    grad_up = wide_sum[:, 4 * model_width :]
    return (
        output,
        input_grad,
        grad_qkv,
        grad_out,
        grad_up,
        down_sum,
        small_ga,
        small_gm,
        small_router,
    )


def solution(mesh):
    in_specs = (
        P("batch", "seq", None),
        P("batch", "seq", None),
        P("batch"),
        P("batch", None),
        P(("seq", "batch"), None),
        P(("seq", "batch"), None),
        P(("seq", "batch"), None),
        P(("seq", "batch"), None),
        P(("seq", "batch")),
        P(("seq", "batch")),
        P(("seq", "batch")),
    )
    out_specs = (
        P("batch", "seq", None),
        P("batch", "seq", None),
        P(("seq", "batch"), None),
        P(("seq", "batch"), None),
        P(("seq", "batch"), None),
        P(("seq", "batch"), None),
        P(("seq", "batch")),
        P(("seq", "batch")),
        P(("seq", "batch")),
    )
    return jax.shard_map(
        per_device, mesh=mesh, in_specs=in_specs, out_specs=out_specs, check_vma=False
    )
```

profile of v0, /device:TPU:0, one launch (start us, length us, event | category | flops | bytes accessed | tf_op | source)
XLA Modules:
  0.0 1085.4 jit_solution(18348194795909588926)
XLA Ops:
  8.8 4.7 fusion.22
  14.2 4.7 fusion.21
  19.7 42.4 %all-reduce.9 = (bf16[1024]{0:T(1024)(128)(2,1)S(1)}, bf16[1024]{0:T(1024)(128)(2,1)S(1)}, bf16[1024]{0:T(1024)(128)(2,1)S(1)}) all-reduce(bf16[1024]{0:T(1024)(128)(2,1)S(1)} %dynamic-update-slice.1, bf16[1024]{0:T(1024)(128)(2,1)S(1)} %dynamic-update-slice.2, ...), channel_id=1, replica_groups=mesh['seq'=2,'batch'=16] {'seq','batch'}, use_global_device_ids=true, to_apply=%add.1 | all-reduce | flops 3072 | bytes 12288
  66.0 36.0 %all-gather.9.cloned.1.call-done = bf16[1024,3072]{1,0:T(8,128)(2,1)} async-done(((bf16[32,3072]{1,0:T(8,128)(2,1)}), bf16[1024,3072]{1,0:T(8,128)(2,1)}) %all-gather.9.cloned.1.call-update) | async-done | bytes 6291472 | tf_op jit(solution)/shard_map/all_gather | solution.py:38
  101.9 4.6 convolution_convert_fusion
  112.5 2.6 copy.60
  115.1 2.0 reshape.236
  121.7 6.8 all-gather.13.cloned.1.call-done
  128.5 2.4 copy.55
  130.9 20.9 %all-gather.11.cloned.1.call-done = bf16[256,2,1024]{2,1,0:T(2,128)(2,1)} async-done(((bf16[128,2,1024]{2,1,0:T(2,128)(2,1)}), bf16[256,2,1024]{2,1,0:T(2,128)(2,1)}) %all-gather.11.cloned.1.call-update) | async-done | bytes 1048592 | tf_op jit(solution)/shard_map/all_gather | solution.py:77
  151.8 3.7 copy.54
  155.5 2.3 fusion.10
  159.6 2.4 fusion.54
  162.1 2.5 copy.57
  166.0 45.0 %all-gather.15.cloned.1.call-done = bf16[1024,1024]{1,0:T(8,128)(2,1)} async-done(((bf16[32,1024]{1,0:T(8,128)(2,1)}), bf16[1024,1024]{1,0:T(8,128)(2,1)}) %all-gather.15.cloned.1.call-update) | async-done | bytes 2097168 | tf_op jit(solution)/shard_map/all_gather | solution.py:39
  211.0 3.5 multiply_reduce_fusion.7
  214.5 75.6 %all-gather.17.cloned.1.call-done = bf16[1024,4096]{1,0:T(8,128)(2,1)} async-done(((bf16[32,4096]{1,0:T(8,128)(2,1)}), bf16[1024,4096]{1,0:T(8,128)(2,1)}) %all-gather.17.cloned.1.call-update) | async-done | bytes 8388624 | tf_op jit(solution)/shard_map/all_gather | solution.py:40
  290.2 7.8 fusion.52
  298.0 71.3 %all-gather.19.cloned.1.call-done = bf16[4096,1024]{1,0:T(8,128)(2,1)} async-done(((bf16[128,1024]{1,0:T(8,128)(2,1)}), bf16[4096,1024]{1,0:T(8,128)(2,1)}) %all-gather.19.cloned.1.call-update) | async-done | bytes 8388624 | tf_op jit(solution)/shard_map/all_gather | solution.py:41
  369.3 8.7 multiply_reduce_fusion.3
  378.0 8.1 fusion.6
  387.5 2.9 multiply_reduce_fusion.1
  395.0 2.5 reshape.229
  397.5 3.0 copy.61
  400.5 6.2 fusion.18
  406.9 2.5 multiply_convert_fusion
  412.3 3.7 copy.65
  416.0 3.7 copy.67
  421.0 2.0 reshape.226
  423.1 2.1 copy.58
  425.2 3.6 fusion.25
  428.8 3.3 copy.63
  432.1 3.0 reshape.230
  437.0 4.1 fusion.56
  441.1 8.2 fusion.51
  449.4 32.2 %all-reduce.13.cloned.1.call-done = (bf16[256,2,1024]{2,1,0:T(2,128)(2,1)}, bf16[256,2,1024]{2,1,0:T(2,128)(2,1)}) async-done(((bf16[256,2,1024]{2,1,0:T(2,128)(2,1)}, bf16[256,2,1024]{2,1,0:T(2,128)(2,1)}), (bf16[256,2,1024]{2,1,0:T(2,128)(2,1)}, bf16[256,2,1024]{2,1,0:T(2,128)(2,1)})) %all-reduce.13.cloned.1.call-update) | async-done | bytes 2097168
  481.5 2.9 constant_dynamic-slice_fusion
  484.4 2.1 reshape.232
  486.5 2.0 reshape.231
  492.4 5.4 multiply_reduce_fusion.2
  501.3 7.8 fusion.50
  509.2 22.8 %pad_maximum_fusion = f32[1024,8192]{1,0:T(8,128)} fusion(f32[1024,4096]{1,0:T(8,128)} %fusion.51, f32[1024,1024]{1,0:T(8,128)} %fusion.56, f32[1024,3072]{1,0:T(8,128)} %fusion.50), kind=kLoop, calls=%fused_computation | loop fusion | flops 16777216 | bytes 67108864 | tf_op jit(solution)/shard_map/concatenate | solution.py:177
  532.2 11.3 %fusion.48 = f32[4096,1024]{1,0:T(8,128)} fusion(f32[256,1024]{1,0:T(8,128)S(1)} %reshape.236, f32[256]{0:T(256)S(1)} %get-tuple-element.22, f32[256,4096]{1,0:T(8,128)} %fusion.52), kind=kOutput, calls=%fused_computation.97 | convolution fusion | flops 2157445120 | bytes 22021120 | tf_op jit(solution)/shard_map/rf,rd->fd/dot_general | solution.py:183
  544.8 4.9 add_convert_fusion.1
  549.6 51.4 %all-reduce.8 = (f32[1024]{0:T(1024)S(1)}, f32[1024]{0:T(1024)S(1)}, f32[1024]{0:T(1024)S(1)}) all-reduce(f32[1024]{0:T(1024)S(1)} %get-tuple-element.11, f32[1024]{0:T(1024)S(1)} %get-tuple-element.9, f32[1024]{0:T(1024)S(1)} %multiply_reduce_fusion), channel_id=8, replica_groups=mesh['seq'=2,'batch'=16] {'seq','batch'}, use_global_device_ids=true, to_apply=%region_15.16.clone | all-reduce | flops 3072 | bytes 24576
  602.8 4.9 add_convert_fusion
  607.7 279.4 %reduce-scatter.9.cloned.1.call-done = f32[32,8192]{1,0:T(8,128)} async-done(((f32[1024,8192]{1,0:T(8,128)}), f32[32,8192]{1,0:T(8,128)}) %reduce-scatter.9.cloned.1.call-update) | async-done | bytes 1048592 | tf_op jit(solution)/shard_map/reduce_scatter | solution.py:176
  892.2 185.4 %reduce-scatter.11.cloned.1.call-done = f32[128,1024]{1,0:T(8,128)} async-done(((f32[4096,1024]{1,0:T(8,128)}), f32[128,1024]{1,0:T(8,128)}) %reduce-scatter.11.cloned.1.call-update) | async-done | bytes 524304 | tf_op jit(solution)/shard_map/reduce_scatter | solution.py:182
  (139 shorter events, 47.2 us)
Async XLA Ops:
  8.0 6.2 copy-start.20
  8.0 54.1 %reduce-scatter.5.cloned.1.call-start = ((), (), s32[]{:S(2)}) async-start(), calls=%async_computation.4 | async-start | bytes 1572864 | tf_op jit(solution)/shard_map/reduce_scatter | solution.py:59
  13.5 5.4 copy-start.21
  13.5 5.7 copy-start.22
  13.6 5.9 copy-start.23
  13.6 88.4 %all-gather.9.cloned.1.call-start = ((), (), s32[]{:S(2)}) async-start(), calls=%async_computation.5 | async-start | bytes 6488064 | tf_op jit(solution)/shard_map/all_gather | solution.py:38
  14.1 98.4 %reduce-scatter.7.cloned.1.call-start = ((), (), s32[]{:S(2)}) async-start(), calls=%async_computation.12 | async-start | bytes 1572864 | tf_op jit(solution)/shard_map/reduce_scatter | solution.py:62
  18.9 109.6 %all-gather.13.cloned.1.call-start = ((), (), s32[]{:S(2)}) async-start(), calls=%async_computation.7 | async-start | bytes 1572864 | tf_op jit(solution)/shard_map/all_gather | solution.py:76
  107.5 9.6 copy-start.6
  108.5 43.3 %all-gather.11.cloned.1.call-start = ((), (), s32[]{:S(2)}) async-start(), calls=%async_computation.6 | async-start | bytes 1572864 | tf_op jit(solution)/shard_map/all_gather | solution.py:77
  109.6 101.4 %all-gather.15.cloned.1.call-start = ((), (), s32[]{:S(2)}) async-start(), calls=%async_computation.8 | async-start | bytes 2162688 | tf_op jit(solution)/shard_map/all_gather | solution.py:39
  110.2 180.0 %all-gather.17.cloned.1.call-start = ((), (), s32[]{:S(2)}) async-start(), calls=%async_computation.9 | async-start | bytes 8650752 | tf_op jit(solution)/shard_map/all_gather | solution.py:40
  110.8 258.5 %all-gather.19.cloned.1.call-start = ((), (), s32[]{:S(2)}) async-start(), calls=%async_computation.10 | async-start | bytes 8650752 | tf_op jit(solution)/shard_map/all_gather | solution.py:41
  111.5 370.0 %all-reduce.13.cloned.1.call-start = ((), (), s32[]{:S(2)}) async-start(), calls=%async_computation.16 | async-start | bytes 4194304
  130.9 28.6 %copy-start.4 = (bf16[256,2,1024]{0,2,1:T(8,128)(2,1)}, bf16[256,2,1024]{0,2,1:T(8,128)(2,1)S(1)}, u32[]{:S(2)}) copy-start(bf16[256,2,1024]{0,2,1:T(8,128)(2,1)S(1)} %copy.55) | copy-start | bytes 3145732
  155.5 4.1 copy-start.18
  157.8 4.3 copy-start.1
  369.3 8.7 copy-start
  378.0 9.5 copy-start.3
  386.1 1.4 copy-start.12
  387.5 3.9 copy-start.16
  390.4 1.0 copy-start.9
  390.4 3.1 copy-start.11
  392.6 0.8 copy-start.14
  400.5 6.2 copy-start.15
  400.5 6.2 copy-start.17
  400.5 6.4 copy-start.2
  400.5 6.4 copy-start.19
  406.9 3.9 copy-start.8
  409.4 1.3 copy-start.5
  410.8 9.0 copy-start.24
  419.7 125.0 %all-gather.21.cloned.1.call-start = ((), (), s32[]{:S(2)}) async-start(), calls=%async_computation.11 | async-start | bytes 1572864 | tf_op jit(solution)/shard_map/all_gather | solution.py:108
  437.0 4.1 copy-start.13
  449.3 153.5 %all-gather.23.cloned.1.call-start = ((), (), s32[]{:S(2)}) async-start(), calls=%async_computation.13 | async-start | bytes 1572864 | tf_op jit(solution)/shard_map/all_gather | solution.py:168
  492.4 5.4 copy-start.10
  509.1 377.9 %reduce-scatter.9.cloned.1.call-start = ((), (), s32[]{:S(2)}) async-start(), calls=%async_computation.14 | async-start | bytes 34603008 | tf_op jit(solution)/shard_map/reduce_scatter | solution.py:176
  532.0 545.6 %reduce-scatter.11.cloned.1.call-start = ((), (), s32[]{:S(2)}) async-start(), calls=%async_computation.15 | async-start | bytes 17301504 | tf_op jit(solution)/shard_map/reduce_scatter | solution.py:182
  543.5 1.0 copy-start.7
Sparse Core Ops, SparseCore 0:
  13.7 23.8 reduce-scatter.4
  40.4 20.9 reduce-scatter.6
  108.7 19.7 all-gather.12
  130.5 21.2 all-gather.10
  154.5 56.4 all-gather.14
  213.7 76.4 all-gather.16
  293.1 76.1 all-gather.18
  419.8 61.6 all-reduce.12
  483.2 21.2 all-gather.20
  509.2 21.2 all-gather.22
Sparse Core Ops, SparseCore 1:
  16.9 84.9 all-gather.8
  532.1 354.9 reduce-scatter.8
  889.9 187.7 reduce-scatter.10
where the time goes:
time: 1090 us
  waiting for transfers between devices  755 us (69%)
  matrix products  112 us (10%)
  blocking collectives  93.9 us (9%)
  local copies, waits for them, and re-layouts  76.8 us (7%)
  other arithmetic  29.7 us (3%)
  between operations  17.1 us (2%)
    reduce_scatter x1, waiting for transfers between devices, per_device(): lax.psum_scatter(jnp.concatenate([part_qkv, part_out, part_up], axis=1),...  279 us
    reduce_scatter x1, waiting for transfers between devices, per_device(): lax.psum_scatter(jnp.einsum('rf,rd->fd', activated, grad_m, preferred_ele...  185 us
    unnamed x2, blocking collectives  93.9 us
    all_gather x1, waiting for transfers between devices, per_device(): lax.all_gather(w_up, ('seq', 'batch'), axis=0, tiled=True)  75.6 us
    all_gather x1, waiting for transfers between devices, per_device(): lax.all_gather(w_down, ('seq', 'batch'), axis=0, tiled=True)  71.3 us
    all_gather x1, waiting for transfers between devices, per_device(): lax.all_gather(w_out, ('seq', 'batch'), axis=0, tiled=True)  45 us
    all_gather x1, waiting for transfers between devices, per_device(): lax.all_gather(w_qkv, ('seq', 'batch'), axis=0, tiled=True)  36 us
    unnamed x14, waiting for transfers between devices  34.6 us
  transfers between devices with their start and end apart: 13, of which 9 were waited for; matrix products, arithmetic and copies ran while one was open for 15% of the time, Pallas kernels for 0%

commit v1 on v0

--- a/solution.py
+++ b/solution.py
@@ -173,26 +173,22 @@
     part_qkv = jnp.einsum("rd,re->de", normed_one, grad_joined, preferred_element_type=f32)
     part_out = jnp.einsum("re,rd->ed", attended, grad_a, preferred_element_type=f32)
     part_up = jnp.einsum("rd,rf->df", normed_two, grad_u, preferred_element_type=f32)
-    wide_sum = lax.psum_scatter(
-        jnp.concatenate([part_qkv, part_out, part_up], axis=1),
-        ("seq", "batch"),
-        scatter_dimension=0,
-        tiled=True,
-    )
-    down_sum = lax.psum_scatter(
-        jnp.einsum("rf,rd->fd", activated, grad_m, preferred_element_type=f32),
-        ("seq", "batch"),
-        scatter_dimension=0,
-        tiled=True,
-    )
+    part_down = jnp.einsum("rf,rd->fd", activated, grad_m, preferred_element_type=f32)
+
+    def sum_rows(part):
+        return lax.psum_scatter(
+            part.astype(bf16), ("seq", "batch"), scatter_dimension=0, tiled=True
+        ).astype(f32)
+
+    down_sum = sum_rows(part_down)
+    grad_up = sum_rows(part_up)
+    grad_out = sum_rows(part_out)
+    grad_qkv = sum_rows(part_qkv)
     small_ga, small_gm, small_router = (
         lax.psum_scatter(grad_ga, ("seq", "batch"), scatter_dimension=0, tiled=True),
         lax.psum_scatter(grad_gm, ("seq", "batch"), scatter_dimension=0, tiled=True),
         lax.psum_scatter(grad_router, ("seq", "batch"), scatter_dimension=0, tiled=True),
     )
-    grad_qkv = wide_sum[:, : 3 * model_width]
-    grad_out = wide_sum[:, 3 * model_width : 4 * model_width]
-    grad_up = wide_sum[:, 4 * model_width :]
     return (
         output,
         input_grad,

time: 1090 us -> 1070 us (0.982)
  waiting for transfers between devices: 755 us -> 782 us
  local copies, waits for them, and re-layouts: 76.8 us -> 58.9 us
  other arithmetic: 29.7 us -> 15.1 us
  blocking collectives: 93.9 us -> 82 us
    concatenate x1 -> x0, other arithmetic: 22.8 us -> none  [per_device(): jnp.concatenate([part_qkv, part_out, part_up], axis=1)]
    unnamed x14 -> x16, waiting for transfers between devices: 34.6 us -> 51.4 us
    unnamed x2, blocking collectives: 93.9 us -> 82 us
    reduce_scatter x2 -> x4, waiting for transfers between devices: 465 us -> 470 us  [sum_rows(): lax.psum_scatter(part.astype(bf16), ('seq', 'batch'), scatter_dimension=0...]
  transfers between devices with their start and end apart: 13 -> 15, of which waited for: 9 -> 11; matrix products, arithmetic and copies ran while one was open for 15% -> 11% of each run, Pallas kernels for 0% -> 0%
where the time goes in v1:
time: 1070 us; the launch traced here: 1060 us
  waiting for transfers between devices  782 us (73%)
  matrix products  108 us (10%)
  blocking collectives  82 us (8%)
  local copies, waits for them, and re-layouts  58.9 us (6%)
  between operations  17.4 us (2%)
  other arithmetic  15.1 us (1%)
    reduce_scatter x4, waiting for transfers between devices, sum_rows(): lax.psum_scatter(part.astype(bf16), ('seq', 'batch'), scatter_dimension=0...  470 us
    unnamed x2, blocking collectives  82 us
    all_gather x1, waiting for transfers between devices, per_device(): lax.all_gather(w_up, ('seq', 'batch'), axis=0, tiled=True)  75.7 us
    all_gather x1, waiting for transfers between devices, per_device(): lax.all_gather(w_down, ('seq', 'batch'), axis=0, tiled=True)  71.3 us
    unnamed x16, waiting for transfers between devices  51.4 us
    all_gather x1, waiting for transfers between devices, per_device(): lax.all_gather(w_out, ('seq', 'batch'), axis=0, tiled=True)  45.9 us
    all_gather x1, waiting for transfers between devices, per_device(): lax.all_gather(w_qkv, ('seq', 'batch'), axis=0, tiled=True)  36 us
  transfers between devices with their start and end apart: 15, of which 11 were waited for; matrix products, arithmetic and copies ran while one was open for 11% of the time, Pallas kernels for 0%

profile of v1, /device:TPU:0, one launch (start us, length us, event | category | flops | bytes accessed | tf_op | source)
XLA Modules:
  0.0 1064.2 jit_solution(6516949798522098472)
XLA Ops:
  8.8 4.7 fusion.22
  14.2 4.7 fusion.21
  19.7 42.4 %all-reduce.9 = (bf16[1024]{0:T(1024)(128)(2,1)S(1)}, bf16[1024]{0:T(1024)(128)(2,1)S(1)}, bf16[1024]{0:T(1024)(128)(2,1)S(1)}) all-reduce(bf16[1024]{0:T(1024)(128)(2,1)S(1)} %dynamic-update-slice.1, bf16[1024]{0:T(1024)(128)(2,1)S(1)} %dynamic-update-slice.2, ...), channel_id=1, replica_groups=mesh['seq'=2,'batch'=16] {'seq','batch'}, use_global_device_ids=true, to_apply=%add.1 | all-reduce | flops 3072 | bytes 12288
  66.0 36.0 %all-gather.9.cloned.1.call-done = bf16[1024,3072]{1,0:T(8,128)(2,1)} async-done(((bf16[32,3072]{1,0:T(8,128)(2,1)}), bf16[1024,3072]{1,0:T(8,128)(2,1)}) %all-gather.9.cloned.1.call-update) | async-done | bytes 6291472 | tf_op jit(solution)/shard_map/all_gather | solution.py:38
  101.9 4.6 convolution_convert_fusion.3
  117.5 10.2 all-gather.13.cloned.1.call-done
  127.7 2.4 copy.53
  130.1 20.9 %all-gather.11.cloned.1.call-done = bf16[256,2,1024]{2,1,0:T(2,128)(2,1)} async-done(((bf16[128,2,1024]{2,1,0:T(2,128)(2,1)}), bf16[256,2,1024]{2,1,0:T(2,128)(2,1)}) %all-gather.11.cloned.1.call-update) | async-done | bytes 1048592 | tf_op jit(solution)/shard_map/all_gather | solution.py:77
  151.0 3.7 copy.52
  155.9 1.8 fusion.11
  157.7 2.7 fusion.51
  160.4 2.5 copy.55
  164.3 45.9 %all-gather.15.cloned.1.call-done = bf16[1024,1024]{1,0:T(8,128)(2,1)} async-done(((bf16[32,1024]{1,0:T(8,128)(2,1)}), bf16[1024,1024]{1,0:T(8,128)(2,1)}) %all-gather.15.cloned.1.call-update) | async-done | bytes 2097168 | tf_op jit(solution)/shard_map/all_gather | solution.py:39
  210.2 3.5 multiply_reduce_fusion.7
  213.7 75.7 %all-gather.17.cloned.1.call-done = bf16[1024,4096]{1,0:T(8,128)(2,1)} async-done(((bf16[32,4096]{1,0:T(8,128)(2,1)}), bf16[1024,4096]{1,0:T(8,128)(2,1)}) %all-gather.17.cloned.1.call-update) | async-done | bytes 8388624 | tf_op jit(solution)/shard_map/all_gather | solution.py:40
  289.4 7.8 fusion.49
  297.2 71.3 %all-gather.19.cloned.1.call-done = bf16[4096,1024]{1,0:T(8,128)(2,1)} async-done(((bf16[128,1024]{1,0:T(8,128)(2,1)}), bf16[4096,1024]{1,0:T(8,128)(2,1)}) %all-gather.19.cloned.1.call-update) | async-done | bytes 8388624 | tf_op jit(solution)/shard_map/all_gather | solution.py:41
  368.5 9.0 multiply_reduce_fusion.3
  377.5 9.5 fusion.6
  387.0 4.5 multiply_reduce_fusion.1
  395.1 2.6 reshape.229
  397.7 3.0 copy.59
  400.7 6.0 fusion.18
  406.7 3.7 copy.65
  412.0 4.2 multiply_convert_fusion
  418.9 3.7 copy.63
  424.2 3.2 fusion.25
  427.5 2.5 copy.61
  433.6 1.9 constant_dynamic-update-slice_fusion.2
  435.6 49.0 %all-reduce.13.cloned.1.call-done = (bf16[256,2,1024]{2,1,0:T(2,128)(2,1)}, bf16[256,2,1024]{2,1,0:T(2,128)(2,1)}) async-done(((bf16[256,2,1024]{2,1,0:T(2,128)(2,1)}, bf16[256,2,1024]{2,1,0:T(2,128)(2,1)}), (bf16[256,2,1024]{2,1,0:T(2,128)(2,1)}, bf16[256,2,1024]{2,1,0:T(2,128)(2,1)})) %all-reduce.13.cloned.1.call-update) | async-done | bytes 2097168
  484.5 1.9 constant_dynamic-slice_fusion
  487.7 1.9 constant_dynamic-update-slice_fusion.1
  490.4 5.6 multiply_reduce_fusion.2
  497.4 2.1 reshape.233
  499.5 2.0 copy.66
  501.5 2.1 convolution_convert_fusion.4
  503.8 6.0 convolution_convert_fusion.2
  509.8 7.3 convolution_convert_fusion.1
  518.5 8.5 convolution_convert_fusion
  528.2 4.9 add_convert_fusion.1
  533.1 39.5 %all-reduce.8 = (f32[1024]{0:T(1024)S(1)}, f32[1024]{0:T(1024)S(1)}, f32[1024]{0:T(1024)S(1)}) all-reduce(f32[1024]{0:T(1024)S(1)} %get-tuple-element.11, f32[1024]{0:T(1024)S(1)} %get-tuple-element.9, f32[1024]{0:T(1024)S(1)} %multiply_reduce_fusion), channel_id=10, replica_groups=mesh['seq'=2,'batch'=16] {'seq','batch'}, use_global_device_ids=true, to_apply=%region_17.18.clone | all-reduce | flops 3072 | bytes 24576
  574.4 4.9 add_convert_fusion
  579.2 62.2 %reduce-scatter.13.cloned.1.call-done = bf16[32,1024]{1,0:T(8,128)(2,1)} async-done(((bf16[1024,1024]{1,0:T(8,128)(2,1)}), bf16[32,1024]{1,0:T(8,128)(2,1)}) %reduce-scatter.13.cloned.1.call-update) | async-done | bytes 65552 | tf_op jit(solution)/shard_map/reduce_scatter | solution.py:179
  642.9 113.9 %reduce-scatter.11.cloned.1.call-done = bf16[32,3072]{1,0:T(8,128)(2,1)} async-done(((bf16[1024,3072]{1,0:T(8,128)(2,1)}), bf16[32,3072]{1,0:T(8,128)(2,1)}) %reduce-scatter.11.cloned.1.call-update) | async-done | bytes 196624 | tf_op jit(solution)/shard_map/reduce_scatter | solution.py:179
  758.5 148.7 %reduce-scatter.15.cloned.1.call-done = bf16[32,4096]{1,0:T(8,128)(2,1)} async-done(((bf16[1024,4096]{1,0:T(8,128)(2,1)}), bf16[32,4096]{1,0:T(8,128)(2,1)}) %reduce-scatter.15.cloned.1.call-update) | async-done | bytes 262160 | tf_op jit(solution)/shard_map/reduce_scatter | solution.py:179
  907.2 1.8 convert_element_type.184
  909.0 145.4 %reduce-scatter.17.cloned.1.call-done = bf16[128,1024]{1,0:T(8,128)(2,1)} async-done(((bf16[4096,1024]{1,0:T(8,128)(2,1)}), bf16[128,1024]{1,0:T(8,128)(2,1)}) %reduce-scatter.17.cloned.1.call-update) | async-done | bytes 262160 | tf_op jit(solution)/shard_map/reduce_scatter | solution.py:179
  1054.4 1.8 convert_element_type.186
  (141 shorter events, 43.1 us)
Async XLA Ops:
  8.0 6.2 copy-start.18
  8.0 54.1 %reduce-scatter.7.cloned.1.call-start = ((), (), s32[]{:S(2)}) async-start(), calls=%async_computation.6 | async-start | bytes 1572864 | tf_op jit(solution)/shard_map/reduce_scatter | solution.py:59
  13.5 5.4 copy-start.19
  13.6 5.7 copy-start.20
  13.6 5.9 copy-start.21
  13.6 88.4 %all-gather.9.cloned.1.call-start = ((), (), s32[]{:S(2)}) async-start(), calls=%async_computation.7 | async-start | bytes 6488064 | tf_op jit(solution)/shard_map/all_gather | solution.py:38
  14.2 97.3 %reduce-scatter.9.cloned.1.call-start = ((), (), s32[]{:S(2)}) async-start(), calls=%async_computation.14 | async-start | bytes 1572864 | tf_op jit(solution)/shard_map/reduce_scatter | solution.py:62
  18.9 108.8 %all-gather.13.cloned.1.call-start = ((), (), s32[]{:S(2)}) async-start(), calls=%async_computation.9 | async-start | bytes 1572864 | tf_op jit(solution)/shard_map/all_gather | solution.py:76
  106.7 8.0 copy-start.3
  107.7 43.3 %all-gather.11.cloned.1.call-start = ((), (), s32[]{:S(2)}) async-start(), calls=%async_computation.8 | async-start | bytes 1572864 | tf_op jit(solution)/shard_map/all_gather | solution.py:77
  108.8 101.4 %all-gather.15.cloned.1.call-start = ((), (), s32[]{:S(2)}) async-start(), calls=%async_computation.10 | async-start | bytes 2162688 | tf_op jit(solution)/shard_map/all_gather | solution.py:39
  109.4 180.0 %all-gather.17.cloned.1.call-start = ((), (), s32[]{:S(2)}) async-start(), calls=%async_computation.11 | async-start | bytes 8650752 | tf_op jit(solution)/shard_map/all_gather | solution.py:40
  110.0 258.5 %all-gather.19.cloned.1.call-start = ((), (), s32[]{:S(2)}) async-start(), calls=%async_computation.12 | async-start | bytes 8650752 | tf_op jit(solution)/shard_map/all_gather | solution.py:41
  110.7 373.8 %all-reduce.13.cloned.1.call-start = ((), (), s32[]{:S(2)}) async-start(), calls=%async_computation.20 | async-start | bytes 4194304
  117.5 38.4 %copy-start.5 = (bf16[128,2,16,64]{0,3,2,1:T(8,128)(2,1)}, bf16[128,2,16,64]{0,3,2,1:T(8,128)(2,1)S(1)}, u32[]{:S(2)}) copy-start(bf16[128,2,16,64]{0,3,2,1:T(8,128)(2,1)S(1)} %copy.54) | copy-start | bytes 1572868
  154.7 3.0 copy-start.17
  155.9 4.5 copy-start
  368.5 9.0 copy-start.8
  368.5 9.0 copy-start.9
  377.5 9.5 copy-start.1
  387.0 4.5 copy-start.16
  391.4 1.3 copy-start.11
  391.4 2.2 copy-start.13
  392.7 0.8 copy-start.14
  412.0 5.5 copy-start.6
  416.2 1.3 copy-start.2
  417.5 5.5 copy-start.22
  422.7 105.5 %all-gather.21.cloned.1.call-start = ((), (), s32[]{:S(2)}) async-start(), calls=%async_computation.13 | async-start | bytes 1572864 | tf_op jit(solution)/shard_map/all_gather | solution.py:108
  435.5 138.8 %all-gather.23.cloned.1.call-start = ((), (), s32[]{:S(2)}) async-start(), calls=%async_computation.15 | async-start | bytes 1572864 | tf_op jit(solution)/shard_map/all_gather | solution.py:168
  490.4 5.6 copy-start.12
  496.0 5.5 copy-start.7
  496.0 5.5 copy-start.15
  501.5 140.0 %reduce-scatter.13.cloned.1.call-start = ((), (), s32[]{:S(2)}) async-start(), calls=%async_computation.17 | async-start | bytes 2162688 | tf_op jit(solution)/shard_map/reduce_scatter | solution.py:179
  503.7 253.1 %reduce-scatter.11.cloned.1.call-start = ((), (), s32[]{:S(2)}) async-start(), calls=%async_computation.16 | async-start | bytes 6488064 | tf_op jit(solution)/shard_map/reduce_scatter | solution.py:179
  509.8 397.4 %reduce-scatter.15.cloned.1.call-start = ((), (), s32[]{:S(2)}) async-start(), calls=%async_computation.18 | async-start | bytes 8650752 | tf_op jit(solution)/shard_map/reduce_scatter | solution.py:179
  517.2 1.3 copy-start.10
  517.2 537.2 %reduce-scatter.17.cloned.1.call-start = ((), (), s32[]{:S(2)}) async-start(), calls=%async_computation.19 | async-start | bytes 8650752 | tf_op jit(solution)/shard_map/reduce_scatter | solution.py:179
  527.0 1.0 copy-start.4
Sparse Core Ops, SparseCore 0:
  13.7 23.8 reduce-scatter.6
  40.4 20.9 reduce-scatter.8
  107.9 19.7 all-gather.12
  129.7 21.3 all-gather.10
  153.7 56.4 all-gather.14
  212.9 76.4 all-gather.16
  292.3 76.1 all-gather.18
  422.8 61.6 all-reduce.12
  486.7 21.2 all-gather.20
  509.6 21.3 all-gather.22
Sparse Core Ops, SparseCore 1:
  17.0 84.9 all-gather.8
  504.3 137.1 reduce-scatter.12
  646.9 109.8 reduce-scatter.10
  759.2 147.9 reduce-scatter.14
  909.6 144.7 reduce-scatter.16

commit v2 on v1

--- a/solution.py
+++ b/solution.py
@@ -1,13 +1,75 @@
+import functools
+
 import jax
 import jax.numpy as jnp
 from jax import lax
+from jax.experimental import pallas as pl
+from jax.experimental.pallas import tpu as pltpu
 from jax.sharding import PartitionSpec as P
 
 HEAD_DIM = 64
+MESH = pl.DeviceIdType.MESH
 
 
 epsilon = 1e-05
 highest = lax.Precision.HIGHEST
+f32 = jnp.float32
+bf16 = jnp.bfloat16
+
+LINE = 4
+GELU_C = 0.7978845608
+GELU_K = 0.044715
+
+
+def dot_nn(a, b):
+    return lax.dot_general(a, b, (((1,), (0,)), ((), ())), preferred_element_type=f32)
+
+
+def dot_nt(a, b):
+    return lax.dot_general(a, b, (((1,), (1,)), ((), ())), preferred_element_type=f32)
+
+
+def dot_tn(a, b):
+    return lax.dot_general(a, b, (((0,), (0,)), ((), ())), preferred_element_type=f32)
+
+
+def place():
+    s = lax.axis_index("seq")
+    b = lax.axis_index("batch")
+    return s, b // 4, lax.rem(b // 2, 2), lax.rem(b, 2)
+
+
+def device(s, z, y, c):
+    return (s, z * 4 + y * 2 + c)
+
+
+def remote(src, dst, send, recv, target):
+    return pltpu.make_async_remote_copy(
+        src_ref=src, dst_ref=dst, send_sem=send, recv_sem=recv, device_id=target, device_id_type=MESH
+    )
+
+
+def greet(targets):
+    barrier = pltpu.get_barrier_semaphore()
+    for target in targets:
+        pl.semaphore_signal(barrier, inc=1, device_id=target, device_id_type=MESH)
+    pl.semaphore_wait(barrier, len(targets))
+
+
+def inverse_rms(values):
+    return lax.rsqrt(jnp.mean(values * values, axis=-1, keepdims=True) + epsilon)
+
+
+def head_mask(parity):
+    lane = lax.broadcasted_iota(jnp.int32, (1, 128), 1)
+    return jnp.where(lane // HEAD_DIM == parity, 1.0, 0.0).astype(f32)
+
+
+def allowed_pairs(bias_row):
+    count = bias_row.shape[-1]
+    query = lax.broadcasted_iota(jnp.int32, (count, count), 0)
+    key = lax.broadcasted_iota(jnp.int32, (count, count), 1)
+    return (key <= query) & (bias_row > -1.0)
 
 
 def norm_apply(values_in, gain_vec):
@@ -22,7 +84,7 @@
     return jax.nn.gelu(values_in, approximate=True)
 
 
-def per_device(
+def general_device(
     tokens, cotangent, lengths, routed, w_qkv, w_out, w_up, w_down, gain_attn, gain_mlp, router
 ):
     slot_count, local_len, model_width = tokens.shape
@@ -32,8 +94,6 @@
     head_count = model_width // HEAD_DIM
     row_count = own_count * slot_count
     score_scale = HEAD_DIM ** (-0.5)
-    f32 = jnp.float32
-    bf16 = jnp.bfloat16
     gathered = (
         lax.all_gather(w_qkv, ("seq", "batch"), axis=0, tiled=True),
         lax.all_gather(w_out, ("seq", "batch"), axis=0, tiled=True),
@@ -202,6 +262,669 @@
     )
 
 
+def first_kernel(
+    tok_hbm, cot_hbm, vec_hbm, wq_hbm, wo_hbm, wu_hbm, wd_hbm, pos_ref, bias_ref,
+    xr_out, dr_out, h_out, qkv_out, o_out, wq_out, wo_out, gains_out, gd_out, gu_out, d2s_out, d2r_out, ms_out,
+    tok, cot, wq, wo, wu, wd, gv, stq, stu, stv, rcv,
+    xs, xr, ds, dr, a_s, a_r, hid, n2, qkv, att, act, gp, m_s, d2s, d2r, dm, gd, gu, gains,
+    loc, out_sem, sz, rz, sy, ry, sc, rc, sx, rx,
+):
+    s, z, y, c = place()
+    xdev, ydev, cdev = device(1 - s, z, y, c), device(s, z, 1 - y, c), device(s, z, y, 1 - c)
+    zdev = [device(s, lax.rem(z + i + 1, LINE), y, c) for i in range(3)]
+    zsrc = [lax.rem(z + 3 - i, LINE) for i in range(3)]
+    half_q, half_u = stq.shape[1] // 3, stu.shape[1]
+    model = xr.shape[2]
+
+    local = []
+
+    def fetch(src, dst):
+        copy = pltpu.make_async_copy(src, dst, loc.at[len(local)])
+        copy.start()
+        local.append(copy)
+        return copy
+
+    stage = [fetch(vec_hbm, stv)]
+    for j in range(3):
+        stage.append(fetch(wq_hbm.at[:, pl.ds(j * 2 * half_q + (1 - s) * half_q, half_q)], stq.at[:, pl.ds(j * half_q, half_q)]))
+    own_q = [
+        fetch(wq_hbm.at[:, pl.ds(j * 2 * half_q + s * half_q, half_q)], wq.at[s, z, y, c, :, pl.ds(j * half_q, half_q)])
+        for j in range(3)
+    ]
+    stage.append(fetch(wu_hbm.at[:, pl.ds((1 - s) * half_u, half_u)], stu))
+    own_o = fetch(wo_hbm, wo.at[z, y, c])
+    own_u = fetch(wu_hbm.at[:, pl.ds(s * half_u, half_u)], wu.at[s, z, y, c])
+    own_d = fetch(wd_hbm, wd.at[z, y, c])
+    get_tok = [fetch(tok_hbm.at[i], tok.at[i]) for i in range(2)]
+    get_cot = [fetch(cot_hbm.at[i], cot.at[i]) for i in range(2)]
+
+    blocks = [
+        lambda zz, yy, cc: wq.at[s, zz, yy, cc],
+        lambda zz, yy, cc: wq.at[1 - s, zz, yy, cc],
+        lambda zz, yy, cc: gv.at[zz, yy, cc],
+        lambda zz, yy, cc: wo.at[zz, yy, cc],
+        lambda zz, yy, cc: wu.at[s, zz, yy, cc],
+        lambda zz, yy, cc: wu.at[1 - s, zz, yy, cc],
+        lambda zz, yy, cc: wd.at[zz, yy, cc],
+    ]
+    lines = [
+        lambda yy, cc: wq.at[s, :, yy, cc],
+        lambda yy, cc: wq.at[1 - s, :, yy, cc],
+        lambda yy, cc: gv.at[:, yy, cc],
+        lambda yy, cc: wo.at[:, yy, cc],
+        lambda yy, cc: wu.at[s, :, yy, cc],
+        lambda yy, cc: wu.at[1 - s, :, yy, cc],
+        lambda yy, cc: wd.at[:, yy, cc],
+    ]
+    sent = []
+
+    def send(src, dst, send_sem, recv_sem, target):
+        copy = remote(src, dst, send_sem, recv_sem, target)
+        copy.start()
+        sent.append(copy)
+        return copy
+
+    def spread(p):
+        own = blocks[p](z, y, c)
+        for i in range(3):
+            send(own, own, sz.at[p, i], rz.at[p, i], zdev[i])
+        send(own, own, sy.at[p, 3], ry.at[p, 3], ydev)
+
+    def after_z(p):
+        for i in range(3):
+            ref = blocks[p](zsrc[i], y, c)
+            remote(ref, ref, sz.at[p, i], rz.at[p, i], zdev[i]).wait_recv()
+            send(ref, ref, sy.at[p, i], ry.at[p, i], ydev)
+        line = lines[p](y, c)
+        send(line, line, sc.at[p, 0], rc.at[p, 0], cdev)
+
+    def after_y(p):
+        for i, zz in enumerate([z] + zsrc):
+            ref = blocks[p](zz, 1 - y, c)
+            remote(ref, ref, sy.at[p, (i + 3) % 4], ry.at[p, (i + 3) % 4], ydev).wait_recv()
+        line = lines[p](1 - y, c)
+        send(line, line, sc.at[p, 1], rc.at[p, 1], cdev)
+
+    def after_c(p):
+        for i, yy in enumerate([y, 1 - y]):
+            ref = lines[p](yy, 1 - c)
+            remote(ref, ref, sc.at[p, i], rc.at[p, i], cdev).wait_recv()
+
+    outs = []
+
+    def put(src, dst):
+        copy = pltpu.make_async_copy(src, dst, out_sem.at[len(outs)])
+        copy.start()
+        outs.append(copy)
+
+    greet([xdev, ydev, cdev] + zdev)
+    for copy in stage:
+        copy.wait()
+    swap_v = send(stv, rcv, sx.at[0], rx.at[0], xdev)
+    swap_q = send(stq, wq.at[s, z, y, c], sx.at[1], rx.at[1], xdev)
+    for copy in own_q:
+        copy.wait()
+    spread(0)
+    swap_u = send(stu, wu.at[s, z, y, c], sx.at[2], rx.at[2], xdev)
+    own_o.wait()
+    spread(3)
+
+    position = lax.broadcasted_iota(jnp.int32, (pos_ref.shape[1], tok.shape[1]), 1) + s * tok.shape[1]
+
+    def chooser(i):
+        return jnp.where(position == pos_ref[i], 1.0, 0.0).astype(bf16)
+
+    get_tok[0].wait()
+    xs[0] = dot_nn(chooser(0), tok[0]).astype(bf16)
+    x_swap = [send(xs.at[0], xr.at[0], sx.at[3], rx.at[3], xdev)]
+    get_tok[1].wait()
+    xs[1] = dot_nn(chooser(1), tok[1]).astype(bf16)
+    x_swap.append(send(xs.at[1], xr.at[1], sx.at[4], rx.at[4], xdev))
+
+    swap_v.wait_recv()
+    gv[z, y, c] = stv[...] + rcv[...]
+    spread(2)
+    remote(wq.at[1 - s, z, y, c], wq.at[1 - s, z, y, c], sx.at[1], rx.at[1], xdev).wait_recv()
+    spread(1)
+    for i in range(2):
+        get_cot[i].wait()
+        ds[i] = dot_nn(chooser(i), cot[i]).astype(bf16)
+    own_u.wait()
+    after_z(0)
+    spread(4)
+    after_z(3)
+    after_z(2)
+    remote(wu.at[1 - s, z, y, c], wu.at[1 - s, z, y, c], sx.at[2], rx.at[2], xdev).wait_recv()
+    spread(5)
+    after_y(0)
+    after_z(1)
+    own_d.wait()
+    spread(6)
+    after_y(3)
+    after_y(2)
+    after_y(1)
+    after_c(0)
+    after_c(3)
+    after_c(2)
+    after_c(1)
+
+    gains[...] = jnp.sum(gv[...].astype(f32).reshape(16, 16, model), axis=0)
+    gain_one, gain_two, router = gains[0:1], gains[1:2], gains[2:3]
+    put(wq, wq_out)
+    put(wo, wo_out)
+    put(gains, gains_out)
+
+    def attend(i):
+        ok = allowed_pairs(bias_ref[i])
+
+        def pair(j, carry):
+            q2 = qkv[i, :, pl.ds(j * 128, 128)].astype(f32)
+            k2 = qkv[i, :, pl.ds(half_q + j * 128, 128)]
+            v2 = qkv[i, :, pl.ds(2 * half_q + j * 128, 128)]
+            mixed = jnp.zeros(q2.shape, f32)
+            for parity in range(2):
+                mask = head_mask(parity)
+                score = dot_nt((q2 * mask).astype(bf16), k2) * (HEAD_DIM**-0.5)
+                score = jnp.where(ok, score, -1000000000.0)
+                weight = jnp.exp(score - jnp.max(score, axis=-1, keepdims=True))
+                total = jnp.sum(weight, axis=-1, keepdims=True)
+                mixed += dot_nn(weight.astype(bf16), v2) / total * mask
+            att[i, :, pl.ds(j * 128, 128)] = mixed.astype(bf16)
+            return carry
+
+        lax.fori_loop(0, half_q // 128, pair, 0)
+
+    d_swap, a_swap = [], []
+    for i in range(2):
+        x_swap[i].wait()
+        row = xr[i].astype(f32) + xs[i].astype(f32)
+        xr[i] = row.astype(bf16)
+        normed = (row * inverse_rms(row) * gain_one).astype(bf16)
+        for j in range(3):
+            qkv[i, :, pl.ds(j * half_q, half_q)] = dot_nn(
+                normed, wq[:, :, :, :, :, pl.ds(j * half_q, half_q)].reshape(model, half_q)
+            ).astype(bf16)
+        attend(i)
+        for j in range(2):
+            cols = pl.ds(j * (model // 2), model // 2)
+            a_s[i, :, cols] = dot_nn(att[i], wo[:, :, :, :, cols].reshape(half_q, model // 2)).astype(bf16)
+        a_swap.append(send(a_s.at[i], a_r.at[i], sx.at[5 + i], rx.at[5 + i], xdev))
+        if i == 0:
+            after_z(4)
+            after_z(5)
+            after_y(4)
+    for i in range(2):
+        d_swap.append(send(ds.at[i], dr.at[i], sx.at[7 + i], rx.at[7 + i], xdev))
+    put(xr, xr_out)
+    put(qkv, qkv_out)
+    put(att, o_out)
+    after_z(6)
+    after_y(5)
+    after_c(4)
+    after_c(5)
+
+    def mlp_up(i):
+        a_swap[i].wait()
+        row = xr[i].astype(f32) + (a_s[i].astype(f32) + a_r[i].astype(f32))
+        hid[i] = row
+        n2[i] = (row * inverse_rms(row) * gain_two).astype(bf16)
+
+        def tile(t, carry):
+            cols = pl.ds(t * 512, 512)
+            up = dot_nn(n2[i], wu[:, :, :, :, :, cols].reshape(model, 512))
+            curve = jnp.tanh(GELU_C * (up + GELU_K * up * up * up))
+            act[i, :, cols] = (0.5 * up * (1.0 + curve)).astype(bf16)
+            slope = 0.5 * (1.0 + curve) + 0.5 * up * (1.0 - curve * curve) * (
+                GELU_C * (1.0 + 3.0 * GELU_K * up * up)
+            )
+            gp[i, :, cols] = slope.astype(bf16)
+            return carry
+
+        lax.fori_loop(0, half_u // 512, tile, 0)
+
+    mlp_up(0)
+    after_y(6)
+    mlp_up(1)
+    put(hid, h_out)
+    after_c(6)
+
+    def mlp_back(i):
+        d_swap[i].wait()
+        cot_row = dr[i].astype(f32) + ds[i].astype(f32)
+        dr[i] = cot_row.astype(bf16)
+        gate = jax.nn.sigmoid(jnp.sum(xr[i].astype(f32) * router, axis=-1, keepdims=True))
+        dm[i] = (gate * cot_row).astype(bf16)
+
+        def tile(t, carry):
+            cols = pl.ds(t * 512, 512)
+            back = dot_nt(dm[i], wd[t].reshape(512, model))
+            gp[i, :, cols] = (back * gp[i, :, cols].astype(f32)).astype(bf16)
+            return carry
+
+        lax.fori_loop(0, half_u // 512, tile, 0)
+        for j in range(2):
+            cols = pl.ds(j * (model // 2), model // 2)
+            d2s[i, :, cols] = dot_nt(gp[i], wu[j].reshape(model // 2, half_u)).astype(bf16)
+        return send(d2s.at[i], d2r.at[i], sx.at[9 + i], rx.at[9 + i], xdev)
+
+    d2_swap = [mlp_back(0), mlp_back(1)]
+    put(dr, dr_out)
+    put(d2s, d2s_out)
+    rows = act.shape[0] * act.shape[1]
+
+    def down_tile(t, carry):
+        part = dot_tn(act[:, :, pl.ds(t * 512, 512)].reshape(rows, 512), dm[...].reshape(rows, model))
+        gd[t] = part.astype(bf16).reshape(gd.shape[1:])
+        return carry
+
+    lax.fori_loop(0, half_u // 512, down_tile, 0)
+    put(gd, gd_out)
+
+    def up_tile(t, carry):
+        cols = pl.ds(t * 512, 512)
+        part = dot_tn(n2[...].reshape(rows, model), gp[:, :, cols].reshape(rows, 512))
+        gu[:, :, :, :, :, cols] = part.astype(bf16).reshape(gu.shape[:5] + (512,))
+        return carry
+
+    lax.fori_loop(0, half_u // 512, up_tile, 0)
+    put(gu, gu_out)
+    for i in range(2):
+        for j in range(2):
+            cols = pl.ds(j * (model // 2), model // 2)
+            m_s[i, :, cols] = dot_nn(act[i], wd[:, :, :, :, cols].reshape(half_u, model // 2)).astype(bf16)
+    put(m_s, ms_out)
+    for copy in d2_swap:
+        copy.wait_recv()
+    put(d2r, d2r_out)
+    waited = x_swap + a_swap + d_swap
+    for copy in sent:
+        if not any(copy is other for other in waited):
+            copy.wait_send()
+    for copy in outs:
+        copy.wait()
+
+
+def second_kernel(
+    xr_in, dr_in, h_in, qkv_in, o_in, wq_in, wo_in, gains_in, gd_in, gu_in, d2s_in, d2r_in, ms_in, live_ref, bias_ref,
+    upd_out, dx_out, fq_out, fo_out, fu_out, fd_out, vec_out,
+    xr, dr, hid, qkv, att, wq, wo, gains, d2s, d2r, m_s, m_r, n1, dh, da, do, dqkv, d1s, d1r, upd, dx, logit,
+    go, gq, lcd, lcu, rcd, rcu, rco, rcq, ryd, ryu, ryo, ryq, rzd, rzu, rzo, rzq,
+    fq, fo, fu, fd, suq, suu, ruq, ruu, vs, vr, v_all,
+    loc, out_sem, sc, rc, sy, ry, sz, rz, sx, rx,
+):
+    s, z, y, c = place()
+    xdev, ydev, cdev = device(1 - s, z, y, c), device(s, z, 1 - y, c), device(s, z, y, 1 - c)
+    zdev = [device(s, lax.rem(z + i + 1, LINE), y, c) for i in range(3)]
+    model, half_q, half_u = xr.shape[2], att.shape[2], fu.shape[2]
+    rows = xr.shape[0] * xr.shape[1]
+    local, sent, outs = [], [], []
+
+    def fetch(src, dst):
+        copy = pltpu.make_async_copy(src, dst, loc.at[len(local)])
+        copy.start()
+        local.append(copy)
+        return copy
+
+    def send(src, dst, send_sem, recv_sem, target):
+        copy = remote(src, dst, send_sem, recv_sem, target)
+        copy.start()
+        sent.append(copy)
+        return copy
+
+    def put(src, dst):
+        copy = pltpu.make_async_copy(src, dst, out_sem.at[len(outs)])
+        copy.start()
+        outs.append(copy)
+
+    half_d = lcd.shape[3]
+    other = [
+        lambda cc, i=i: gd_in.at[:, :, cc, pl.ds(half_d * i, half_d)] for i in range(2)
+    ] + [lambda cc, i=i: gu_in.at[i, :, :, cc] for i in range(2)] + [lambda cc: go.at[:, :, cc]] + [
+        lambda cc, i=i: gq.at[i, :, :, cc] for i in range(2)
+    ]
+    land_c = [rcd.at[0], rcd.at[1], rcu.at[0], rcu.at[1], rco.at[0], rcq.at[0], rcq.at[1]]
+    land_y = [ryd.at[0], ryd.at[1], ryu.at[0], ryu.at[1], ryo.at[0], ryq.at[0], ryq.at[1]]
+    land_z = [rzd.at[0], rzd.at[1], rzu.at[0], rzu.at[1], rzo.at[0], rzq.at[0], rzq.at[1]]
+
+    def c_start(k):
+        return send(other[k](1 - c), land_c[k], sc.at[k], rc.at[k], cdev)
+
+    def c_end(k, own):
+        remote(land_c[k], land_c[k], sc.at[k], rc.at[k], cdev).wait_recv()
+        ref = land_c[k]
+
+        def add(i, carry):
+            ref[i] = (ref[i].astype(f32) + own(i).astype(f32)).astype(bf16)
+            return carry
+
+        lax.fori_loop(0, LINE, add, 0)
+        send(ref.at[:, 1 - y], land_y[k], sy.at[k], ry.at[k], ydev)
+
+    def y_end(k):
+        ref = land_y[k]
+        remote(ref, ref, sy.at[k], ry.at[k], ydev).wait_recv()
+
+        def add(i, carry):
+            ref[i] = (ref[i].astype(f32) + land_c[k][i, y].astype(f32)).astype(bf16)
+            return carry
+
+        lax.fori_loop(0, LINE, add, 0)
+        for i in range(3):
+            send(ref.at[lax.rem(z + i + 1, LINE)], land_z[k].at[i], sz.at[k, i], rz.at[k, i], zdev[i])
+
+    def z_end(k):
+        total = land_y[k][z].astype(f32)
+        for i in range(3):
+            remote(land_z[k].at[i], land_z[k].at[i], sz.at[k, i], rz.at[k, i], zdev[i]).wait_recv()
+            total += land_z[k][i].astype(f32)
+        return total
+
+    get_d2 = [fetch(d2s_in, d2s), fetch(d2r_in, d2r), fetch(h_in, hid), fetch(gains_in, gains), fetch(dr_in, dr), fetch(xr_in, xr)]
+    get_m = fetch(ms_in, m_s)
+    get_own = [fetch(other[k](c), (lcd.at[k] if k < 2 else lcu.at[k - 2])) for k in range(4)]
+    get_att = [fetch(wo_in, wo), fetch(o_in, att), fetch(qkv_in, qkv)]
+    get_wq = fetch(wq_in, wq)
+    greet([xdev, ydev, cdev] + zdev)
+    for k in range(4):
+        c_start(k)
+    get_m.wait()
+    m_swap = [send(m_s.at[i], m_r.at[i], sx.at[i], rx.at[i], xdev) for i in range(2)]
+    for k in range(2):
+        get_own[k].wait()
+        c_end(k, lambda i, k=k: lcd[k, i])
+    for copy in get_d2:
+        copy.wait()
+    gain_one, gain_two, router = gains[0:1], gains[1:2], gains[2:3]
+
+    def gate_of(i):
+        return jax.nn.sigmoid(jnp.sum(xr[i].astype(f32) * router, axis=-1, keepdims=True))
+
+    def hidden_back(i):
+        back = d2s[i].astype(f32) + d2r[i].astype(f32)
+        row = hid[i]
+        r2 = inverse_rms(row)
+        scaled = back * gain_two
+        step = r2 * scaled - row * (r2 * r2 * r2 * jnp.mean(scaled * row, axis=-1, keepdims=True))
+        dh[i] = step
+        da[i] = (gate_of(i) * dr[i].astype(f32) + step).astype(bf16)
+        for j in range(1):
+            do[i] = dot_nt(da[i], wo[...].reshape(half_q, model)).astype(bf16)
+        return jnp.sum(d2s[i].astype(f32) * row * r2, axis=0, keepdims=True)
+
+    def attend_back(i):
+        ok = allowed_pairs(bias_ref[i])
+        scale = HEAD_DIM**-0.5
+
+        def pair(j, carry):
+            q2 = qkv[i, :, pl.ds(j * 128, 128)]
+            k2 = qkv[i, :, pl.ds(half_q + j * 128, 128)]
+            v2 = qkv[i, :, pl.ds(2 * half_q + j * 128, 128)]
+            g2 = do[i, :, pl.ds(j * 128, 128)].astype(f32)
+            q2f = q2.astype(f32)
+            dq2 = jnp.zeros(q2.shape, f32)
+            dk2 = jnp.zeros(q2.shape, f32)
+            dv2 = jnp.zeros(q2.shape, f32)
+            for parity in range(2):
+                mask = head_mask(parity)
+                score = dot_nt((q2f * mask).astype(bf16), k2) * scale
+                score = jnp.where(ok, score, -1000000000.0)
+                weight = jnp.exp(score - jnp.max(score, axis=-1, keepdims=True))
+                over = 1.0 / jnp.sum(weight, axis=-1, keepdims=True)
+                gh = g2 * mask
+                dp = dot_nt(gh.astype(bf16), v2)
+                prob = weight * over
+                delta = jnp.sum(prob * dp, axis=-1, keepdims=True)
+                dscore = (prob * (dp - delta)).astype(bf16)
+                dq2 += dot_nn(dscore, k2) * mask
+                dk2 += dot_tn(dscore, q2) * mask
+                dv2 += dot_tn(weight.astype(bf16), (gh * over).astype(bf16))
+            dqkv[i, :, pl.ds(j * 128, 128)] = (dq2 * scale).astype(bf16)
+            dqkv[i, :, pl.ds(half_q + j * 128, 128)] = (dk2 * scale).astype(bf16)
+            dqkv[i, :, pl.ds(2 * half_q + j * 128, 128)] = dv2.astype(bf16)
+            return carry
+
+        lax.fori_loop(0, half_q // 128, pair, 0)
+
+    def inner_back(i):
+        row = xr[i].astype(f32)
+        r1 = inverse_rms(row)
+        n1[i] = (row * r1 * gain_one).astype(bf16)
+        grad = jnp.zeros((1, model // 2), f32)
+        parts = []
+        for j in range(2):
+            cols = pl.ds(j * (model // 2), model // 2)
+            part = dot_nt(dqkv[i], wq[j].reshape(model // 2, 3 * half_q))
+            d1s[i, :, cols] = part.astype(bf16)
+            parts.append(jnp.sum(part * xr[i, :, cols].astype(f32) * r1, axis=0, keepdims=True))
+        swap = send(d1s.at[i], d1r.at[i], sx.at[2 + i], rx.at[2 + i], xdev)
+        return swap, parts
+
+    for copy in get_att:
+        copy.wait()
+    grad_gm = hidden_back(0)
+    get_own[2].wait()
+    c_end(2, lambda i: lcu[0, i])
+    attend_back(0)
+    get_own[3].wait()
+    c_end(3, lambda i: lcu[1, i])
+    get_wq.wait()
+    swap_0, parts_0 = inner_back(0)
+    y_end(0)
+    grad_gm += hidden_back(1)
+    attend_back(1)
+    swap_1, parts_1 = inner_back(1)
+    d1_swap = [swap_0, swap_1]
+    y_end(1)
+
+    for j in range(2):
+        cols = pl.ds(j * (model // 2), model // 2)
+        vs[0:1, cols] = parts_0[j] + parts_1[j]
+    vs[1:2] = grad_gm
+
+    for t in range(2):
+        cols = pl.ds(t * (model // 2), model // 2)
+        part = dot_tn(att[...].reshape(rows, half_q), da[:, :, cols].reshape(rows, model // 2))
+        go[:, :, :, :, cols] = part.astype(bf16).reshape(go.shape[:4] + (model // 2,))
+    c_start(4)
+
+    def qkv_tile(t, carry):
+        cols = pl.ds(t * half_q, half_q)
+        part = dot_tn(n1[...].reshape(rows, model), dqkv[:, :, cols].reshape(rows, half_q))
+        gq[:, :, :, :, :, cols] = part.astype(bf16).reshape(gq.shape[:5] + (half_q,))
+        return carry
+
+    lax.fori_loop(0, 3, qkv_tile, 0)
+    c_start(5)
+    c_start(6)
+    c_end(4, lambda i: go[i, :, c])
+
+    grad_router = jnp.zeros((1, model), f32)
+    for i in range(2):
+        m_swap[i].wait()
+        row = xr[i].astype(f32)
+        gate = gate_of(i)
+        branch = (hid[i] - row) + (m_s[i].astype(f32) + m_r[i].astype(f32))
+        upd[i] = (gate * branch * live_ref[i]).astype(bf16)
+        slope = jnp.sum(dr[i].astype(f32) * branch, axis=-1, keepdims=True) * gate * (1.0 - gate)
+        logit[i] = slope
+        grad_router += jnp.sum(row * slope, axis=0, keepdims=True)
+    put(upd, upd_out)
+    vs[2:3] = 0.5 * grad_router
+    vs[3:8] = jnp.zeros((5, model), f32)
+    send(vs, vr.at[0], sc.at[7], rc.at[7], cdev)
+    c_end(5, lambda i: gq[0, i, :, c])
+    c_end(6, lambda i: gq[1, i, :, c])
+
+    y_end(2)
+    fd[0:half_d] = z_end(0)
+    y_end(3)
+    fd[half_d:] = z_end(1)
+    put(fd, fd_out)
+    remote(vs, vr.at[0], sc.at[7], rc.at[7], cdev).wait_recv()
+    v_all[0] = vs[...] + vr[0]
+    send(v_all.at[0], vr.at[1], sy.at[7], ry.at[7], ydev)
+    y_end(4)
+    fu[0] = z_end(2)
+
+    for i in range(2):
+        d1_swap[i].wait()
+        row = xr[i].astype(f32)
+        r1 = inverse_rms(row)
+        scaled = (d1s[i].astype(f32) + d1r[i].astype(f32)) * gain_one
+        step = r1 * scaled - row * (r1 * r1 * r1 * jnp.mean(scaled * row, axis=-1, keepdims=True))
+        dx[i] = (dh[i] + step + logit[i] * router).astype(bf16)
+    put(dx, dx_out)
+
+    fu[1] = z_end(3)
+    suu[...] = fu[1 - s].astype(bf16)
+    send(suu, ruu, sx.at[4], rx.at[4], xdev)
+    remote(vs, vr.at[1], sy.at[7], ry.at[7], ydev).wait_recv()
+    v_all[1] = v_all[0] + vr[1]
+    for i in range(3):
+        send(v_all.at[1], vr.at[2 + i], sz.at[7, i], rz.at[7, i], zdev[i])
+    y_end(5)
+    fo[...] = z_end(4)
+    put(fo, fo_out)
+    y_end(6)
+    for i in range(3):
+        remote(vs, vr.at[2 + i], sz.at[7, i], rz.at[7, i], zdev[i]).wait_recv()
+    v_all[2] = v_all[1] + vr[2] + vr[3] + vr[4]
+    send(v_all.at[2], vr.at[5], sx.at[6], rx.at[6], xdev)
+    put(fu.at[s], fu_out.at[:, pl.ds(s * half_u, half_u)])
+    fq[0] = z_end(5)
+    remote(ruu, ruu, sx.at[4], rx.at[4], xdev).wait_recv()
+    fu[1 - s] = ruu[...].astype(f32)
+    put(fu.at[1 - s], fu_out.at[:, pl.ds((1 - s) * half_u, half_u)])
+    fq[1] = z_end(6)
+    suq[...] = fq[1 - s].astype(bf16)
+    send(suq, ruq, sx.at[5], rx.at[5], xdev)
+    for j in range(3):
+        put(fq.at[s, :, pl.ds(j * half_q, half_q)], fq_out.at[:, pl.ds(2 * j * half_q + s * half_q, half_q)])
+    remote(vs, vr.at[5], sx.at[6], rx.at[6], xdev).wait_recv()
+    v_all[3] = v_all[2] + vr[5]
+    put(v_all.at[3], vec_out)
+    remote(ruq, ruq, sx.at[5], rx.at[5], xdev).wait_recv()
+    fq[1 - s] = ruq[...].astype(f32)
+    for j in range(3):
+        put(fq.at[1 - s, :, pl.ds(j * half_q, half_q)], fq_out.at[:, pl.ds(2 * j * half_q + (1 - s) * half_q, half_q)])
+    waited = m_swap + d1_swap
+    for copy in sent:
+        if not any(copy is item for item in waited):
+            copy.wait_send()
+    for copy in outs:
+        copy.wait()
+
+
+def split_device(
+    tokens, cotangent, lengths, routed, w_qkv, w_out, w_up, w_down, gain_attn, gain_mlp, router
+):
+    slots, local_len, model = tokens.shape
+    ranks = routed.shape[1]
+    half_q, half_u = w_qkv.shape[1] // 6, w_up.shape[1] // 2
+    part, down = w_qkv.shape[0], w_down.shape[0]
+    s = lax.axis_index("seq")
+    flat = s * lax.axis_size("batch") + lax.axis_index("batch")
+    rank_all = jnp.arange(ranks, dtype=jnp.int32)
+    live = rank_all[None, :] < (lengths // 8)[:, None]
+    where_live = jnp.where(live, routed, -1)
+    bias = jnp.where(live, 0.0, -1000000000.0).astype(f32)[:, None, :]
+    lane = jnp.arange(model, dtype=jnp.int32)
+    small = jnp.stack([gain_attn, gain_mlp, router])
+    vec = jnp.where(lane[None, :] // part == flat, jnp.tile(small, (1, model // part)), 0)
+    vec = jnp.pad(vec, ((0, 13), (0, 0)))
+
+    hbm = pl.BlockSpec(memory_space=pl.ANY)
+    vmem = pl.BlockSpec(memory_space=pltpu.VMEM)
+    sds = jax.ShapeDtypeStruct
+    dma = pltpu.SemaphoreType.DMA
+    rows = (slots, ranks, model)
+    grid = (LINE, 2, 2)
+    wq_shape, wo_shape = (2,) + grid + (part, 3 * half_q), grid + (part, model)
+    wu_shape, wd_shape = (2,) + grid + (part, half_u), grid + (down, model)
+    first = pl.pallas_call(
+        first_kernel,
+        out_shape=(
+            sds(rows, bf16), sds(rows, bf16), sds(rows, f32), sds((slots, ranks, 3 * half_q), bf16),
+            sds((slots, ranks, half_q), bf16), sds(wq_shape, bf16), sds(wo_shape, bf16), sds((16, model), f32),
+            sds(wd_shape, bf16), sds(wu_shape, bf16), sds(rows, bf16), sds(rows, bf16), sds(rows, bf16),
+        ),
+        in_specs=[hbm] * 7 + [vmem] * 2,
+        out_specs=[hbm] * 13,
+        scratch_shapes=[
+            pltpu.VMEM(tokens.shape, bf16), pltpu.VMEM(tokens.shape, bf16),
+            pltpu.VMEM(wq_shape, bf16), pltpu.VMEM(wo_shape, bf16), pltpu.VMEM(wu_shape, bf16), pltpu.VMEM(wd_shape, bf16),
+            pltpu.VMEM(grid + (16, model), bf16),
+            pltpu.VMEM((part, 3 * half_q), bf16), pltpu.VMEM((part, half_u), bf16),
+            pltpu.VMEM((16, model), bf16), pltpu.VMEM((16, model), bf16),
+            pltpu.VMEM(rows, bf16), pltpu.VMEM(rows, bf16), pltpu.VMEM(rows, bf16), pltpu.VMEM(rows, bf16),
+            pltpu.VMEM(rows, bf16), pltpu.VMEM(rows, bf16), pltpu.VMEM(rows, f32), pltpu.VMEM(rows, bf16),
+            pltpu.VMEM((slots, ranks, 3 * half_q), bf16), pltpu.VMEM((slots, ranks, half_q), bf16),
+            pltpu.VMEM((slots, ranks, half_u), bf16), pltpu.VMEM((slots, ranks, half_u), bf16),
+            pltpu.VMEM(rows, bf16), pltpu.VMEM(rows, bf16), pltpu.VMEM(rows, bf16), pltpu.VMEM(rows, bf16),
+            pltpu.VMEM(wd_shape, bf16), pltpu.VMEM(wu_shape, bf16), pltpu.VMEM((16, model), f32),
+            dma((16,)), dma((13,)), dma((7, 3)), dma((7, 3)), dma((7, 4)), dma((7, 4)), dma((7, 2)), dma((7, 2)),
+            dma((11,)), dma((11,)),
+        ],
+        compiler_params=pltpu.CompilerParams(collective_id=1, has_side_effects=True, vmem_limit_bytes=60 << 20),
+        name="gather_and_forward",
+    )
+    xr, dr, hid, qkv, att, wq, wo, gains, gd, gu, d2s, d2r, m_s = first(
+        tokens, cotangent, vec, w_qkv, w_out, w_up, w_down, where_live[:, :, None], bias
+    )
+    land = lambda chunks, tall, wide: [
+        pltpu.VMEM((chunks, LINE, 2, tall, wide), bf16),
+        pltpu.VMEM((chunks, LINE, tall, wide), bf16),
+        pltpu.VMEM((chunks, 3, tall, wide), bf16),
+    ]
+    on_d, on_u, on_o, on_q = (
+        land(2, down // 2, model), land(2, part, half_u), land(1, part, model), land(2, part, 3 * half_q)
+    )
+    upd, dxr, grad_qkv, grad_out, grad_up, grad_down, vec_sum = pl.pallas_call(
+        second_kernel,
+        out_shape=(
+            sds(rows, bf16), sds(rows, bf16), sds((part, 6 * half_q), f32), sds((part, model), f32),
+            sds((part, 2 * half_u), f32), sds((down, model), f32), sds((8, model), f32),
+        ),
+        in_specs=[hbm] * 13 + [vmem] * 2,
+        out_specs=[hbm] * 7,
+        scratch_shapes=[
+            pltpu.VMEM(rows, bf16), pltpu.VMEM(rows, bf16), pltpu.VMEM(rows, f32),
+            pltpu.VMEM((slots, ranks, 3 * half_q), bf16), pltpu.VMEM((slots, ranks, half_q), bf16),
+            pltpu.VMEM(wq_shape, bf16), pltpu.VMEM(wo_shape, bf16), pltpu.VMEM((16, model), f32),
+            pltpu.VMEM(rows, bf16), pltpu.VMEM(rows, bf16), pltpu.VMEM(rows, bf16), pltpu.VMEM(rows, bf16),
+            pltpu.VMEM(rows, bf16), pltpu.VMEM(rows, f32), pltpu.VMEM(rows, bf16),
+            pltpu.VMEM((slots, ranks, half_q), bf16), pltpu.VMEM((slots, ranks, 3 * half_q), bf16),
+            pltpu.VMEM(rows, bf16), pltpu.VMEM(rows, bf16), pltpu.VMEM(rows, bf16), pltpu.VMEM(rows, bf16),
+            pltpu.VMEM((slots, ranks, 1), f32),
+            pltpu.VMEM(wo_shape, bf16), pltpu.VMEM(wq_shape, bf16), on_d[0], on_u[0],
+            on_d[0], on_u[0], on_o[0], on_q[0], on_d[1], on_u[1], on_o[1], on_q[1], on_d[2], on_u[2], on_o[2], on_q[2],
+            pltpu.VMEM((2, part, 3 * half_q), f32), pltpu.VMEM((part, model), f32),
+            pltpu.VMEM((2, part, half_u), f32), pltpu.VMEM((down, model), f32),
+            pltpu.VMEM((part, 3 * half_q), bf16), pltpu.VMEM((part, half_u), bf16),
+            pltpu.VMEM((part, 3 * half_q), bf16), pltpu.VMEM((part, half_u), bf16),
+            pltpu.VMEM((8, model), f32), pltpu.VMEM((6, 8, model), f32), pltpu.VMEM((4, 8, model), f32),
+            dma((16,)), dma((13,)), dma((8,)), dma((8,)), dma((8,)), dma((8,)), dma((8, 3)), dma((8, 3)),
+            dma((7,)), dma((7,)),
+        ],
+        compiler_params=pltpu.CompilerParams(collective_id=2, has_side_effects=True, vmem_limit_bytes=60 << 20),
+        name="backward_and_sum",
+    )(xr, dr, hid, qkv, att, wq, wo, gains, gd, gu, d2s, d2r, m_s, live[:, :, None].astype(f32), bias)
+
+    positions = s * local_len + jnp.arange(local_len, dtype=jnp.int32)
+    chooser = (where_live[:, :, None] == positions[None, None, :]).astype(bf16)
+
+    def place_rows(base, moved):
+        return (
+            base.astype(f32) + jnp.einsum("scp,scd->spd", chooser, moved, preferred_element_type=f32)
+        ).astype(bf16)
+
+    mine = lax.dynamic_slice(vec_sum, (0, flat * part), (8, part))
+    return (
+        place_rows(tokens, upd), place_rows(cotangent, dxr), grad_qkv, grad_out, grad_up, grad_down,
+        mine[0], mine[1], mine[2],
+    )
+
+
 def solution(mesh):
     in_specs = (
         P("batch", "seq", None),
@@ -227,6 +950,6 @@
         P(("seq", "batch")),
         P(("seq", "batch")),
     )
-    return jax.shard_map(
-        per_device, mesh=mesh, in_specs=in_specs, out_specs=out_specs, check_vma=False
-    )
+    small_slice = mesh.shape["seq"] == 2 and mesh.shape["batch"] == 4 * LINE
+    body = split_device if small_slice else general_device
+    return jax.shard_map(body, mesh=mesh, in_specs=in_specs, out_specs=out_specs, check_vma=False)

time: 1070 us -> 254 us (0.24)
  waiting for transfers between devices: 782 us -> 0 us
  Pallas kernels: 0 us -> 236 us
  matrix products: 108 us -> 8.05 us
  blocking collectives: 82 us -> 0 us
  local copies, waits for them, and re-layouts: 58.9 us -> 5.87 us
  between operations: 17.4 us -> 0.73 us
  other arithmetic: 15.1 us -> 3.65 us
    reduce_scatter x6 -> x0, waiting for transfers between devices: 470 us -> none  [the longest x4 470 us: sum_rows(): lax.psum_scatter(part.astype(bf16), ('seq', 'batch'), scatter_dimension=0...]
    all_gather x8 -> x0, waiting for transfers between devices: 260 us -> none  [the longest x1 75.7 us: per_device(): lax.all_gather(w_up, ('seq', 'batch'), axis=0, tiled=True)]
    pallas_call x0 -> x2, Pallas kernels: none -> 236 us  [the longest x1 128 us: split_device(): first(tokens, cotangent, vec, w_qkv, w_out, w_up, w_down, where_live[:, :...]
    dot_general x23 -> x2, matrix products: 108 us -> 8.05 us  [place_rows(): jnp.einsum('scp,scd->spd', chooser, moved, preferred_element_type=f32)]
    unnamed x2 -> x0, blocking collectives: 82 us -> none
    unnamed x16 -> x0, waiting for transfers between devices: 51.4 us -> none
    reshape x17 -> x0, local copies, waits for them, and re-layouts: 22.5 us -> none  [the longest x2 5.56 us: per_device(): grad_att4 = grad_att.reshape(own_count, slot_count, head_count, HEAD_DIM)]
    convert_element_type x6 -> x0, local copies, waits for them, and re-layouts: 13.2 us -> none  [the longest x2 3.97 us: per_device(): attended = mixture.reshape(row_count, model_width).astype(bf16)]
  transfers between devices with their start and end apart: 15 -> 0, of which waited for: 11 -> 0; matrix products, arithmetic and copies ran while one was open for 11% -> 0% of each run, Pallas kernels for 0% -> 0%
where the time goes in v2:
time: 254 us
  Pallas kernels  236 us (93%)
  matrix products  8.05 us (3%)
  local copies, waits for them, and re-layouts  5.87 us (2%)
  other arithmetic  3.65 us (1%)
    pallas_call x1, Pallas kernels, split_device(): first(tokens, cotangent, vec, w_qkv, w_out, w_up, w_down, where_live[:, :...  128 us
    pallas_call x1, Pallas kernels, split_device(): pl.pallas_call(second_kernel, out_shape=(sds(rows, bf16), sds(rows, bf16)...  108 us
    dot_general x2, matrix products, place_rows(): jnp.einsum('scp,scd->spd', chooser, moved, preferred_element_type=f32)  8.05 us

profile of v2, /device:TPU:0, one launch (start us, length us, event | category | flops | bytes accessed | tf_op | source)
XLA Modules:
  0.0 253.9 jit_solution(8094419241275810919)
XLA Ops:
  0.7 0.7 pad_maximum_fusion
  1.4 0.1 tile.10
  1.5 0.6 pad.4.vec_hbm
  2.1 0.7 and_select_fusion
  2.8 0.7 compare_select_fusion.bias_ref
  3.4 0.8 fusion.13
  4.2 0.9 copy.20.pos_ref
  5.0 127.8 %gather_and_forward.1 = (bf16[2,256,1024]{2,1,0:T(8,128)(2,1)}, bf16[2,256,1024]{2,1,0:T(8,128)(2,1)}, f32[2,256,1024]{2,1,0:T(8,128)}, bf16[2,256,1536]{2,1,0:T...) custom-call(bf16[2,1024,1024]{2,1,0:T(8,128)(2,1)} %tok_hbm.1, ...), custom_call_target="tpu_custom_call" | custom-call | tf_op jit(solution)/shard_map/gather_and_forward/pallas_call | solution.py:871
  132.9 0.8 fusion.6.live_ref
  133.7 0.0 copy-start.6
  133.7 107.7 %backward_and_sum.1 = (bf16[2,256,1024]{2,1,0:T(8,128)(2,1)}, bf16[2,256,1024]{2,1,0:T(8,128)(2,1)}, f32[32,3072]{1,0:T(8,128)}, f32[32,1024]{1,0:T(8,128)}, f32...) custom-call(bf16[2,256,1024]{2,1,0:T(8,128)(2,1)} %get-tuple-element.29.xr_in, ...), custom_call_target="tpu_custom_call" | custom-call | tf_op jit(solution)/shard_map/backward_and_sum/pallas_call | solution.py:882
  241.4 0.0 copy-done.6
  241.4 0.1 compare_select_fusion.1
  241.5 0.0 copy-start
  241.5 0.0 copy-start.1
  241.5 5.0 %add_convert_fusion = bf16[2,1024,1024]{2,1,0:T(8,128)(2,1)} fusion(bf16[2,1024,1024]{2,1,0:T(8,128)(2,1)} %cot_hbm.1, bf16[2,256,1024]{2,1,0:T(8,128)(2,1)} %get-tuple-element.43, s32[2,256]{1,0:T(2,128)S(1)} %compare_select_fusion.1, s32[1024]{0:T(1024)S(1)} %iota_add_fusion), kind=kOutput, calls=%fused_computation | convolution fusion | flops 1080557568 | bytes 9443328 | tf_op jit(solution)/shard_map/scp,scd->spd/dot_general | solution.py:918
  246.5 0.0 copy-done
  246.5 0.0 copy-done.1
  246.5 0.0 copy-start.4
  246.5 0.0 copy-start.5
  246.5 0.0 copy-start.3
  246.6 0.0 copy-start.2
  246.6 3.1 %add_convert_fusion.1 = bf16[2,1024,1024]{2,1,0:T(8,128)(2,1)} fusion(bf16[2,1024,1024]{2,1,0:T(8,128)(2,1)S(1)} %copy-done, bf16[2,256,1024]{2,1,0:T(8,128)(2,1)S(1)} %copy-done.1, s32[2,256]{1,0:T(2,128)S(1)} %compare_select_fusion.1, s32[1024]{0:T(1024)S(1)} %iota_add_fusion), kind=kOutput, calls=%fused_computation.1 | convolution fusion | flops 1080557568 | bytes 9443328 | tf_op jit(solution)/shard_map/scp,scd->spd/dot_general | solution.py:918
  249.6 0.7 constant_dynamic-slice_fusion
  250.4 0.5 slice_bitcast_fusion
  250.9 0.0 copy-done.4
  250.9 0.7 copy.25
  251.6 0.0 copy-done.5
  251.6 0.7 copy.26
  252.3 0.0 copy-done.3
  252.3 0.8 copy.27
  253.1 0.0 copy-done.2
  253.1 0.8 copy.28
  (4 shorter events, 0.0 us)
Async XLA Ops:
  133.7 107.8 %copy-start.6 = (s32[2,256]{1,0:T(2,128)S(1)}, s32[2,256]{1,0:T(2,128)}, u32[]{:S(2)}) copy-start(s32[2,256]{1,0:T(2,128)} %param.14) | copy-start | bytes 6148
  241.5 5.0 %copy-start = (bf16[2,1024,1024]{2,1,0:T(8,128)(2,1)S(1)}, bf16[2,1024,1024]{2,1,0:T(8,128)(2,1)}, u32[]{:S(2)}) copy-start(bf16[2,1024,1024]{2,1,0:T(8,128)(2,1)} %tok_hbm.1) | copy-start | bytes 12582916
  241.5 5.0 %copy-start.1 = (bf16[2,256,1024]{2,1,0:T(8,128)(2,1)S(1)}, bf16[2,256,1024]{2,1,0:T(8,128)(2,1)}, u32[]{:S(2)}) copy-start(bf16[2,256,1024]{2,1,0:T(8,128)(2,1)} %get-tuple-element.42) | copy-start | bytes 3145732
  246.5 4.4 %copy-start.4 = (f32[32,3072]{1,0:T(8,128)S(1)}, f32[32,3072]{1,0:T(8,128)}, u32[]{:S(2)}) copy-start(f32[32,3072]{1,0:T(8,128)} %get-tuple-element.63) | copy-start | bytes 1179652
  246.5 5.1 %copy-start.5 = (f32[32,1024]{1,0:T(8,128)S(1)}, f32[32,1024]{1,0:T(8,128)}, u32[]{:S(2)}) copy-start(f32[32,1024]{1,0:T(8,128)} %get-tuple-element.64) | copy-start | bytes 393220
  246.5 5.8 %copy-start.3 = (f32[32,4096]{1,0:T(8,128)S(1)}, f32[32,4096]{1,0:T(8,128)}, u32[]{:S(2)}) copy-start(f32[32,4096]{1,0:T(8,128)} %get-tuple-element.65) | copy-start | bytes 1572868
  246.6 6.5 %copy-start.2 = (f32[128,1024]{1,0:T(8,128)S(1)}, f32[128,1024]{1,0:T(8,128)}, u32[]{:S(2)}) copy-start(f32[128,1024]{1,0:T(8,128)} %get-tuple-element.66) | copy-start | bytes 1572868

commit v3 on v1

--- a/solution.py
+++ b/solution.py
@@ -1,13 +1,68 @@
+import functools
+
 import jax
 import jax.numpy as jnp
 from jax import lax
+from jax.experimental import pallas as pl
+from jax.experimental.pallas import tpu as pltpu
 from jax.sharding import PartitionSpec as P
 
 HEAD_DIM = 64
+MESH = pl.DeviceIdType.MESH
 
 
 epsilon = 1e-05
 highest = lax.Precision.HIGHEST
+f32 = jnp.float32
+bf16 = jnp.bfloat16
+
+LINE = 4
+GELU_C = 0.7978845608
+GELU_K = 0.044715
+
+
+def dot_nn(a, b):
+    return lax.dot_general(a, b, (((1,), (0,)), ((), ())), preferred_element_type=f32)
+
+
+def dot_nt(a, b):
+    return lax.dot_general(a, b, (((1,), (1,)), ((), ())), preferred_element_type=f32)
+
+
+def dot_tn(a, b):
+    return lax.dot_general(a, b, (((0,), (0,)), ((), ())), preferred_element_type=f32)
+
+
+def place():
+    s = lax.axis_index("seq")
+    b = lax.axis_index("batch")
+    return s, b // 4, lax.rem(b // 2, 2), lax.rem(b, 2)
+
+
+def device(s, z, y, c):
+    return (s, z * 4 + y * 2 + c)
+
+
+def remote(src, dst, send, recv, target):
+    return pltpu.make_async_remote_copy(
+        src_ref=src, dst_ref=dst, send_sem=send, recv_sem=recv, device_id=target, device_id_type=MESH
+    )
+
+
+def greet(targets):
+    barrier = pltpu.get_barrier_semaphore()
+    for target in targets:
+        pl.semaphore_signal(barrier, inc=1, device_id=target, device_id_type=MESH)
+    pl.semaphore_wait(barrier, len(targets))
+
+
+def inverse_rms(values):
+    return lax.rsqrt(jnp.mean(values * values, axis=-1, keepdims=True) + epsilon)
+
+
+def head_mask(parity):
+    lane = lax.broadcasted_iota(jnp.int32, (1, 128), 1)
+    return jnp.where(lane // HEAD_DIM == parity, 1.0, 0.0).astype(f32)
 
 
 def norm_apply(values_in, gain_vec):
@@ -22,7 +77,7 @@
     return jax.nn.gelu(values_in, approximate=True)
 
 
-def per_device(
+def general_device(
     tokens, cotangent, lengths, routed, w_qkv, w_out, w_up, w_down, gain_attn, gain_mlp, router
 ):
     slot_count, local_len, model_width = tokens.shape
@@ -32,8 +87,6 @@
     head_count = model_width // HEAD_DIM
     row_count = own_count * slot_count
     score_scale = HEAD_DIM ** (-0.5)
-    f32 = jnp.float32
-    bf16 = jnp.bfloat16
     gathered = (
         lax.all_gather(w_qkv, ("seq", "batch"), axis=0, tiled=True),
         lax.all_gather(w_out, ("seq", "batch"), axis=0, tiled=True),
@@ -202,6 +255,702 @@
     )
 
 
+def block_kernel(
+    tok_hbm, cot_hbm, wq_hbm, wo_hbm, wu_hbm, wd_hbm, small_ref, routed_ref, len_ref,
+    upd_out, dx_out, fq_out, fo_out, fu_out, fd_out, vec_out,
+    wq, wo, wu, wd, gv, stq, stu, stv, rcv,
+    xs, xr, ds, dr, a_s, a_r, d2s, d2r, d1r, m_s, m_r, hid, dh, qkv, att, act, gp, logit, gains,
+    gd, gu, rcd, rcu, ryd, ryu, rzd, rzu,
+    fqk, fv, fo, fu, fd, sqk, sv, suu, rqk, rv, ruu, vs, vr, v_all,
+    loc, out_sem, wz, vz, wy, vy, wc, vc, sx, rx, gc, hc, gy, hy, gz, hz, free,
+):
+    s, z, y, c = place()
+    near, far = z + 1 - 2 * lax.rem(z, 2), LINE - 1 - z
+    xdev, ydev, cdev = device(1 - s, z, y, c), device(s, z, 1 - y, c), device(s, z, y, 1 - c)
+    ndev, fdev = device(s, near, y, c), device(s, far, y, c)
+    model, half_q, half_u = xr.shape[2], att.shape[2], act.shape[2]
+    ranks, half = xr.shape[1], xr.shape[2] // 2
+    rows = xr.shape[0] * ranks
+    part, half_d = stq.shape[0], wd.shape[3] // 2
+    local, sent, outs = [], [], []
+
+    def fetch(src, dst):
+        copy = pltpu.make_async_copy(src, dst, loc.at[len(local)])
+        copy.start()
+        local.append(copy)
+        return copy
+
+    def send(src, dst, send_sem, recv_sem, target):
+        copy = remote(src, dst, send_sem, recv_sem, target)
+        copy.start()
+        sent.append(copy)
+        return copy
+
+    def gone(copy):
+        copy.wait_send()
+        sent[:] = [other for other in sent if other is not copy]
+
+    def arrive(ref, send_sem, recv_sem, target):
+        remote(ref, ref, send_sem, recv_sem, target).wait_recv()
+
+    def put(src, dst):
+        copy = pltpu.make_async_copy(src, dst, out_sem.at[len(outs)])
+        copy.start()
+        outs.append(copy)
+
+    stage, own_q = [], []
+    for j in range(3):
+        base, dst = 2 * j * half_q, pl.ds(j * half_q, half_q)
+        stage.append(fetch(wq_hbm.at[:, pl.ds(base + (1 - s) * half_q, half_q)], stq.at[:, dst]))
+        own_q.append(fetch(wq_hbm.at[:, pl.ds(base + s * half_q, half_q)], wq.at[s, z, y, c, :, dst]))
+    get_tok = [fetch(tok_hbm.at[i], gd.at[pl.ds(2 * i, 2)]) for i in range(2)]
+    own_o = fetch(wo_hbm, wo.at[z, y, c])
+    stage_u = fetch(wu_hbm.at[:, pl.ds((1 - s) * half_u, half_u)], stu)
+    own_u = fetch(wu_hbm.at[:, pl.ds(s * half_u, half_u)], wu.at[s, z, y, c])
+    own_d = fetch(wd_hbm, wd.at[z, y, c])
+
+    def down_half(i):
+        return pl.ds(half_d * i, half_d)
+
+    blocks = [
+        lambda zz, yy, cc: wq.at[s, zz, yy, cc],
+        lambda zz, yy, cc: wq.at[1 - s, zz, yy, cc],
+        lambda zz, yy, cc: gv.at[zz, yy, cc],
+        lambda zz, yy, cc: wo.at[zz, yy, cc],
+        lambda zz, yy, cc: wu.at[s, zz, yy, cc],
+        lambda zz, yy, cc: wu.at[1 - s, zz, yy, cc],
+        lambda zz, yy, cc: wd.at[zz, yy, cc, down_half(0)],
+        lambda zz, yy, cc: wd.at[zz, yy, cc, down_half(1)],
+    ]
+    lines = [
+        lambda yy, cc: wq.at[s, :, yy, cc],
+        lambda yy, cc: wq.at[1 - s, :, yy, cc],
+        lambda yy, cc: gv.at[:, yy, cc],
+        lambda yy, cc: wo.at[:, yy, cc],
+        lambda yy, cc: wu.at[s, :, yy, cc],
+        lambda yy, cc: wu.at[1 - s, :, yy, cc],
+        lambda yy, cc: wd.at[:, yy, cc, down_half(0)],
+        lambda yy, cc: wd.at[:, yy, cc, down_half(1)],
+    ]
+    Q_OWN, Q_SWAP, VEC, OUT, U_OWN, U_SWAP, D_0, D_1 = range(8)
+
+    def spread(p):
+        own = blocks[p](z, y, c)
+        send(own, own, wz.at[p, 0], vz.at[p, 0], fdev)
+        send(own, own, wz.at[p, 1], vz.at[p, 1], ndev)
+        send(own, own, wy.at[p, 0], vy.at[p, 0], ydev)
+
+    def after_far(p):
+        ref = blocks[p](far, y, c)
+        arrive(ref, wz.at[p, 0], vz.at[p, 0], fdev)
+        send(ref, ref, wz.at[p, 2], vz.at[p, 2], ndev)
+        send(ref, ref, wy.at[p, 1], vy.at[p, 1], ydev)
+
+    def after_near(p):
+        for i, zz in ((1, near), (2, LINE - 1 - near)):
+            ref = blocks[p](zz, y, c)
+            arrive(ref, wz.at[p, i], vz.at[p, i], ndev)
+            send(ref, ref, wy.at[p, i + 1], vy.at[p, i + 1], ydev)
+        line = lines[p](y, c)
+        send(line, line, wc.at[p, 0], vc.at[p, 0], cdev)
+
+    def after_y(p):
+        for i, zz in enumerate((z, far, near, LINE - 1 - near)):
+            arrive(blocks[p](zz, 1 - y, c), wy.at[p, i], vy.at[p, i], ydev)
+        line = lines[p](1 - y, c)
+        send(line, line, wc.at[p, 1], vc.at[p, 1], cdev)
+
+    def after_c(p):
+        for i, yy in enumerate((y, 1 - y)):
+            arrive(lines[p](yy, 1 - c), wc.at[p, i], vc.at[p, i], cdev)
+
+    parts = [
+        lambda cc: gd.at[:, :, cc, down_half(0)],
+        lambda cc: gd.at[:, :, cc, down_half(1)],
+        lambda cc: gu.at[0, :, :, cc],
+        lambda cc: gu.at[1, :, :, cc],
+    ]
+    parts += parts[:2]
+    land_c = [rcd.at[0], rcd.at[1], rcu.at[0], rcu.at[1], rcd.at[0], rcd.at[1]]
+    land_y = [ryd.at[0], ryd.at[1], ryu.at[0], ryu.at[1], ryd.at[0], ryd.at[1]]
+    land_z = [rzd.at[0], rzd.at[1], rzu.at[0], rzu.at[1], rzd.at[0], rzd.at[1]]
+
+    def c_start(k):
+        return send(parts[k](1 - c), land_c[k], gc.at[k], hc.at[k], cdev)
+
+    def c_end(k):
+        ref, own = land_c[k], parts[k](c)
+        arrive(ref, gc.at[k], hc.at[k], cdev)
+
+        def add(i, carry):
+            ref[i] = (ref[i].astype(f32) + own[i].astype(f32)).astype(bf16)
+            return carry
+
+        lax.fori_loop(0, LINE, add, 0)
+        return send(ref.at[:, 1 - y], land_y[k], gy.at[k], hy.at[k], ydev)
+
+    def y_end(k):
+        ref, own = land_y[k], land_c[k]
+        arrive(ref, gy.at[k], hy.at[k], ydev)
+
+        def add(i, carry):
+            ref[i] = (ref[i].astype(f32) + own[i, y].astype(f32)).astype(bf16)
+            return carry
+
+        lax.fori_loop(0, LINE, add, 0)
+        return [
+            send(ref.at[LINE - 1 - near], land_z[k].at[1], gz.at[k, 1], hz.at[k, 1], ndev),
+            send(ref.at[near], land_z[k].at[0], gz.at[k, 0], hz.at[k, 0], ndev),
+        ]
+
+    def z_mid(k):
+        ref = land_z[k].at[1]
+        arrive(ref, gz.at[k, 1], hz.at[k, 1], ndev)
+        ref[...] = (ref[...].astype(f32) + land_y[k][far].astype(f32)).astype(bf16)
+        return send(ref, land_z[k].at[2], gz.at[k, 2], hz.at[k, 2], fdev)
+
+    def z_end(k):
+        arrive(land_z[k].at[0], gz.at[k, 0], hz.at[k, 0], ndev)
+        arrive(land_z[k].at[2], gz.at[k, 2], hz.at[k, 2], fdev)
+        return land_y[k][z].astype(f32) + land_z[k][0].astype(f32) + land_z[k][2].astype(f32)
+
+    lane = lax.broadcasted_iota(jnp.int32, (part, model), 1)
+    fits = (lax.rem(lane, part) == lax.broadcasted_iota(jnp.int32, (part, model), 0)) & (
+        lane // part == s * 4 * LINE + z * 4 + y * 2 + c
+    )
+    stv[...] = dot_nn(small_ref[...], jnp.where(fits, 1.0, 0.0).astype(bf16)).astype(bf16)
+
+    def chooser(i):
+        count = len_ref[i] // 8
+        rank = lax.broadcasted_iota(jnp.int32, (1, ranks), 1)
+        row = jnp.where(rank < count, routed_ref[i : i + 1], -1).astype(f32)
+        eye = lax.broadcasted_iota(jnp.int32, (ranks, ranks), 0) == lax.broadcasted_iota(
+            jnp.int32, (ranks, ranks), 1
+        )
+        column = jnp.sum(jnp.where(eye, row, 0.0), axis=1, keepdims=True).astype(jnp.int32)
+        count_here = tok_hbm.shape[1] * 512
+        position = lax.broadcasted_iota(jnp.int32, (ranks, count_here), 1) + s * count_here
+        return jnp.where(position == column, 1.0, 0.0).astype(bf16)
+
+    def pick(i, dst):
+        dst[i] = dot_nn(chooser(i), gd[2 * i : 2 * i + 2].reshape(tok_hbm.shape[1] * 512, model)).astype(bf16)
+
+    def live_column(i):
+        rank = lax.broadcasted_iota(jnp.int32, (ranks, 1), 0)
+        return jnp.where(rank < len_ref[i] // 8, 1.0, 0.0).astype(f32)
+
+    def allowed(i):
+        query = lax.broadcasted_iota(jnp.int32, (ranks, ranks), 0)
+        key = lax.broadcasted_iota(jnp.int32, (ranks, ranks), 1)
+        return (key <= query) & (key < len_ref[i] // 8)
+
+    greet([xdev, ydev, cdev, ndev, fdev])
+    swap_v = send(stv, rcv, sx.at[0], rx.at[0], xdev)
+    for copy in stage:
+        copy.wait()
+    send(stq, wq.at[s, z, y, c], sx.at[1], rx.at[1], xdev)
+    for copy in own_q:
+        copy.wait()
+    spread(Q_OWN)
+    x_swap = []
+    get_tok[0].wait()
+    pick(0, xs)
+    x_swap.append(send(xs.at[0], xr.at[0], sx.at[3], rx.at[3], xdev))
+    get_cot = [fetch(cot_hbm.at[0], gd.at[pl.ds(0, 2)])]
+    stage_u.wait()
+    send(stu, wu.at[s, z, y, c], sx.at[2], rx.at[2], xdev)
+    get_tok[1].wait()
+    pick(1, xs)
+    x_swap.append(send(xs.at[1], xr.at[1], sx.at[4], rx.at[4], xdev))
+    get_cot.append(fetch(cot_hbm.at[1], gd.at[pl.ds(2, 2)]))
+    swap_v.wait_recv()
+    gv[z, y, c] = stv[...] + rcv[...]
+    spread(VEC)
+    arrive(wq.at[1 - s, z, y, c], sx.at[1], rx.at[1], xdev)
+    spread(Q_SWAP)
+    own_o.wait()
+    spread(OUT)
+    own_u.wait()
+    spread(U_OWN)
+    own_d.wait()
+    get_cot[0].wait()
+    pick(0, ds)
+    d_swap = [send(ds.at[0], dr.at[0], sx.at[7], rx.at[7], xdev)]
+    after_far(Q_OWN)
+    get_cot[1].wait()
+    pick(1, ds)
+    after_near(Q_OWN)
+    after_far(VEC)
+    after_far(Q_SWAP)
+    after_near(VEC)
+    after_near(Q_SWAP)
+    arrive(wu.at[1 - s, z, y, c], sx.at[2], rx.at[2], xdev)
+    spread(U_SWAP)
+    spread(D_0)
+    spread(D_1)
+    after_far(OUT)
+    after_y(Q_OWN)
+    after_near(OUT)
+    after_y(VEC)
+    after_y(Q_SWAP)
+    after_far(U_OWN)
+    after_c(Q_OWN)
+    after_c(VEC)
+    after_c(Q_SWAP)
+
+    gains[...] = jnp.sum(gv[...].astype(f32).reshape(4 * LINE, 16, model), axis=0)
+    gain_one, gain_two, router = gains[0:1], gains[1:2], gains[2:3]
+
+    def enter(i):
+        x_swap[i].wait()
+        row = xr[i].astype(f32) + xs[i].astype(f32)
+        xr[i] = row.astype(bf16)
+        xs[i] = (row * inverse_rms(row) * gain_one).astype(bf16)
+        for j in range(3):
+            cols = pl.ds(j * half_q, half_q)
+            qkv[i, :, cols] = dot_nn(xs[i], wq[:, :, :, :, :, cols].reshape(model, half_q)).astype(bf16)
+
+    def attend(i):
+        ok = allowed(i)
+
+        def pair(j, carry):
+            q2 = qkv[i, :, pl.ds(j * 128, 128)].astype(f32)
+            k2 = qkv[i, :, pl.ds(half_q + j * 128, 128)]
+            v2 = qkv[i, :, pl.ds(2 * half_q + j * 128, 128)]
+            mixed = jnp.zeros(q2.shape, f32)
+            for parity in range(2):
+                mask = head_mask(parity)
+                score = dot_nt((q2 * mask).astype(bf16), k2) * (HEAD_DIM**-0.5)
+                score = jnp.where(ok, score, -1000000000.0)
+                weight = jnp.exp(score - jnp.max(score, axis=-1, keepdims=True))
+                total = jnp.sum(weight, axis=-1, keepdims=True)
+                mixed += dot_nn(weight.astype(bf16), v2) / total * mask
+            att[i, :, pl.ds(j * 128, 128)] = mixed.astype(bf16)
+            return carry
+
+        lax.fori_loop(0, half_q // 128, pair, 0)
+
+    def leave(i):
+        for j in range(2):
+            cols = pl.ds(j * half, half)
+            a_s[i, :, cols] = dot_nn(att[i], wo[:, :, :, :, cols].reshape(half_q, half)).astype(bf16)
+        return send(a_s.at[i], a_r.at[i], sx.at[5 + i], rx.at[5 + i], xdev)
+
+    enter(0)
+    after_y(OUT)
+    after_near(U_OWN)
+    attend(0)
+    after_c(OUT)
+    a_swap = [leave(0)]
+    after_far(U_SWAP)
+    enter(1)
+    after_y(U_OWN)
+    after_near(U_SWAP)
+    attend(1)
+    after_far(D_0)
+    a_swap.append(leave(1))
+    d_swap.append(send(ds.at[1], dr.at[1], sx.at[8], rx.at[8], xdev))
+    after_y(U_SWAP)
+    after_near(D_0)
+    after_c(U_OWN)
+    after_c(U_SWAP)
+
+    def mlp_up(i):
+        a_swap[i].wait()
+        row = xr[i].astype(f32) + (a_s[i].astype(f32) + a_r[i].astype(f32))
+        hid[i] = row
+        a_s[i] = (row * inverse_rms(row) * gain_two).astype(bf16)
+
+        def tile(t, carry):
+            cols = pl.ds(t * 512, 512)
+            up = dot_nn(a_s[i], wu[:, :, :, :, :, cols].reshape(model, 512))
+            curve = jnp.tanh(GELU_C * (up + GELU_K * up * up * up))
+            act[i, :, cols] = (0.5 * up * (1.0 + curve)).astype(bf16)
+            slope = 0.5 * (1.0 + curve) + 0.5 * up * (1.0 - curve * curve) * (
+                GELU_C * (1.0 + 3.0 * GELU_K * up * up)
+            )
+            gp[i, :, cols] = slope.astype(bf16)
+            return carry
+
+        lax.fori_loop(0, half_u // 512, tile, 0)
+
+    def gate_of(i):
+        return jax.nn.sigmoid(jnp.sum(xr[i].astype(f32) * router, axis=-1, keepdims=True))
+
+    def cotangent_rows(i):
+        d_swap[i].wait()
+        row = dr[i].astype(f32) + ds[i].astype(f32)
+        dr[i] = row.astype(bf16)
+        ds[i] = (gate_of(i) * row).astype(bf16)
+
+    def mlp_back(i):
+        def tile(t, carry):
+            cols = pl.ds(t * 512, 512)
+            back = dot_nt(ds[i], wd[t].reshape(512, model))
+            gp[i, :, cols] = (back * gp[i, :, cols].astype(f32)).astype(bf16)
+            return carry
+
+        lax.fori_loop(0, half_u // 512, tile, 0)
+        for j in range(2):
+            cols = pl.ds(j * half, half)
+            d2s[i, :, cols] = dot_nt(gp[i], wu[j].reshape(half, half_u)).astype(bf16)
+        return send(d2s.at[i], d2r.at[i], sx.at[9 + i], rx.at[9 + i], xdev)
+
+    def mlp_out(i):
+        for j in range(2):
+            cols = pl.ds(j * half, half)
+            m_s[i, :, cols] = dot_nn(act[i], wd[:, :, :, :, cols].reshape(half_u, half)).astype(bf16)
+        return send(m_s.at[i], m_r.at[i], sx.at[11 + i], rx.at[11 + i], xdev)
+
+    mlp_up(0)
+    after_far(D_1)
+    after_y(D_0)
+    after_near(D_1)
+    cotangent_rows(0)
+    mlp_up(1)
+    after_y(D_1)
+    after_c(D_0)
+    after_c(D_1)
+    d2_swap = [mlp_back(0)]
+    cotangent_rows(1)
+
+    def down_tile(t, carry):
+        grad = dot_tn(act[:, :, pl.ds(t * 512, 512)].reshape(rows, 512), ds[...].reshape(rows, model))
+        gd[t] = grad.astype(bf16).reshape(gd.shape[1:])
+        return carry
+
+    lax.fori_loop(0, half_u // 512, down_tile, 0)
+    c_down = [c_start(0), c_start(1)]
+    d2_swap.append(mlp_back(1))
+    y_down = [c_end(0)]
+
+    def up_tile(t, carry):
+        cols = pl.ds(t * 512, 512)
+        grad = dot_tn(a_s[...].reshape(rows, model), gp[:, :, cols].reshape(rows, 512))
+        gu[:, :, :, :, :, cols] = grad.astype(bf16).reshape(gu.shape[:5] + (512,))
+        return carry
+
+    lax.fori_loop(0, half_u // 512, up_tile, 0)
+    c_start(2)
+    c_start(3)
+    y_down.append(c_end(1))
+    m_swap = [mlp_out(0), mlp_out(1)]
+    c_end(2)
+    c_end(3)
+
+    def hidden_back(i):
+        d2_swap[i].wait()
+        back = d2s[i].astype(f32) + d2r[i].astype(f32)
+        row = hid[i]
+        r2 = inverse_rms(row)
+        scaled = back * gain_two
+        step = r2 * scaled - row * (r2 * r2 * r2 * jnp.mean(scaled * row, axis=-1, keepdims=True))
+        dh[i] = step
+        gp[i, :, 0:model] = (gate_of(i) * dr[i].astype(f32) + step).astype(bf16)
+        gp[i, :, model : model + half_q] = dot_nt(gp[i, :, 0:model], wo[...].reshape(half_q, model)).astype(bf16)
+        return jnp.sum(d2s[i].astype(f32) * row * r2, axis=0, keepdims=True)
+
+    def attend_back(i):
+        ok = allowed(i)
+        scale = HEAD_DIM**-0.5
+
+        def pair(j, carry):
+            q2 = qkv[i, :, pl.ds(j * 128, 128)]
+            k2 = qkv[i, :, pl.ds(half_q + j * 128, 128)]
+            v2 = qkv[i, :, pl.ds(2 * half_q + j * 128, 128)]
+            g2 = gp[i, :, pl.ds(model + j * 128, 128)].astype(f32)
+            q2f = q2.astype(f32)
+            dq2 = jnp.zeros(q2.shape, f32)
+            dk2 = jnp.zeros(q2.shape, f32)
+            dv2 = jnp.zeros(q2.shape, f32)
+            for parity in range(2):
+                mask = head_mask(parity)
+                score = dot_nt((q2f * mask).astype(bf16), k2) * scale
+                score = jnp.where(ok, score, -1000000000.0)
+                weight = jnp.exp(score - jnp.max(score, axis=-1, keepdims=True))
+                over = 1.0 / jnp.sum(weight, axis=-1, keepdims=True)
+                gh = g2 * mask
+                dp = dot_nt(gh.astype(bf16), v2)
+                prob = weight * over
+                delta = jnp.sum(prob * dp, axis=-1, keepdims=True)
+                dscore = (prob * (dp - delta)).astype(bf16)
+                dq2 += dot_nn(dscore, k2) * mask
+                dk2 += dot_tn(dscore, q2) * mask
+                dv2 += dot_tn(weight.astype(bf16), (gh * over).astype(bf16))
+            act[i, :, pl.ds(j * 128, 128)] = (dq2 * scale).astype(bf16)
+            act[i, :, pl.ds(half_q + j * 128, 128)] = (dk2 * scale).astype(bf16)
+            act[i, :, pl.ds(2 * half_q + j * 128, 128)] = dv2.astype(bf16)
+            return carry
+
+        lax.fori_loop(0, half_q // 128, pair, 0)
+
+    def inner_back(i):
+        r1 = inverse_rms(xr[i].astype(f32))
+        sums = []
+        for j in range(2):
+            cols = pl.ds(j * half, half)
+            step = dot_nt(act[i, :, 0 : 3 * half_q], wq[j].reshape(half, 3 * half_q))
+            d2s[i, :, cols] = step.astype(bf16)
+            sums.append(jnp.sum(step * xr[i, :, cols].astype(f32) * r1, axis=0, keepdims=True))
+        return send(d2s.at[i], d1r.at[i], sx.at[13 + i], rx.at[13 + i], xdev), sums
+
+    z_down = []
+    grad_gm = hidden_back(0)
+    attend_back(0)
+    z_down += y_end(0)
+    swap_0, sums_0 = inner_back(0)
+    grad_gm += hidden_back(1)
+    z_down += y_end(1)
+    z_down.append(z_mid(0))
+    attend_back(1)
+    z_down.append(z_mid(1))
+    fd[0:half_d] = z_end(0)
+    y_end(2)
+    fd[half_d:] = z_end(1)
+    put(fd, fd_out)
+    for copy in c_down + y_down + z_down:
+        gone(copy)
+    for target in (ydev, cdev, ndev, fdev):
+        pl.semaphore_signal(free, inc=1, device_id=target, device_id_type=MESH)
+
+    def out_tile(t):
+        cols = pl.ds(t * half, half)
+        grad = dot_tn(att[...].reshape(rows, half_q), gp[:, :, cols].reshape(rows, half))
+        gd[:, :, :, 3 * part :, cols] = grad.astype(bf16).reshape(wo.shape[:4] + (half,))
+
+    def qkv_tile(t):
+        grad = dot_tn(xs[...].reshape(rows, model), act[:, :, t * half_q : (t + 1) * half_q].reshape(rows, half_q))
+        grad = grad.astype(bf16).reshape(wq.shape[:5] + (half_q,))
+        if t < 2:
+            gd[:, :, :, 0:part, t * half_q : (t + 1) * half_q] = grad[0]
+            gd[:, :, :, part : 2 * part, t * half_q : (t + 1) * half_q] = grad[1]
+        else:
+            gd[:, :, :, 2 * part : 3 * part, 0:half_q] = grad[0]
+            gd[:, :, :, 2 * part : 3 * part, half_q:] = grad[1]
+
+    qkv_tile(0)
+    qkv_tile(1)
+    pl.semaphore_wait(free, 4)
+    c_start(4)
+    out_tile(0)
+    out_tile(1)
+    qkv_tile(2)
+    c_start(5)
+    c_end(4)
+    swap_1, sums_1 = inner_back(1)
+    d1_swap = [swap_0, swap_1]
+    for j in range(2):
+        vs[0:1, j * half : (j + 1) * half] = sums_0[j] + sums_1[j]
+    vs[1:2] = grad_gm
+    c_end(5)
+    z_mid(2)
+    y_end(3)
+
+    grad_router = jnp.zeros((1, model), f32)
+    for i in range(2):
+        m_swap[i].wait()
+        row = xr[i].astype(f32)
+        gate = gate_of(i)
+        branch = (hid[i] - row) + (m_s[i].astype(f32) + m_r[i].astype(f32))
+        m_s[i] = (gate * branch * live_column(i)).astype(bf16)
+        slope = jnp.sum(dr[i].astype(f32) * branch, axis=-1, keepdims=True) * gate * (1.0 - gate)
+        logit[i] = slope
+        grad_router += jnp.sum(row * slope, axis=0, keepdims=True)
+    put(m_s, upd_out)
+    vs[2:3] = 0.5 * grad_router
+    vs[3:8] = jnp.zeros((5, model), f32)
+    send(vs, vr.at[0], gc.at[6], hc.at[6], cdev)
+    fu[0] = z_end(2)
+    z_mid(3)
+    arrive(vr.at[0], gc.at[6], hc.at[6], cdev)
+    v_all[0] = vs[...] + vr[0]
+    send(v_all.at[0], vr.at[1], gy.at[6], hy.at[6], ydev)
+    y_end(4)
+    fu[1] = z_end(3)
+    suu[...] = fu[1 - s].astype(bf16)
+    send(suu, ruu, sx.at[15], rx.at[15], xdev)
+    put(fu.at[s], fu_out.at[:, pl.ds(s * half_u, half_u)])
+    arrive(vr.at[1], gy.at[6], hy.at[6], ydev)
+    v_all[1] = v_all[0] + vr[1]
+    send(v_all.at[1], vr.at[2], gz.at[6, 0], hz.at[6, 0], ndev)
+    z_mid(4)
+
+    for i in range(2):
+        d1_swap[i].wait()
+        row = xr[i].astype(f32)
+        r1 = inverse_rms(row)
+        scaled = (d2s[i].astype(f32) + d1r[i].astype(f32)) * gain_one
+        step = r1 * scaled - row * (r1 * r1 * r1 * jnp.mean(scaled * row, axis=-1, keepdims=True))
+        d2s[i] = (dh[i] + step + logit[i] * router).astype(bf16)
+    put(d2s, dx_out)
+
+    y_end(5)
+    arrive(vr.at[2], gz.at[6, 0], hz.at[6, 0], ndev)
+    v_all[2] = v_all[1] + vr[2]
+    send(v_all.at[2], vr.at[3], gz.at[6, 1], hz.at[6, 1], fdev)
+    fqk[...] = z_end(4).reshape(fqk.shape)
+    sqk[...] = fqk[1 - s].astype(bf16)
+    send(sqk, rqk, sx.at[16], rx.at[16], xdev)
+    z_mid(5)
+    arrive(ruu, sx.at[15], rx.at[15], xdev)
+    fu[1 - s] = ruu[...].astype(f32)
+    put(fu.at[1 - s], fu_out.at[:, pl.ds((1 - s) * half_u, half_u)])
+    for j in range(2):
+        put(fqk.at[s, :, pl.ds(j * half_q, half_q)], fq_out.at[:, pl.ds(2 * j * half_q + s * half_q, half_q)])
+    arrive(vr.at[3], gz.at[6, 1], hz.at[6, 1], fdev)
+    v_all[3] = v_all[2] + vr[3]
+    send(v_all.at[3], vr.at[4], sx.at[18], rx.at[18], xdev)
+    last = z_end(5)
+    fv[...] = last[0:part]
+    sv[...] = fv[:, pl.ds((1 - s) * half_q, half_q)].astype(bf16)
+    send(sv, rv, sx.at[17], rx.at[17], xdev)
+    fo[...] = last[part:]
+    put(fo, fo_out)
+    put(fv.at[:, pl.ds(s * half_q, half_q)], fq_out.at[:, pl.ds(4 * half_q + s * half_q, half_q)])
+    arrive(rqk, sx.at[16], rx.at[16], xdev)
+    fqk[1 - s] = rqk[...].astype(f32)
+    for j in range(2):
+        put(
+            fqk.at[1 - s, :, pl.ds(j * half_q, half_q)],
+            fq_out.at[:, pl.ds(2 * j * half_q + (1 - s) * half_q, half_q)],
+        )
+    arrive(vr.at[4], sx.at[18], rx.at[18], xdev)
+    v_all[4] = v_all[3] + vr[4]
+    put(v_all.at[4], vec_out)
+    arrive(rv, sx.at[17], rx.at[17], xdev)
+    fv[:, pl.ds((1 - s) * half_q, half_q)] = rv[...].astype(f32)
+    put(
+        fv.at[:, pl.ds((1 - s) * half_q, half_q)],
+        fq_out.at[:, pl.ds(4 * half_q + (1 - s) * half_q, half_q)],
+    )
+    waited = x_swap + a_swap + d_swap + d2_swap + m_swap + d1_swap
+    for copy in list(sent):
+        if not any(copy is other for other in waited):
+            copy.wait_send()
+    for copy in outs:
+        copy.wait()
+
+
+def rows_kernel(
+    len_ref, routed_ref, tok_ref, cot_ref, upd_ref, dx_ref, fq_ref, fo_ref, fu_ref, fd_ref, vec_ref,
+    out_ref, grad_ref, fq_out, fo_out, fu_out, fd_out, one_out, two_out, three_out,
+):
+    slot, step = pl.program_id(0), pl.program_id(1)
+    s = lax.axis_index("seq")
+    tall, model = tok_ref.shape[1:]
+    ranks = upd_ref.shape[1]
+    rank = lax.broadcasted_iota(jnp.int32, (1, ranks), 1)
+    routed = jnp.where(rank < len_ref[slot] // 8, routed_ref[pl.ds(slot, 1)], -1)
+    first = (s * pl.num_programs(1) + step) * tall
+    position = lax.broadcasted_iota(jnp.int32, (tall, ranks), 0) + first
+    chooser = jnp.where(position == routed, 1.0, 0.0).astype(bf16)
+    out_ref[0] = (tok_ref[0].astype(f32) + dot_nn(chooser, upd_ref[0])).astype(bf16)
+    grad_ref[0] = (cot_ref[0].astype(f32) + dot_nn(chooser, dx_ref[0])).astype(bf16)
+
+    @pl.when((slot == 0) & (step == 0))
+    def _():
+        fq_out[...] = fq_ref[...]
+        fo_out[...] = fo_ref[...]
+        fu_out[...] = fu_ref[...]
+        fd_out[...] = fd_ref[...]
+        part = one_out.shape[1]
+        flat = s * lax.axis_size("batch") + lax.axis_index("batch")
+        lane = lax.broadcasted_iota(jnp.int32, (part, model), 1)
+        here = (lane // part == flat) & (
+            lax.rem(lane, part) == lax.broadcasted_iota(jnp.int32, (part, model), 0)
+        )
+        eye = lax.broadcasted_iota(jnp.int32, (part, part), 0) == lax.broadcasted_iota(
+            jnp.int32, (part, part), 1
+        )
+        for j, ref in enumerate((one_out, two_out, three_out)):
+            column = jnp.sum(jnp.where(here, vec_ref[j : j + 1], 0.0), axis=1, keepdims=True)
+            ref[...] = jnp.sum(jnp.where(eye, column, 0.0), axis=0, keepdims=True)
+
+
+def split_device(
+    tokens, cotangent, lengths, routed, w_qkv, w_out, w_up, w_down, gain_attn, gain_mlp, router
+):
+    slots, local_len, model = tokens.shape
+    ranks = routed.shape[1]
+    half_q, half_u = w_qkv.shape[1] // 6, w_up.shape[1] // 2
+    part, down = w_qkv.shape[0], w_down.shape[0]
+    small = jnp.concatenate(
+        [gain_attn[None], gain_mlp[None], router[None], jnp.zeros((13, part), bf16)], axis=0
+    )
+    hbm = pl.BlockSpec(memory_space=pl.ANY)
+    vmem = pl.BlockSpec(memory_space=pltpu.VMEM)
+    smem = pl.BlockSpec(memory_space=pltpu.SMEM)
+    sds, space, dma = jax.ShapeDtypeStruct, pltpu.VMEM, pltpu.SemaphoreType.DMA
+    rows = (slots, ranks, model)
+    grid = (LINE, 2, 2)
+    wq_shape, wo_shape = (2,) + grid + (part, 3 * half_q), grid + (part, model)
+    wu_shape, wd_shape = (2,) + grid + (part, half_u), grid + (down, model)
+    blocked = (slots, local_len // 512, 2, 2, 128, model)
+    row_bf16 = space(rows, bf16)
+
+    def land(tall, wide):
+        return [
+            space((2, LINE, 2, tall, wide), bf16),
+            space((2, LINE, tall, wide), bf16),
+            space((2, 3, tall, wide), bf16),
+        ]
+
+    on_d, on_u = land(down // 2, model), land(part, half_u)
+    grad_shapes = (
+        sds((part, 6 * half_q), f32), sds((part, model), f32), sds((part, 2 * half_u), f32), sds((down, model), f32),
+    )
+    upd, dxr, *sums, vec = pl.pallas_call(
+        block_kernel,
+        out_shape=(sds(rows, bf16), sds(rows, bf16)) + grad_shapes + (sds((8, model), f32),),
+        in_specs=[hbm] * 6 + [vmem] * 2 + [smem],
+        out_specs=[hbm] * 7,
+        scratch_shapes=[
+            space(wq_shape, bf16), space(wo_shape, bf16), space(wu_shape, bf16), space(wd_shape, bf16),
+            space(grid + (16, model), bf16),
+            space((part, 3 * half_q), bf16), space((part, half_u), bf16), space((16, model), bf16), space((16, model), bf16),
+            *[row_bf16] * 11, space(rows, f32), space(rows, f32),
+            space((slots, ranks, 3 * half_q), bf16), space((slots, ranks, half_q), bf16),
+            space((slots, ranks, half_u), bf16), space((slots, ranks, half_u), bf16),
+            space((slots, ranks, 1), f32), space((16, model), f32),
+            space(wd_shape, bf16), space(wu_shape, bf16),
+            on_d[0], on_u[0], on_d[1], on_u[1], on_d[2], on_u[2],
+            space((2, part, model), f32), space((part, model), f32), space((part, model), f32),
+            space((2, part, half_u), f32), space((down, model), f32),
+            space((part, model), bf16), space((part, half_q), bf16), space((part, half_u), bf16),
+            space((part, model), bf16), space((part, half_q), bf16), space((part, half_u), bf16),
+            space((8, model), f32), space((5, 8, model), f32), space((5, 8, model), f32),
+            dma((16,)), dma((16,)), dma((8, 3)), dma((8, 3)), dma((8, 4)), dma((8, 4)), dma((8, 2)), dma((8, 2)),
+            dma((19,)), dma((19,)), dma((7,)), dma((7,)), dma((7,)), dma((7,)), dma((7, 3)), dma((7, 3)),
+            pltpu.SemaphoreType.REGULAR,
+        ],
+        compiler_params=pltpu.CompilerParams(collective_id=1, has_side_effects=True, vmem_limit_bytes=60 << 20),
+        name="block",
+    )(tokens.reshape(blocked), cotangent.reshape(blocked), w_qkv, w_out, w_up, w_down, small, routed, lengths)
+
+    tall = 512
+    big = pl.BlockSpec((1, tall, model), lambda i, j: (i, j, 0))
+    moved = pl.BlockSpec((1, ranks, model), lambda i, j: (i, 0, 0))
+
+    def whole(shape):
+        return pl.BlockSpec(shape, lambda i, j: (0, 0))
+
+    whole_grads = [whole(g.shape) for g in grad_shapes]
+    vectors = (sds((1, part), f32),) * 3
+    output, input_grad, g_qkv, g_out, g_up, g_down, g_one, g_two, g_three = pl.pallas_call(
+        rows_kernel,
+        grid=(slots, local_len // tall),
+        out_shape=(sds(tokens.shape, bf16), sds(tokens.shape, bf16)) + grad_shapes + vectors,
+        in_specs=[smem, whole(routed.shape), big, big, moved, moved] + whole_grads + [whole((8, model))],
+        out_specs=[big, big] + whole_grads + [whole((1, part))] * 3,
+        compiler_params=pltpu.CompilerParams(vmem_limit_bytes=40 << 20),
+        name="rows",
+    )(lengths, routed, tokens, cotangent, upd, dxr, *sums, vec)
+    return (
+        output, input_grad, g_qkv, g_out, g_up, g_down,
+        g_one.reshape(part), g_two.reshape(part), g_three.reshape(part),
+    )
+
+
 def solution(mesh):
     in_specs = (
         P("batch", "seq", None),
@@ -227,6 +976,6 @@
         P(("seq", "batch")),
         P(("seq", "batch")),
     )
-    return jax.shard_map(
-        per_device, mesh=mesh, in_specs=in_specs, out_specs=out_specs, check_vma=False
-    )
+    small_slice = mesh.shape["seq"] == 2 and mesh.shape["batch"] == 4 * LINE
+    body = split_device if small_slice else general_device
+    return jax.shard_map(body, mesh=mesh, in_specs=in_specs, out_specs=out_specs, check_vma=False)

time: 1070 us -> 212 us (0.20)
  waiting for transfers between devices: 782 us -> 0 us
  Pallas kernels: 0 us -> 197 us
  matrix products: 108 us -> 0 us
  blocking collectives: 82 us -> 0 us
  local copies, waits for them, and re-layouts: 58.9 us -> 11.6 us
  between operations: 17.4 us -> 0.87 us
  other arithmetic: 15.1 us -> 1.35 us
    reduce_scatter x6 -> x0, waiting for transfers between devices: 470 us -> none  [the longest x4 470 us: sum_rows(): lax.psum_scatter(part.astype(bf16), ('seq', 'batch'), scatter_dimension=0...]
    all_gather x8 -> x0, waiting for transfers between devices: 260 us -> none  [the longest x1 75.7 us: per_device(): lax.all_gather(w_up, ('seq', 'batch'), axis=0, tiled=True)]
    pallas_call x0 -> x2, Pallas kernels: none -> 197 us  [the longest x1 191 us: split_device(): pl.pallas_call(block_kernel, out_shape=(sds(rows, bf16), sds(rows, bf16))...]
    dot_general x23 -> x0, matrix products: 108 us -> none  [the longest x1 9.48 us: per_device(): jnp.einsum('rd,fd->rf', grad_m, full_down, preferred_element_type=f32)]
    unnamed x2 -> x0, blocking collectives: 82 us -> none
    unnamed x16 -> x0, waiting for transfers between devices: 51.4 us -> none
    reshape x17 -> x0, local copies, waits for them, and re-layouts: 22.5 us -> none  [the longest x2 5.56 us: per_device(): grad_att4 = grad_att.reshape(own_count, slot_count, head_count, HEAD_DIM)]
    convert_element_type x6 -> x0, local copies, waits for them, and re-layouts: 13.2 us -> none  [the longest x2 3.97 us: per_device(): attended = mixture.reshape(row_count, model_width).astype(bf16)]
  transfers between devices with their start and end apart: 15 -> 0, of which waited for: 11 -> 0; matrix products, arithmetic and copies ran while one was open for 11% -> 0% of each run, Pallas kernels for 0% -> 0%
where the time goes in v3:
time: 212 us; the launch traced here: 211 us
  Pallas kernels  197 us (93%)
  local copies, waits for them, and re-layouts  11.6 us (5%)
    pallas_call x1, Pallas kernels, split_device(): pl.pallas_call(block_kernel, out_shape=(sds(rows, bf16), sds(rows, bf16))...  191 us
    unnamed x22, local copies, waits for them, and re-layouts  11.6 us
    pallas_call x1, Pallas kernels, split_device(): pl.pallas_call(rows_kernel, grid=(slots, local_len // tall), out_shape=(s...  5.97 us

profile of v3, /device:TPU:0, one launch (start us, length us, event | category | flops | bytes accessed | tf_op | source)
XLA Modules:
  0.0 211.1 jit_solution(6662489187087510314)
XLA Ops:
  0.7 0.1 pad.3.clone
  0.7 1.4 maximum_maximum_fusion.small_ref
  2.1 0.0 copy-start.9
  2.1 0.0 copy-start.10
  2.1 191.2 %block.1 = (bf16[2,256,1024]{2,1,0:T(8,128)(2,1)}, bf16[2,256,1024]{2,1,0:T(8,128)(2,1)}, f32[32,3072]{1,0:T(8,128)}, f32[32,1024]{1,0:T(8,128)}, f32[32,4096]{1...) custom-call(bf16[2,2,2,2,128,1024]{5,4,3,2,1,0:T(8,128)(2,1)} %bitcast.8, bf16[2,2,2,2,128,1024]{5,4,3,2,1,0:T(8,128)(2,1)} %bitcast.9, ...), custom_call_target="tpu_custom_call" | custom-call | tf_op jit(solution)/shard_map/block/pallas_call | solution.py:902
  193.3 0.0 copy-done.9
  193.3 0.0 copy-done.10
  193.3 0.0 copy-start
  193.3 2.2 %copy-done = bf16[2,1024,1024]{2,1,0:T(8,128)(2,1)S(1)} copy-done((bf16[2,1024,1024]{2,1,0:T(8,128)(2,1)S(1)}, bf16[2,1024,1024]{2,1,0:T(8,128)(2,1)}, u32[]{:S(2)}) %copy-start) | copy-done | bytes 4194328
  195.5 0.0 copy-start.1
  195.5 2.2 %copy-done.1 = bf16[2,1024,1024]{2,1,0:T(8,128)(2,1)S(1)} copy-done((bf16[2,1024,1024]{2,1,0:T(8,128)(2,1)S(1)}, bf16[2,1024,1024]{2,1,0:T(8,128)(2,1)}, u32[]{:S(2)}) %copy-start.1) | copy-done | bytes 4194328
  197.7 0.0 copy-start.2
  197.7 1.2 copy-done.2
  198.9 0.0 copy-start.3
  198.9 1.2 copy-done.3
  200.2 0.0 copy-start.4
  200.2 1.0 copy-done.4
  201.2 0.0 copy-start.5
  201.2 1.0 copy-done.5
  202.2 0.0 copy-start.6
  202.2 1.0 copy-done.6
  203.2 0.0 copy-start.7
  203.2 0.9 copy-done.7
  204.1 0.0 copy-start.8
  204.2 0.8 copy-done.8
  204.9 6.0 %rows.1 = (bf16[2,1024,1024]{2,1,0:T(8,128)(2,1)}, bf16[2,1024,1024]{2,1,0:T(8,128)(2,1)}, f32[32,3072]{1,0:T(8,128)}, f32[32,1024]{1,0:T(8,128)}, f32[32,4096]{...) custom-call(s32[2]{0:T(128)S(1)} %copy-done.10, ...), custom_call_target="tpu_custom_call" | custom-call | tf_op jit(solution)/shard_map/rows/pallas_call | solution.py:939
  (1 shorter events, 0.0 us)
Async XLA Ops:
  2.1 191.2 %copy-start.9 = (s32[2,256]{1,0:T(2,128)S(1)}, s32[2,256]{1,0:T(2,128)}, u32[]{:S(2)}) copy-start(s32[2,256]{1,0:T(2,128)} %routed_ref.3) | copy-start | bytes 6148
  2.1 191.2 %copy-start.10 = (s32[2]{0:T(128)S(1)}, s32[2]{0:T(128)}, u32[]{:S(2)}) copy-start(s32[2]{0:T(128)} %len_ref.3) | copy-start | bytes 28
  193.3 2.2 %copy-start = (bf16[2,1024,1024]{2,1,0:T(8,128)(2,1)S(1)}, bf16[2,1024,1024]{2,1,0:T(8,128)(2,1)}, u32[]{:S(2)}) copy-start(bf16[2,1024,1024]{2,1,0:T(8,128)(2,1)} %tok_ref.1) | copy-start | bytes 12582916
  195.5 2.2 %copy-start.1 = (bf16[2,1024,1024]{2,1,0:T(8,128)(2,1)S(1)}, bf16[2,1024,1024]{2,1,0:T(8,128)(2,1)}, u32[]{:S(2)}) copy-start(bf16[2,1024,1024]{2,1,0:T(8,128)(2,1)} %cot_ref.1) | copy-start | bytes 12582916
  197.7 1.2 copy-start.2
  198.9 1.2 copy-start.3
  200.2 1.0 copy-start.4
  201.2 1.0 copy-start.5
  202.2 1.0 copy-start.6
  203.2 0.9 copy-start.7
  204.1 0.8 copy-start.8

commit v4 on v3

--- a/solution.py
+++ b/solution.py
@@ -260,7 +260,7 @@
     upd_out, dx_out, fq_out, fo_out, fu_out, fd_out, vec_out,
     wq, wo, wu, wd, gv, stq, stu, stv, rcv,
     xs, xr, ds, dr, a_s, a_r, d2s, d2r, d1r, m_s, m_r, hid, dh, qkv, att, act, gp, logit, gains,
-    gd, gu, rcd, rcu, ryd, ryu, rzd, rzu,
+    gd, gu, rcd, rcu, ryd, ryu, rzd, rzu, rzb, ryb,
     fqk, fv, fo, fu, fd, sqk, sv, suu, rqk, rv, ruu, vs, vr, v_all,
     loc, out_sem, wz, vz, wy, vy, wc, vc, sx, rx, gc, hc, gy, hy, gz, hz, free,
 ):
@@ -338,6 +338,9 @@
         own = blocks[p](z, y, c)
         send(own, own, wz.at[p, 0], vz.at[p, 0], fdev)
         send(own, own, wz.at[p, 1], vz.at[p, 1], ndev)
+
+    def spread_y(p):
+        own = blocks[p](z, y, c)
         send(own, own, wy.at[p, 0], vy.at[p, 0], ydev)
 
     def after_far(p):
@@ -364,16 +367,38 @@
         for i, yy in enumerate((y, 1 - y)):
             arrive(lines[p](yy, 1 - c), wc.at[p, i], vc.at[p, i], cdev)
 
+    def both(zz, cc):
+        return wd.at[zz, :, cc, down_half(1)]
+
+    def after_first_y():
+        arrive(blocks[D_1](z, 1 - y, c), wy.at[D_1, 0], vy.at[D_1, 0], ydev)
+        own = both(z, c)
+        send(own, own, wz.at[D_1, 0], vz.at[D_1, 0], fdev)
+        send(own, own, wz.at[D_1, 1], vz.at[D_1, 1], ndev)
+
+    def after_first_far():
+        ref = both(far, c)
+        arrive(ref, wz.at[D_1, 0], vz.at[D_1, 0], fdev)
+        send(ref, ref, wz.at[D_1, 2], vz.at[D_1, 2], ndev)
+
+    def after_first_near():
+        for i, zz in ((1, near), (2, LINE - 1 - near)):
+            arrive(both(zz, c), wz.at[D_1, i], vz.at[D_1, i], ndev)
+        ref = wd.at[:, :, c, down_half(1)]
+        send(ref, ref, wc.at[D_1, 0], vc.at[D_1, 0], cdev)
+
+    def after_first_c():
+        arrive(wd.at[:, :, 1 - c, down_half(1)], wc.at[D_1, 0], vc.at[D_1, 0], cdev)
+
+    spans = [pl.ds(0, 2 * part), pl.ds(2 * part, 2 * part), None, None]
+    spans += [pl.ds(0, 2 * part), pl.ds(2 * part, part), pl.ds(3 * part, part)]
     parts = [
-        lambda cc: gd.at[:, :, cc, down_half(0)],
-        lambda cc: gd.at[:, :, cc, down_half(1)],
-        lambda cc: gu.at[0, :, :, cc],
-        lambda cc: gu.at[1, :, :, cc],
+        (lambda cc, i=i: gu.at[i - 2, :, :, cc]) if q is None else (lambda cc, q=q: gd.at[:, :, cc, q])
+        for i, q in enumerate(spans)
     ]
-    parts += parts[:2]
-    land_c = [rcd.at[0], rcd.at[1], rcu.at[0], rcu.at[1], rcd.at[0], rcd.at[1]]
-    land_y = [ryd.at[0], ryd.at[1], ryu.at[0], ryu.at[1], ryd.at[0], ryd.at[1]]
-    land_z = [rzd.at[0], rzd.at[1], rzu.at[0], rzu.at[1], rzd.at[0], rzd.at[1]]
+    land_c = [rcu.at[i - 2] if q is None else rcd.at[:, :, q] for i, q in enumerate(spans)]
+    land_y = [ryu.at[i - 2] if q is None else ryd.at[:, q] for i, q in enumerate(spans)]
+    land_z = [rzu.at[i - 2] if q is None else rzd.at[:, q] for i, q in enumerate(spans)]
 
     def c_start(k):
         return send(parts[k](1 - c), land_c[k], gc.at[k], hc.at[k], cdev)
@@ -387,7 +412,12 @@
             return carry
 
         lax.fori_loop(0, LINE, add, 0)
-        return send(ref.at[:, 1 - y], land_y[k], gy.at[k], hy.at[k], ydev)
+        if k == 0:
+            return [
+                send(ref.at[LINE - 1 - near], rzb.at[1], gz.at[k, 1], hz.at[k, 1], ndev),
+                send(ref.at[near], rzb.at[0], gz.at[k, 0], hz.at[k, 0], ndev),
+            ]
+        return [send(ref.at[:, 1 - y], land_y[k], gy.at[k], hy.at[k], ydev)]
 
     def y_end(k):
         ref, own = land_y[k], land_c[k]
@@ -413,6 +443,21 @@
         arrive(land_z[k].at[0], gz.at[k, 0], hz.at[k, 0], ndev)
         arrive(land_z[k].at[2], gz.at[k, 2], hz.at[k, 2], fdev)
         return land_y[k][z].astype(f32) + land_z[k][0].astype(f32) + land_z[k][2].astype(f32)
+
+    def first_mid():
+        arrive(rzb.at[1], gz.at[0, 1], hz.at[0, 1], ndev)
+        rzb[1] = (rzb[1].astype(f32) + land_c[0][far].astype(f32)).astype(bf16)
+        return send(rzb.at[1], rzb.at[2], gz.at[0, 2], hz.at[0, 2], fdev)
+
+    def first_end():
+        arrive(rzb.at[0], gz.at[0, 0], hz.at[0, 0], ndev)
+        arrive(rzb.at[2], gz.at[0, 2], hz.at[0, 2], fdev)
+        rzb[0] = (land_c[0][z].astype(f32) + rzb[0].astype(f32) + rzb[2].astype(f32)).astype(bf16)
+        return send(rzb.at[0, 1 - y], ryb, gy.at[0], hy.at[0], ydev)
+
+    def first_sum():
+        arrive(ryb, gy.at[0], hy.at[0], ydev)
+        return rzb[0, y].astype(f32) + ryb[...].astype(f32)
 
     lane = lax.broadcasted_iota(jnp.int32, (part, model), 1)
     fits = (lax.rem(lane, part) == lax.broadcasted_iota(jnp.int32, (part, model), 0)) & (
@@ -452,6 +497,7 @@
     for copy in own_q:
         copy.wait()
     spread(Q_OWN)
+    spread_y(Q_OWN)
     x_swap = []
     get_tok[0].wait()
     pick(0, xs)
@@ -465,37 +511,43 @@
     get_cot.append(fetch(cot_hbm.at[1], gd.at[pl.ds(2, 2)]))
     swap_v.wait_recv()
     gv[z, y, c] = stv[...] + rcv[...]
+    after_far(Q_OWN)
     spread(VEC)
+    spread_y(VEC)
     arrive(wq.at[1 - s, z, y, c], sx.at[1], rx.at[1], xdev)
     spread(Q_SWAP)
-    own_o.wait()
-    spread(OUT)
-    own_u.wait()
-    spread(U_OWN)
+    spread_y(Q_SWAP)
     own_d.wait()
     get_cot[0].wait()
     pick(0, ds)
     d_swap = [send(ds.at[0], dr.at[0], sx.at[7], rx.at[7], xdev)]
-    after_far(Q_OWN)
+    after_near(Q_OWN)
+    after_far(VEC)
+    spread_y(D_1)
     get_cot[1].wait()
     pick(1, ds)
-    after_near(Q_OWN)
-    after_far(VEC)
     after_far(Q_SWAP)
+    own_o.wait()
+    spread(OUT)
     after_near(VEC)
     after_near(Q_SWAP)
+    after_far(OUT)
+    spread_y(OUT)
+    own_u.wait()
+    spread(U_OWN)
+    spread_y(U_OWN)
     arrive(wu.at[1 - s, z, y, c], sx.at[2], rx.at[2], xdev)
     spread(U_SWAP)
-    spread(D_0)
-    spread(D_1)
-    after_far(OUT)
     after_y(Q_OWN)
+    after_y(VEC)
+    after_c(Q_OWN)
+    after_c(VEC)
     after_near(OUT)
-    after_y(VEC)
     after_y(Q_SWAP)
     after_far(U_OWN)
-    after_c(Q_OWN)
-    after_c(VEC)
+    spread(D_0)
+    spread_y(U_SWAP)
+    spread_y(D_0)
     after_c(Q_SWAP)
 
     gains[...] = jnp.sum(gv[...].astype(f32).reshape(4 * LINE, 16, model), axis=0)
@@ -537,23 +589,21 @@
         return send(a_s.at[i], a_r.at[i], sx.at[5 + i], rx.at[5 + i], xdev)
 
     enter(0)
+    attend(0)
     after_y(OUT)
-    after_near(U_OWN)
-    attend(0)
     after_c(OUT)
     a_swap = [leave(0)]
     after_far(U_SWAP)
+    after_first_y()
+    after_near(U_OWN)
     enter(1)
-    after_y(U_OWN)
-    after_near(U_SWAP)
     attend(1)
-    after_far(D_0)
     a_swap.append(leave(1))
     d_swap.append(send(ds.at[1], dr.at[1], sx.at[8], rx.at[8], xdev))
-    after_y(U_SWAP)
-    after_near(D_0)
+    after_far(D_0)
+    after_near(U_SWAP)
+    after_y(U_OWN)
     after_c(U_OWN)
-    after_c(U_SWAP)
 
     def mlp_up(i):
         a_swap[i].wait()
@@ -600,17 +650,21 @@
         for j in range(2):
             cols = pl.ds(j * half, half)
             m_s[i, :, cols] = dot_nn(act[i], wd[:, :, :, :, cols].reshape(half_u, half)).astype(bf16)
+
+    def mlp_send(i):
         return send(m_s.at[i], m_r.at[i], sx.at[11 + i], rx.at[11 + i], xdev)
 
+    after_y(U_SWAP)
+    after_first_far()
+    after_c(U_SWAP)
     mlp_up(0)
-    after_far(D_1)
+    after_near(D_0)
+    mlp_up(1)
     after_y(D_0)
-    after_near(D_1)
+    after_c(D_0)
+    after_first_near()
+    after_first_c()
     cotangent_rows(0)
-    mlp_up(1)
-    after_y(D_1)
-    after_c(D_0)
-    after_c(D_1)
     d2_swap = [mlp_back(0)]
     cotangent_rows(1)
 
@@ -622,7 +676,10 @@
     lax.fori_loop(0, half_u // 512, down_tile, 0)
     c_down = [c_start(0), c_start(1)]
     d2_swap.append(mlp_back(1))
-    y_down = [c_end(0)]
+    z_first = c_end(0)
+    y_down = c_end(1)
+    mlp_out(0)
+    m_swap = [mlp_send(0)]
 
     def up_tile(t, carry):
         cols = pl.ds(t * 512, 512)
@@ -633,10 +690,8 @@
     lax.fori_loop(0, half_u // 512, up_tile, 0)
     c_start(2)
     c_start(3)
-    y_down.append(c_end(1))
-    m_swap = [mlp_out(0), mlp_out(1)]
-    c_end(2)
-    c_end(3)
+    mlp_out(1)
+    m_swap.append(mlp_send(1))
 
     def hidden_back(i):
         d2_swap[i].wait()
@@ -694,24 +749,21 @@
             sums.append(jnp.sum(step * xr[i, :, cols].astype(f32) * r1, axis=0, keepdims=True))
         return send(d2s.at[i], d1r.at[i], sx.at[13 + i], rx.at[13 + i], xdev), sums
 
-    z_down = []
     grad_gm = hidden_back(0)
+    c_end(2)
     attend_back(0)
-    z_down += y_end(0)
+    c_end(3)
+    z_first.append(first_mid())
     swap_0, sums_0 = inner_back(0)
+    z_down = y_end(1)
     grad_gm += hidden_back(1)
-    z_down += y_end(1)
-    z_down.append(z_mid(0))
     attend_back(1)
     z_down.append(z_mid(1))
-    fd[0:half_d] = z_end(0)
+    for copy in c_down + z_first:
+        gone(copy)
+    first_end()
+    pl.semaphore_signal(free.at[0], inc=1, device_id=cdev, device_id_type=MESH)
     y_end(2)
-    fd[half_d:] = z_end(1)
-    put(fd, fd_out)
-    for copy in c_down + y_down + z_down:
-        gone(copy)
-    for target in (ydev, cdev, ndev, fdev):
-        pl.semaphore_signal(free, inc=1, device_id=target, device_id_type=MESH)
 
     def out_tile(t):
         cols = pl.ds(t * half, half)
@@ -730,21 +782,29 @@
 
     qkv_tile(0)
     qkv_tile(1)
-    pl.semaphore_wait(free, 4)
+    pl.semaphore_wait(free.at[0], 1)
     c_start(4)
+    qkv_tile(2)
+    fd[2 * part :] = z_end(1)
+    for copy in y_down + z_down:
+        gone(copy)
+    for target in (ydev, cdev, ndev, fdev):
+        pl.semaphore_signal(free.at[1], inc=1, device_id=target, device_id_type=MESH)
     out_tile(0)
     out_tile(1)
-    qkv_tile(2)
-    c_start(5)
     c_end(4)
     swap_1, sums_1 = inner_back(1)
     d1_swap = [swap_0, swap_1]
     for j in range(2):
         vs[0:1, j * half : (j + 1) * half] = sums_0[j] + sums_1[j]
     vs[1:2] = grad_gm
+    pl.semaphore_wait(free.at[1], 4)
+    c_start(5)
+    c_start(6)
+    z_mid(2)
     c_end(5)
-    z_mid(2)
     y_end(3)
+    fu[0] = z_end(2)
 
     grad_router = jnp.zeros((1, model), f32)
     for i in range(2):
@@ -759,54 +819,57 @@
     put(m_s, upd_out)
     vs[2:3] = 0.5 * grad_router
     vs[3:8] = jnp.zeros((5, model), f32)
-    send(vs, vr.at[0], gc.at[6], hc.at[6], cdev)
-    fu[0] = z_end(2)
+    send(vs, vr.at[0], gc.at[7], hc.at[7], cdev)
     z_mid(3)
-    arrive(vr.at[0], gc.at[6], hc.at[6], cdev)
+    arrive(vr.at[0], gc.at[7], hc.at[7], cdev)
     v_all[0] = vs[...] + vr[0]
-    send(v_all.at[0], vr.at[1], gy.at[6], hy.at[6], ydev)
-    y_end(4)
+    send(v_all.at[0], vr.at[1], gy.at[7], hy.at[7], ydev)
+    c_end(6)
+    fd[0 : 2 * part] = first_sum()
+    put(fd, fd_out)
     fu[1] = z_end(3)
     suu[...] = fu[1 - s].astype(bf16)
     send(suu, ruu, sx.at[15], rx.at[15], xdev)
     put(fu.at[s], fu_out.at[:, pl.ds(s * half_u, half_u)])
-    arrive(vr.at[1], gy.at[6], hy.at[6], ydev)
-    v_all[1] = v_all[0] + vr[1]
-    send(v_all.at[1], vr.at[2], gz.at[6, 0], hz.at[6, 0], ndev)
-    z_mid(4)
-
-    for i in range(2):
+    y_end(4)
+
+    def rows_back(i):
         d1_swap[i].wait()
         row = xr[i].astype(f32)
         r1 = inverse_rms(row)
         scaled = (d2s[i].astype(f32) + d1r[i].astype(f32)) * gain_one
         step = r1 * scaled - row * (r1 * r1 * r1 * jnp.mean(scaled * row, axis=-1, keepdims=True))
         d2s[i] = (dh[i] + step + logit[i] * router).astype(bf16)
-    put(d2s, dx_out)
-
+        put(d2s.at[i], dx_out.at[i])
+
+    rows_back(0)
     y_end(5)
-    arrive(vr.at[2], gz.at[6, 0], hz.at[6, 0], ndev)
-    v_all[2] = v_all[1] + vr[2]
-    send(v_all.at[2], vr.at[3], gz.at[6, 1], hz.at[6, 1], fdev)
+    arrive(vr.at[1], gy.at[7], hy.at[7], ydev)
+    v_all[1] = v_all[0] + vr[1]
+    send(v_all.at[1], vr.at[2], gz.at[7, 0], hz.at[7, 0], ndev)
+    z_mid(4)
+    rows_back(1)
+    y_end(6)
+    z_mid(5)
     fqk[...] = z_end(4).reshape(fqk.shape)
     sqk[...] = fqk[1 - s].astype(bf16)
     send(sqk, rqk, sx.at[16], rx.at[16], xdev)
-    z_mid(5)
+    for j in range(2):
+        put(fqk.at[s, :, pl.ds(j * half_q, half_q)], fq_out.at[:, pl.ds(2 * j * half_q + s * half_q, half_q)])
+    arrive(vr.at[2], gz.at[7, 0], hz.at[7, 0], ndev)
+    v_all[2] = v_all[1] + vr[2]
+    send(v_all.at[2], vr.at[3], gz.at[7, 1], hz.at[7, 1], fdev)
+    fv[...] = z_end(5)
+    sv[...] = fv[:, pl.ds((1 - s) * half_q, half_q)].astype(bf16)
+    send(sv, rv, sx.at[17], rx.at[17], xdev)
+    put(fv.at[:, pl.ds(s * half_q, half_q)], fq_out.at[:, pl.ds(4 * half_q + s * half_q, half_q)])
+    z_mid(6)
+    arrive(vr.at[3], gz.at[7, 1], hz.at[7, 1], fdev)
+    v_all[3] = v_all[2] + vr[3]
+    send(v_all.at[3], vr.at[4], sx.at[18], rx.at[18], xdev)
     arrive(ruu, sx.at[15], rx.at[15], xdev)
     fu[1 - s] = ruu[...].astype(f32)
     put(fu.at[1 - s], fu_out.at[:, pl.ds((1 - s) * half_u, half_u)])
-    for j in range(2):
-        put(fqk.at[s, :, pl.ds(j * half_q, half_q)], fq_out.at[:, pl.ds(2 * j * half_q + s * half_q, half_q)])
-    arrive(vr.at[3], gz.at[6, 1], hz.at[6, 1], fdev)
-    v_all[3] = v_all[2] + vr[3]
-    send(v_all.at[3], vr.at[4], sx.at[18], rx.at[18], xdev)
-    last = z_end(5)
-    fv[...] = last[0:part]
-    sv[...] = fv[:, pl.ds((1 - s) * half_q, half_q)].astype(bf16)
-    send(sv, rv, sx.at[17], rx.at[17], xdev)
-    fo[...] = last[part:]
-    put(fo, fo_out)
-    put(fv.at[:, pl.ds(s * half_q, half_q)], fq_out.at[:, pl.ds(4 * half_q + s * half_q, half_q)])
     arrive(rqk, sx.at[16], rx.at[16], xdev)
     fqk[1 - s] = rqk[...].astype(f32)
     for j in range(2):
@@ -814,15 +877,17 @@
             fqk.at[1 - s, :, pl.ds(j * half_q, half_q)],
             fq_out.at[:, pl.ds(2 * j * half_q + (1 - s) * half_q, half_q)],
         )
-    arrive(vr.at[4], sx.at[18], rx.at[18], xdev)
-    v_all[4] = v_all[3] + vr[4]
-    put(v_all.at[4], vec_out)
+    fo[...] = z_end(6)
+    put(fo, fo_out)
     arrive(rv, sx.at[17], rx.at[17], xdev)
     fv[:, pl.ds((1 - s) * half_q, half_q)] = rv[...].astype(f32)
     put(
         fv.at[:, pl.ds((1 - s) * half_q, half_q)],
         fq_out.at[:, pl.ds(4 * half_q + (1 - s) * half_q, half_q)],
     )
+    arrive(vr.at[4], sx.at[18], rx.at[18], xdev)
+    v_all[4] = v_all[3] + vr[4]
+    put(v_all.at[4], vec_out)
     waited = x_swap + a_swap + d_swap + d2_swap + m_swap + d1_swap
     for copy in list(sent):
         if not any(copy is other for other in waited):
@@ -888,14 +953,10 @@
     blocked = (slots, local_len // 512, 2, 2, 128, model)
     row_bf16 = space(rows, bf16)
 
-    def land(tall, wide):
-        return [
-            space((2, LINE, 2, tall, wide), bf16),
-            space((2, LINE, tall, wide), bf16),
-            space((2, 3, tall, wide), bf16),
-        ]
-
-    on_d, on_u = land(down // 2, model), land(part, half_u)
+    def land(lead, tall, wide):
+        return [space(lead + mid + (tall, wide), bf16) for mid in ((LINE, 2), (LINE,), (3,))]
+
+    on_d, on_u = land((), down, model), land((2,), part, half_u)
     grad_shapes = (
         sds((part, 6 * half_q), f32), sds((part, model), f32), sds((part, 2 * half_u), f32), sds((down, model), f32),
     )
@@ -914,14 +975,15 @@
             space((slots, ranks, 1), f32), space((16, model), f32),
             space(wd_shape, bf16), space(wu_shape, bf16),
             on_d[0], on_u[0], on_d[1], on_u[1], on_d[2], on_u[2],
+            space((3, 2, 2 * part, model), bf16), space((2 * part, model), bf16),
             space((2, part, model), f32), space((part, model), f32), space((part, model), f32),
             space((2, part, half_u), f32), space((down, model), f32),
             space((part, model), bf16), space((part, half_q), bf16), space((part, half_u), bf16),
             space((part, model), bf16), space((part, half_q), bf16), space((part, half_u), bf16),
             space((8, model), f32), space((5, 8, model), f32), space((5, 8, model), f32),
             dma((16,)), dma((16,)), dma((8, 3)), dma((8, 3)), dma((8, 4)), dma((8, 4)), dma((8, 2)), dma((8, 2)),
-            dma((19,)), dma((19,)), dma((7,)), dma((7,)), dma((7,)), dma((7,)), dma((7, 3)), dma((7, 3)),
-            pltpu.SemaphoreType.REGULAR,
+            dma((19,)), dma((19,)), dma((8,)), dma((8,)), dma((8,)), dma((8,)), dma((8, 3)), dma((8, 3)),
+            pltpu.SemaphoreType.REGULAR((2,)),
         ],
         compiler_params=pltpu.CompilerParams(collective_id=1, has_side_effects=True, vmem_limit_bytes=60 << 20),
         name="block",
@@ -942,7 +1004,7 @@
         out_shape=(sds(tokens.shape, bf16), sds(tokens.shape, bf16)) + grad_shapes + vectors,
         in_specs=[smem, whole(routed.shape), big, big, moved, moved] + whole_grads + [whole((8, model))],
         out_specs=[big, big] + whole_grads + [whole((1, part))] * 3,
-        compiler_params=pltpu.CompilerParams(vmem_limit_bytes=40 << 20),
+        compiler_params=pltpu.CompilerParams(vmem_limit_bytes=60 << 20),
         name="rows",
     )(lengths, routed, tokens, cotangent, upd, dxr, *sums, vec)
     return (

time: 212 us -> 182 us (0.86)
  Pallas kernels: 197 us -> 179 us
  local copies, waits for them, and re-layouts: 11.6 us -> 0.08 us
    pallas_call x1, Pallas kernels: 191 us -> 169 us  [split_device(): pl.pallas_call(block_kernel, out_shape=(sds(rows, bf16), sds(rows, bf16))...]
    unnamed x22 -> x0, local copies, waits for them, and re-layouts: 11.6 us -> none
    pallas_call x1, Pallas kernels: 5.97 us -> 10.3 us  [split_device(): pl.pallas_call(rows_kernel, grid=(slots, local_len // tall), out_shape=(s...]
where the time goes in v4:
time: 182 us
  Pallas kernels  179 us (98%)
    pallas_call x1, Pallas kernels, split_device(): pl.pallas_call(block_kernel, out_shape=(sds(rows, bf16), sds(rows, bf16))...  169 us
    pallas_call x1, Pallas kernels, split_device(): pl.pallas_call(rows_kernel, grid=(slots, local_len // tall), out_shape=(s...  10.3 us

profile of v4, /device:TPU:0, one launch (start us, length us, event | category | flops | bytes accessed | tf_op | source)
XLA Modules:
  0.0 181.6 jit_solution(13307914378377873873)
XLA Ops:
  0.7 0.1 pad.3.clone
  0.7 1.4 maximum_maximum_fusion.small_ref
  2.1 169.1 %block.1 = (bf16[2,256,1024]{2,1,0:T(8,128)(2,1)}, bf16[2,256,1024]{2,1,0:T(8,128)(2,1)}, f32[32,3072]{1,0:T(8,128)}, f32[32,1024]{1,0:T(8,128)}, f32[32,4096]{1...) custom-call(bf16[2,2,2,2,128,1024]{5,4,3,2,1,0:T(8,128)(2,1)} %bitcast.8, bf16[2,2,2,2,128,1024]{5,4,3,2,1,0:T(8,128)(2,1)} %bitcast.9, ...), custom_call_target="tpu_custom_call" | custom-call | tf_op jit(solution)/shard_map/block/pallas_call | solution.py:963
  171.1 10.3 %rows.1 = (bf16[2,1024,1024]{2,1,0:T(8,128)(2,1)}, bf16[2,1024,1024]{2,1,0:T(8,128)(2,1)}, f32[32,3072]{1,0:T(8,128)}, f32[32,1024]{1,0:T(8,128)}, f32[32,4096]{...) custom-call(s32[2]{0:T(128)} %len_ref.3, s32[2,256]{1,0:T(2,128)} %routed_ref.3, ...), custom_call_target="tpu_custom_call" | custom-call | tf_op jit(solution)/shard_map/rows/pallas_call | solution.py:1001
  (1 shorter events, 0.0 us)

commit v5 on v4

--- a/solution.py
+++ b/solution.py
@@ -256,13 +256,13 @@
 
 
 def block_kernel(
-    tok_hbm, cot_hbm, wq_hbm, wo_hbm, wu_hbm, wd_hbm, small_ref, routed_ref, len_ref,
-    upd_out, dx_out, fq_out, fo_out, fu_out, fd_out, vec_out,
+    tok_hbm, cot_hbm, wq_hbm, wo_hbm, wu_hbm, wd_hbm, one_ref, two_ref, three_ref, routed_ref, len_ref,
+    upd_out, dx_out, fq_out, fo_out, fu_out, fd_out, vec_out, live_out,
     wq, wo, wu, wd, gv, stq, stu, stv, rcv,
     xs, xr, ds, dr, a_s, a_r, d2s, d2r, d1r, m_s, m_r, hid, dh, qkv, att, act, gp, logit, gains,
     gd, gu, rcd, rcu, ryd, ryu, rzd, rzu, rzb, ryb,
-    fqk, fv, fo, fu, fd, sqk, sv, suu, rqk, rv, ruu, vs, vr, v_all,
-    loc, out_sem, wz, vz, wy, vy, wc, vc, sx, rx, gc, hc, gy, hy, gz, hz, free,
+    fqk, fv, fo, fu, fd, sqk, sv, suu, rqk, rv, ruu, vs, vr, v_all, live,
+    loc, out_sem, wz, vz, wy, vy, wc, vc, sx, rx, gc, hc, gt, ht, gy, hy, gz, hz, free,
 ):
     s, z, y, c = place()
     near, far = z + 1 - 2 * lax.rem(z, 2), LINE - 1 - z
@@ -391,7 +391,7 @@
         arrive(wd.at[:, :, 1 - c, down_half(1)], wc.at[D_1, 0], vc.at[D_1, 0], cdev)
 
     spans = [pl.ds(0, 2 * part), pl.ds(2 * part, 2 * part), None, None]
-    spans += [pl.ds(0, 2 * part), pl.ds(2 * part, part), pl.ds(3 * part, part)]
+    spans += [pl.ds(i * part, part) for i in range(4)]
     parts = [
         (lambda cc, i=i: gu.at[i - 2, :, :, cc]) if q is None else (lambda cc, q=q: gd.at[:, :, cc, q])
         for i, q in enumerate(spans)
@@ -405,7 +405,11 @@
 
     def c_end(k):
         ref, own = land_c[k], parts[k](c)
-        arrive(ref, gc.at[k], hc.at[k], cdev)
+        if k < 2:
+            for t in range(LINE):
+                arrive(ref.at[t], gt.at[k, t], ht.at[k, t], cdev)
+        else:
+            arrive(ref, gc.at[k], hc.at[k], cdev)
 
         def add(i, carry):
             ref[i] = (ref[i].astype(f32) + own[i].astype(f32)).astype(bf16)
@@ -463,12 +467,18 @@
     fits = (lax.rem(lane, part) == lax.broadcasted_iota(jnp.int32, (part, model), 0)) & (
         lane // part == s * 4 * LINE + z * 4 + y * 2 + c
     )
-    stv[...] = dot_nn(small_ref[...], jnp.where(fits, 1.0, 0.0).astype(bf16)).astype(bf16)
+    line = lax.broadcasted_iota(jnp.int32, (16, part), 0)
+    small = jnp.zeros((16, part), f32)
+    for j, ref in enumerate((one_ref, two_ref, three_ref)):
+        small = jnp.where(line == j, ref[...].astype(f32), small)
+    stv[...] = dot_nn(small.astype(bf16), jnp.where(fits, 1.0, 0.0).astype(bf16)).astype(bf16)
+
+    rank = lax.broadcasted_iota(jnp.int32, (1, ranks), 1)
+    for i in range(2):
+        live[i : i + 1] = jnp.where(rank < len_ref[i] // 8, routed_ref[i : i + 1], -1)
 
     def chooser(i):
-        count = len_ref[i] // 8
-        rank = lax.broadcasted_iota(jnp.int32, (1, ranks), 1)
-        row = jnp.where(rank < count, routed_ref[i : i + 1], -1).astype(f32)
+        row = live[i : i + 1].astype(f32)
         eye = lax.broadcasted_iota(jnp.int32, (ranks, ranks), 0) == lax.broadcasted_iota(
             jnp.int32, (ranks, ranks), 1
         )
@@ -498,6 +508,8 @@
         copy.wait()
     spread(Q_OWN)
     spread_y(Q_OWN)
+    own_d.wait()
+    spread_y(D_1)
     x_swap = []
     get_tok[0].wait()
     pick(0, xs)
@@ -509,6 +521,7 @@
     pick(1, xs)
     x_swap.append(send(xs.at[1], xr.at[1], sx.at[4], rx.at[4], xdev))
     get_cot.append(fetch(cot_hbm.at[1], gd.at[pl.ds(2, 2)]))
+    put(live, live_out)
     swap_v.wait_recv()
     gv[z, y, c] = stv[...] + rcv[...]
     after_far(Q_OWN)
@@ -517,13 +530,11 @@
     arrive(wq.at[1 - s, z, y, c], sx.at[1], rx.at[1], xdev)
     spread(Q_SWAP)
     spread_y(Q_SWAP)
-    own_d.wait()
     get_cot[0].wait()
     pick(0, ds)
     d_swap = [send(ds.at[0], dr.at[0], sx.at[7], rx.at[7], xdev)]
     after_near(Q_OWN)
     after_far(VEC)
-    spread_y(D_1)
     get_cot[1].wait()
     pick(1, ds)
     after_far(Q_SWAP)
@@ -668,16 +679,15 @@
     d2_swap = [mlp_back(0)]
     cotangent_rows(1)
 
-    def down_tile(t, carry):
-        grad = dot_tn(act[:, :, pl.ds(t * 512, 512)].reshape(rows, 512), ds[...].reshape(rows, model))
+    c_down = []
+    for t in range(LINE):
+        grad = dot_tn(act[:, :, t * 512 : t * 512 + 512].reshape(rows, 512), ds[...].reshape(rows, model))
         gd[t] = grad.astype(bf16).reshape(gd.shape[1:])
-        return carry
-
-    lax.fori_loop(0, half_u // 512, down_tile, 0)
-    c_down = [c_start(0), c_start(1)]
+        for k in (1, 0):
+            c_down.append(send(gd.at[t, :, 1 - c, spans[k]], land_c[k].at[t], gt.at[k, t], ht.at[k, t], cdev))
+    y_down = c_end(1)
+    z_first = c_end(0)
     d2_swap.append(mlp_back(1))
-    z_first = c_end(0)
-    y_down = c_end(1)
     mlp_out(0)
     m_swap = [mlp_send(0)]
 
@@ -784,6 +794,7 @@
     qkv_tile(1)
     pl.semaphore_wait(free.at[0], 1)
     c_start(4)
+    c_start(5)
     qkv_tile(2)
     fd[2 * part :] = z_end(1)
     for copy in y_down + z_down:
@@ -793,16 +804,17 @@
     out_tile(0)
     out_tile(1)
     c_end(4)
+    c_end(5)
     swap_1, sums_1 = inner_back(1)
     d1_swap = [swap_0, swap_1]
     for j in range(2):
         vs[0:1, j * half : (j + 1) * half] = sums_0[j] + sums_1[j]
     vs[1:2] = grad_gm
     pl.semaphore_wait(free.at[1], 4)
-    c_start(5)
     c_start(6)
+    c_start(7)
     z_mid(2)
-    c_end(5)
+    c_end(6)
     y_end(3)
     fu[0] = z_end(2)
 
@@ -819,19 +831,21 @@
     put(m_s, upd_out)
     vs[2:3] = 0.5 * grad_router
     vs[3:8] = jnp.zeros((5, model), f32)
-    send(vs, vr.at[0], gc.at[7], hc.at[7], cdev)
+    send(vs, vr.at[0], gc.at[8], hc.at[8], cdev)
     z_mid(3)
-    arrive(vr.at[0], gc.at[7], hc.at[7], cdev)
+    arrive(vr.at[0], gc.at[8], hc.at[8], cdev)
     v_all[0] = vs[...] + vr[0]
-    send(v_all.at[0], vr.at[1], gy.at[7], hy.at[7], ydev)
-    c_end(6)
+    send(v_all.at[0], vr.at[1], gy.at[8], hy.at[8], ydev)
+    c_end(7)
     fd[0 : 2 * part] = first_sum()
     put(fd, fd_out)
+    y_end(4)
     fu[1] = z_end(3)
     suu[...] = fu[1 - s].astype(bf16)
     send(suu, ruu, sx.at[15], rx.at[15], xdev)
     put(fu.at[s], fu_out.at[:, pl.ds(s * half_u, half_u)])
-    y_end(4)
+    z_mid(4)
+    y_end(5)
 
     def rows_back(i):
         d1_swap[i].wait()
@@ -843,28 +857,29 @@
         put(d2s.at[i], dx_out.at[i])
 
     rows_back(0)
-    y_end(5)
-    arrive(vr.at[1], gy.at[7], hy.at[7], ydev)
+    z_mid(5)
+    y_end(6)
+    arrive(vr.at[1], gy.at[8], hy.at[8], ydev)
     v_all[1] = v_all[0] + vr[1]
-    send(v_all.at[1], vr.at[2], gz.at[7, 0], hz.at[7, 0], ndev)
-    z_mid(4)
-    rows_back(1)
-    y_end(6)
-    z_mid(5)
-    fqk[...] = z_end(4).reshape(fqk.shape)
+    send(v_all.at[1], vr.at[2], gz.at[8, 0], hz.at[8, 0], ndev)
+    z_mid(6)
+    y_end(7)
+    for i in range(2):
+        fqk[i] = z_end(4 + i)
     sqk[...] = fqk[1 - s].astype(bf16)
     send(sqk, rqk, sx.at[16], rx.at[16], xdev)
     for j in range(2):
         put(fqk.at[s, :, pl.ds(j * half_q, half_q)], fq_out.at[:, pl.ds(2 * j * half_q + s * half_q, half_q)])
-    arrive(vr.at[2], gz.at[7, 0], hz.at[7, 0], ndev)
+    arrive(vr.at[2], gz.at[8, 0], hz.at[8, 0], ndev)
     v_all[2] = v_all[1] + vr[2]
-    send(v_all.at[2], vr.at[3], gz.at[7, 1], hz.at[7, 1], fdev)
-    fv[...] = z_end(5)
+    send(v_all.at[2], vr.at[3], gz.at[8, 1], hz.at[8, 1], fdev)
+    fv[...] = z_end(6)
     sv[...] = fv[:, pl.ds((1 - s) * half_q, half_q)].astype(bf16)
     send(sv, rv, sx.at[17], rx.at[17], xdev)
     put(fv.at[:, pl.ds(s * half_q, half_q)], fq_out.at[:, pl.ds(4 * half_q + s * half_q, half_q)])
-    z_mid(6)
-    arrive(vr.at[3], gz.at[7, 1], hz.at[7, 1], fdev)
+    z_mid(7)
+    rows_back(1)
+    arrive(vr.at[3], gz.at[8, 1], hz.at[8, 1], fdev)
     v_all[3] = v_all[2] + vr[3]
     send(v_all.at[3], vr.at[4], sx.at[18], rx.at[18], xdev)
     arrive(ruu, sx.at[15], rx.at[15], xdev)
@@ -877,7 +892,7 @@
             fqk.at[1 - s, :, pl.ds(j * half_q, half_q)],
             fq_out.at[:, pl.ds(2 * j * half_q + (1 - s) * half_q, half_q)],
         )
-    fo[...] = z_end(6)
+    fo[...] = z_end(7)
     put(fo, fo_out)
     arrive(rv, sx.at[17], rx.at[17], xdev)
     fv[:, pl.ds((1 - s) * half_q, half_q)] = rv[...].astype(f32)
@@ -897,39 +912,69 @@
 
 
 def rows_kernel(
-    len_ref, routed_ref, tok_ref, cot_ref, upd_ref, dx_ref, fq_ref, fo_ref, fu_ref, fd_ref, vec_ref,
-    out_ref, grad_ref, fq_out, fo_out, fu_out, fd_out, one_out, two_out, three_out,
+    tok_hbm, cot_hbm, upd_hbm, dx_hbm, fq_hbm, fo_hbm, fu_hbm, fd_hbm, vec_hbm, live_hbm,
+    out_hbm, grad_hbm, fq_out, fo_out, fu_out, fd_out, one_out, two_out, three_out,
+    bases, moved, fq, fo, fu, fd, vec_ref, live_ref, one, two, three, get_sem, put_sem, rows_sem, pass_sem,
 ):
-    slot, step = pl.program_id(0), pl.program_id(1)
     s = lax.axis_index("seq")
-    tall, model = tok_ref.shape[1:]
-    ranks = upd_ref.shape[1]
-    rank = lax.broadcasted_iota(jnp.int32, (1, ranks), 1)
-    routed = jnp.where(rank < len_ref[slot] // 8, routed_ref[pl.ds(slot, 1)], -1)
-    first = (s * pl.num_programs(1) + step) * tall
-    position = lax.broadcasted_iota(jnp.int32, (tall, ranks), 0) + first
-    chooser = jnp.where(position == routed, 1.0, 0.0).astype(bf16)
-    out_ref[0] = (tok_ref[0].astype(f32) + dot_nn(chooser, upd_ref[0])).astype(bf16)
-    grad_ref[0] = (cot_ref[0].astype(f32) + dot_nn(chooser, dx_ref[0])).astype(bf16)
-
-    @pl.when((slot == 0) & (step == 0))
-    def _():
-        fq_out[...] = fq_ref[...]
-        fo_out[...] = fo_ref[...]
-        fu_out[...] = fu_ref[...]
-        fd_out[...] = fd_ref[...]
-        part = one_out.shape[1]
-        flat = s * lax.axis_size("batch") + lax.axis_index("batch")
-        lane = lax.broadcasted_iota(jnp.int32, (part, model), 1)
-        here = (lane // part == flat) & (
-            lax.rem(lane, part) == lax.broadcasted_iota(jnp.int32, (part, model), 0)
-        )
-        eye = lax.broadcasted_iota(jnp.int32, (part, part), 0) == lax.broadcasted_iota(
-            jnp.int32, (part, part), 1
-        )
-        for j, ref in enumerate((one_out, two_out, three_out)):
-            column = jnp.sum(jnp.where(here, vec_ref[j : j + 1], 0.0), axis=1, keepdims=True)
-            ref[...] = jnp.sum(jnp.where(eye, column, 0.0), axis=0, keepdims=True)
+    _, slots, chunks, tall, model = bases.shape
+    ranks = moved.shape[2]
+    whole = (tok_hbm, cot_hbm), (out_hbm, grad_hbm)
+    tasks = [(i, t) for i in range(slots) for t in range(chunks)]
+
+    def part_of(ref, i, t):
+        return ref.at[i, pl.ds(t * tall, tall)]
+
+    gets, puts = {}, []
+    rows = [
+        pltpu.make_async_copy(src.at[i], moved.at[a, i], rows_sem.at[a, i])
+        for i in range(slots)
+        for a, src in enumerate((upd_hbm, dx_hbm))
+    ]
+    get_live = pltpu.make_async_copy(live_hbm, live_ref, pass_sem.at[0, 4])
+    get_vec = pltpu.make_async_copy(vec_hbm, vec_ref, pass_sem.at[0, 5])
+    get_live.start()
+    for i, t in tasks:
+        for copy in rows[2 * i : 2 * i + 2] if t == 0 else []:
+            copy.start()
+        for a in range(2):
+            gets[a, i, t] = pltpu.make_async_copy(part_of(whole[0][a], i, t), bases.at[a, i, t], get_sem.at[a, i, t])
+            gets[a, i, t].start()
+    through = ((fq_hbm, fq, fq_out), (fo_hbm, fo, fo_out), (fu_hbm, fu, fu_out), (fd_hbm, fd, fd_out))
+    taken = [pltpu.make_async_copy(src, mid, pass_sem.at[0, j]) for j, (src, mid, _) in enumerate(through)]
+    passed = [pltpu.make_async_copy(mid, dst, pass_sem.at[1, j]) for j, (_, mid, dst) in enumerate(through)]
+    for copy in taken + [get_vec]:
+        copy.start()
+    get_live.wait()
+    for n, (i, t) in enumerate(tasks):
+        if n == len(tasks) - 2:
+            for j in range(4):
+                taken[j].wait()
+                passed[j].start()
+        position = lax.broadcasted_iota(jnp.int32, (tall, ranks), 0) + ((s * chunks + t) * tall)
+        chooser = jnp.where(position == live_ref[i : i + 1], 1.0, 0.0).astype(bf16)
+        for a in range(2):
+            if t == 0:
+                rows[2 * i + a].wait()
+            gets[a, i, t].wait()
+            bases[a, i, t] += dot_nn(chooser, moved[a, i]).astype(bf16)
+            copy = pltpu.make_async_copy(bases.at[a, i, t], part_of(whole[1][a], i, t), put_sem.at[a, i, t])
+            copy.start()
+            puts.append(copy)
+    part = one.shape[1]
+    get_vec.wait()
+    flat = s * lax.axis_size("batch") + lax.axis_index("batch")
+    lane = lax.broadcasted_iota(jnp.int32, (part, model), 1)
+    row = lax.broadcasted_iota(jnp.int32, (part, model), 0)
+    here = (lane // part == flat) & (lax.rem(lane, part) == row)
+    eye = lax.broadcasted_iota(jnp.int32, (part, part), 0) == lax.broadcasted_iota(jnp.int32, (part, part), 1)
+    for j, (ref, dst) in enumerate(((one, one_out), (two, two_out), (three, three_out))):
+        column = jnp.sum(jnp.where(here, vec_ref[j : j + 1], 0.0), axis=1, keepdims=True)
+        ref[...] = jnp.sum(jnp.where(eye, column, 0.0), axis=0, keepdims=True)
+        puts.append(pltpu.make_async_copy(ref, dst, pass_sem.at[1, 4 + j]))
+        puts[-1].start()
+    for copy in passed + puts:
+        copy.wait()
 
 
 def split_device(
@@ -939,9 +984,6 @@
     ranks = routed.shape[1]
     half_q, half_u = w_qkv.shape[1] // 6, w_up.shape[1] // 2
     part, down = w_qkv.shape[0], w_down.shape[0]
-    small = jnp.concatenate(
-        [gain_attn[None], gain_mlp[None], router[None], jnp.zeros((13, part), bf16)], axis=0
-    )
     hbm = pl.BlockSpec(memory_space=pl.ANY)
     vmem = pl.BlockSpec(memory_space=pltpu.VMEM)
     smem = pl.BlockSpec(memory_space=pltpu.SMEM)
@@ -960,11 +1002,11 @@
     grad_shapes = (
         sds((part, 6 * half_q), f32), sds((part, model), f32), sds((part, 2 * half_u), f32), sds((down, model), f32),
     )
-    upd, dxr, *sums, vec = pl.pallas_call(
+    upd, dxr, *sums, vec, live = pl.pallas_call(
         block_kernel,
-        out_shape=(sds(rows, bf16), sds(rows, bf16)) + grad_shapes + (sds((8, model), f32),),
-        in_specs=[hbm] * 6 + [vmem] * 2 + [smem],
-        out_specs=[hbm] * 7,
+        out_shape=(sds(rows, bf16), sds(rows, bf16)) + grad_shapes + (sds((8, model), f32), sds(routed.shape, jnp.int32)),
+        in_specs=[hbm] * 6 + [vmem] * 4 + [smem],
+        out_specs=[hbm] * 8,
         scratch_shapes=[
             space(wq_shape, bf16), space(wo_shape, bf16), space(wu_shape, bf16), space(wd_shape, bf16),
             space(grid + (16, model), bf16),
@@ -980,33 +1022,34 @@
             space((2, part, half_u), f32), space((down, model), f32),
             space((part, model), bf16), space((part, half_q), bf16), space((part, half_u), bf16),
             space((part, model), bf16), space((part, half_q), bf16), space((part, half_u), bf16),
-            space((8, model), f32), space((5, 8, model), f32), space((5, 8, model), f32),
+            space((8, model), f32), space((5, 8, model), f32), space((5, 8, model), f32), space(routed.shape, jnp.int32),
             dma((16,)), dma((16,)), dma((8, 3)), dma((8, 3)), dma((8, 4)), dma((8, 4)), dma((8, 2)), dma((8, 2)),
-            dma((19,)), dma((19,)), dma((8,)), dma((8,)), dma((8,)), dma((8,)), dma((8, 3)), dma((8, 3)),
+            dma((19,)), dma((19,)), dma((9,)), dma((9,)), dma((2, LINE)), dma((2, LINE)), dma((9,)), dma((9,)), dma((9, 3)), dma((9, 3)),
             pltpu.SemaphoreType.REGULAR((2,)),
         ],
         compiler_params=pltpu.CompilerParams(collective_id=1, has_side_effects=True, vmem_limit_bytes=60 << 20),
         name="block",
-    )(tokens.reshape(blocked), cotangent.reshape(blocked), w_qkv, w_out, w_up, w_down, small, routed, lengths)
-
-    tall = 512
-    big = pl.BlockSpec((1, tall, model), lambda i, j: (i, j, 0))
-    moved = pl.BlockSpec((1, ranks, model), lambda i, j: (i, 0, 0))
-
-    def whole(shape):
-        return pl.BlockSpec(shape, lambda i, j: (0, 0))
-
-    whole_grads = [whole(g.shape) for g in grad_shapes]
+    )(
+        tokens.reshape(blocked), cotangent.reshape(blocked), w_qkv, w_out, w_up, w_down,
+        gain_attn[None], gain_mlp[None], router[None], routed, lengths,
+    )
+
+    chunks = 2
     vectors = (sds((1, part), f32),) * 3
     output, input_grad, g_qkv, g_out, g_up, g_down, g_one, g_two, g_three = pl.pallas_call(
         rows_kernel,
-        grid=(slots, local_len // tall),
         out_shape=(sds(tokens.shape, bf16), sds(tokens.shape, bf16)) + grad_shapes + vectors,
-        in_specs=[smem, whole(routed.shape), big, big, moved, moved] + whole_grads + [whole((8, model))],
-        out_specs=[big, big] + whole_grads + [whole((1, part))] * 3,
+        in_specs=[hbm] * 10,
+        out_specs=[hbm] * 9,
+        scratch_shapes=[
+            space((2, slots, chunks, local_len // chunks, model), bf16), space((2,) + rows, bf16),
+            *[space(g.shape, f32) for g in grad_shapes],
+            space((8, model), f32), space(routed.shape, jnp.int32), *[space((1, part), f32)] * 3,
+            dma((2, slots, chunks)), dma((2, slots, chunks)), dma((2, slots)), dma((2, 7)),
+        ],
         compiler_params=pltpu.CompilerParams(vmem_limit_bytes=60 << 20),
         name="rows",
-    )(lengths, routed, tokens, cotangent, upd, dxr, *sums, vec)
+    )(tokens, cotangent, upd, dxr, *sums, vec, live)
     return (
         output, input_grad, g_qkv, g_out, g_up, g_down,
         g_one.reshape(part), g_two.reshape(part), g_three.reshape(part),

time: 182 us -> 172 us (0.945)
  Pallas kernels: 179 us -> 171 us
    pallas_call x1, Pallas kernels: 169 us -> 163 us  [split_device(): pl.pallas_call(block_kernel, out_shape=(sds(rows, bf16), sds(rows, bf16))...]
    pallas_call x1, Pallas kernels: 10.3 us -> 7.65 us  [split_device(): pl.pallas_call(rows_kernel, out_shape=(sds(tokens.shape, bf16), sds(token...]
where the time goes in v5:
time: 172 us
  Pallas kernels  171 us (99%)
    pallas_call x1, Pallas kernels, split_device(): pl.pallas_call(block_kernel, out_shape=(sds(rows, bf16), sds(rows, bf16))...  163 us
    pallas_call x1, Pallas kernels, split_device(): pl.pallas_call(rows_kernel, out_shape=(sds(tokens.shape, bf16), sds(token...  7.65 us

profile of v5, /device:TPU:0, one launch (start us, length us, event | category | flops | bytes accessed | tf_op | source)
XLA Modules:
  0.0 171.8 jit_solution(11092076973926699826)
XLA Ops:
  0.6 163.3 %block.1 = (bf16[2,256,1024]{2,1,0:T(8,128)(2,1)}, bf16[2,256,1024]{2,1,0:T(8,128)(2,1)}, f32[32,3072]{1,0:T(8,128)}, f32[32,1024]{1,0:T(8,128)}, f32[32,4096]{1...) custom-call(bf16[2,2,2,2,128,1024]{5,4,3,2,1,0:T(8,128)(2,1)} %bitcast.8, ...), custom_call_target="tpu_custom_call" | custom-call | tf_op jit(solution)/shard_map/block/pallas_call | solution.py:1005
  164.0 7.7 %rows.1 = (bf16[2,1024,1024]{2,1,0:T(8,128)(2,1)}, bf16[2,1024,1024]{2,1,0:T(8,128)(2,1)}, f32[32,3072]{1,0:T(8,128)}, f32[32,1024]{1,0:T(8,128)}, f32[32,4096]{...) custom-call(bf16[2,1024,1024]{2,1,0:T(8,128)(2,1)} %tok_hbm.1, ...), custom_call_target="tpu_custom_call" | custom-call | tf_op jit(solution)/shard_map/rows/pallas_call | solution.py:1039

commit v6 on v5

--- a/solution.py
+++ b/solution.py
@@ -670,21 +670,32 @@
     after_c(U_SWAP)
     mlp_up(0)
     after_near(D_0)
+    cotangent_rows(0)
+
+    def down_tile(t, carry):
+        gd[t] = dot_tn(act[0, :, pl.ds(t * 512, 512)], ds[0]).astype(bf16).reshape(gd.shape[1:])
+        return carry
+
+    lax.fori_loop(0, LINE, down_tile, 0)
     mlp_up(1)
     after_y(D_0)
     after_c(D_0)
     after_first_near()
     after_first_c()
-    cotangent_rows(0)
     d2_swap = [mlp_back(0)]
     cotangent_rows(1)
 
     c_down = []
+
+    def c_tile(t, k):
+        c_down.append(send(gd.at[t, :, 1 - c, spans[k]], land_c[k].at[t], gt.at[k, t], ht.at[k, t], cdev))
+
     for t in range(LINE):
-        grad = dot_tn(act[:, :, t * 512 : t * 512 + 512].reshape(rows, 512), ds[...].reshape(rows, model))
-        gd[t] = grad.astype(bf16).reshape(gd.shape[1:])
-        for k in (1, 0):
-            c_down.append(send(gd.at[t, :, 1 - c, spans[k]], land_c[k].at[t], gt.at[k, t], ht.at[k, t], cdev))
+        grad = dot_tn(act[1, :, t * 512 : t * 512 + 512], ds[1])
+        gd[t] = (gd[t].astype(f32) + grad.reshape(gd.shape[1:])).astype(bf16)
+        c_tile(t, 1)
+    for t in range(LINE):
+        c_tile(t, 0)
     y_down = c_end(1)
     z_first = c_end(0)
     d2_swap.append(mlp_back(1))
@@ -835,7 +846,7 @@
     z_mid(3)
     arrive(vr.at[0], gc.at[8], hc.at[8], cdev)
     v_all[0] = vs[...] + vr[0]
-    send(v_all.at[0], vr.at[1], gy.at[8], hy.at[8], ydev)
+    send(v_all.at[0], vr.at[1], gz.at[8, 0], hz.at[8, 0], ndev)
     c_end(7)
     fd[0 : 2 * part] = first_sum()
     put(fd, fd_out)
@@ -844,6 +855,9 @@
     suu[...] = fu[1 - s].astype(bf16)
     send(suu, ruu, sx.at[15], rx.at[15], xdev)
     put(fu.at[s], fu_out.at[:, pl.ds(s * half_u, half_u)])
+    arrive(vr.at[1], gz.at[8, 0], hz.at[8, 0], ndev)
+    v_all[1] = v_all[0] + vr[1]
+    send(v_all.at[1], vr.at[2], gz.at[8, 1], hz.at[8, 1], fdev)
     z_mid(4)
     y_end(5)
 
@@ -857,31 +871,28 @@
         put(d2s.at[i], dx_out.at[i])
 
     rows_back(0)
+    arrive(vr.at[2], gz.at[8, 1], hz.at[8, 1], fdev)
+    v_all[2] = v_all[1] + vr[2]
+    send(v_all.at[2], vr.at[3], gy.at[8], hy.at[8], ydev)
     z_mid(5)
     y_end(6)
-    arrive(vr.at[1], gy.at[8], hy.at[8], ydev)
-    v_all[1] = v_all[0] + vr[1]
-    send(v_all.at[1], vr.at[2], gz.at[8, 0], hz.at[8, 0], ndev)
     z_mid(6)
     y_end(7)
+    arrive(vr.at[3], gy.at[8], hy.at[8], ydev)
+    v_all[3] = v_all[2] + vr[3]
+    send(v_all.at[3], vr.at[4], sx.at[18], rx.at[18], xdev)
     for i in range(2):
         fqk[i] = z_end(4 + i)
     sqk[...] = fqk[1 - s].astype(bf16)
     send(sqk, rqk, sx.at[16], rx.at[16], xdev)
     for j in range(2):
         put(fqk.at[s, :, pl.ds(j * half_q, half_q)], fq_out.at[:, pl.ds(2 * j * half_q + s * half_q, half_q)])
-    arrive(vr.at[2], gz.at[8, 0], hz.at[8, 0], ndev)
-    v_all[2] = v_all[1] + vr[2]
-    send(v_all.at[2], vr.at[3], gz.at[8, 1], hz.at[8, 1], fdev)
     fv[...] = z_end(6)
     sv[...] = fv[:, pl.ds((1 - s) * half_q, half_q)].astype(bf16)
     send(sv, rv, sx.at[17], rx.at[17], xdev)
     put(fv.at[:, pl.ds(s * half_q, half_q)], fq_out.at[:, pl.ds(4 * half_q + s * half_q, half_q)])
     z_mid(7)
     rows_back(1)
-    arrive(vr.at[3], gz.at[8, 1], hz.at[8, 1], fdev)
-    v_all[3] = v_all[2] + vr[3]
-    send(v_all.at[3], vr.at[4], sx.at[18], rx.at[18], xdev)
     arrive(ruu, sx.at[15], rx.at[15], xdev)
     fu[1 - s] = ruu[...].astype(f32)
     put(fu.at[1 - s], fu_out.at[:, pl.ds((1 - s) * half_u, half_u)])

time: 172 us -> 170 us (0.988)
  Pallas kernels: 171 us -> 169 us
where the time goes in v6:
time: 170 us
  Pallas kernels  169 us (99%)
    pallas_call x1, Pallas kernels, split_device(): pl.pallas_call(block_kernel, out_shape=(sds(rows, bf16), sds(rows, bf16))...  162 us
    pallas_call x1, Pallas kernels, split_device(): pl.pallas_call(rows_kernel, out_shape=(sds(tokens.shape, bf16), sds(token...  7.65 us

profile of v6, /device:TPU:0, one launch (start us, length us, event | category | flops | bytes accessed | tf_op | source)
XLA Modules:
  0.0 170.2 jit_solution(5404930223589268009)
XLA Ops:
  0.6 161.7 %block.1 = (bf16[2,256,1024]{2,1,0:T(8,128)(2,1)}, bf16[2,256,1024]{2,1,0:T(8,128)(2,1)}, f32[32,3072]{1,0:T(8,128)}, f32[32,1024]{1,0:T(8,128)}, f32[32,4096]{1...) custom-call(bf16[2,2,2,2,128,1024]{5,4,3,2,1,0:T(8,128)(2,1)} %bitcast.8, ...), custom_call_target="tpu_custom_call" | custom-call | tf_op jit(solution)/shard_map/block/pallas_call | solution.py:1016
  162.4 7.7 %rows.1 = (bf16[2,1024,1024]{2,1,0:T(8,128)(2,1)}, bf16[2,1024,1024]{2,1,0:T(8,128)(2,1)}, f32[32,3072]{1,0:T(8,128)}, f32[32,1024]{1,0:T(8,128)}, f32[32,4096]{...) custom-call(bf16[2,1024,1024]{2,1,0:T(8,128)(2,1)} %tok_hbm.1, ...), custom_call_target="tpu_custom_call" | custom-call | tf_op jit(solution)/shard_map/rows/pallas_call | solution.py:1050

commit v7 on v6

--- a/solution.py
+++ b/solution.py
@@ -256,12 +256,13 @@
 
 
 def block_kernel(
-    tok_hbm, cot_hbm, wq_hbm, wo_hbm, wu_hbm, wd_hbm, one_ref, two_ref, three_ref, routed_ref, len_ref,
+    tok_hbm, cot_hbm, wq_hbm, wo_hbm, wu_hbm, wd_hbm, one_hbm, two_hbm, three_hbm, routed_hbm, len_hbm,
     upd_out, dx_out, fq_out, fo_out, fu_out, fd_out, vec_out, live_out,
     wq, wo, wu, wd, gv, stq, stu, stv, rcv,
     xs, xr, ds, dr, a_s, a_r, d2s, d2r, d1r, m_s, m_r, hid, dh, qkv, att, act, gp, logit, gains,
     gd, gu, rcd, rcu, ryd, ryu, rzd, rzu, rzb, ryb,
     fqk, fv, fo, fu, fd, sqk, sv, suu, rqk, rv, ruu, vs, vr, v_all, live,
+    one_ref, two_ref, three_ref, routed_ref, len_ref,
     loc, out_sem, wz, vz, wy, vy, wc, vc, sx, rx, gc, hc, gt, ht, gy, hy, gz, hz, free,
 ):
     s, z, y, c = place()
@@ -298,7 +299,17 @@
         copy.start()
         outs.append(copy)
 
+    barrier = pltpu.get_barrier_semaphore()
+    for target in (xdev, ydev, cdev, ndev, fdev):
+        pl.semaphore_signal(barrier, inc=1, device_id=target, device_id_type=MESH)
+
     stage, own_q = [], []
+    small_in = [
+        fetch(src, dst)
+        for src, dst in (
+            (one_hbm, one_ref), (two_hbm, two_ref), (three_hbm, three_ref), (routed_hbm, routed_ref), (len_hbm, len_ref),
+        )
+    ]
     for j in range(3):
         base, dst = 2 * j * half_q, pl.ds(j * half_q, half_q)
         stage.append(fetch(wq_hbm.at[:, pl.ds(base + (1 - s) * half_q, half_q)], stq.at[:, dst]))
@@ -334,61 +345,85 @@
     ]
     Q_OWN, Q_SWAP, VEC, OUT, U_OWN, U_SWAP, D_0, D_1 = range(8)
 
+    planes = [
+        lambda cc: wq.at[s, :, :, cc],
+        lambda cc: wq.at[1 - s, :, :, cc],
+        lambda cc: gv.at[:, :, cc],
+        lambda cc: wo.at[:, :, cc],
+        lambda cc: wu.at[s, :, :, cc],
+        lambda cc: wu.at[1 - s, :, :, cc],
+        lambda cc: wd.at[:, :, cc, down_half(0)],
+        lambda cc: wd.at[:, :, cc, down_half(1)],
+    ]
+
+    def pass_on(ref, send_sem, recv_sem, target):
+        remote(ref, ref, send_sem, recv_sem, target).start()
+
     def spread(p):
         own = blocks[p](z, y, c)
-        send(own, own, wz.at[p, 0], vz.at[p, 0], fdev)
-        send(own, own, wz.at[p, 1], vz.at[p, 1], ndev)
+        pass_on(own, wz.at[p], vz.at[p, 0], fdev)
+        pass_on(own, wz.at[p], vz.at[p, 1], ndev)
 
     def spread_y(p):
-        own = blocks[p](z, y, c)
-        send(own, own, wy.at[p, 0], vy.at[p, 0], ydev)
+        pass_on(blocks[p](z, y, c), wy.at[p], vy.at[p], ydev)
 
     def after_far(p):
         ref = blocks[p](far, y, c)
-        arrive(ref, wz.at[p, 0], vz.at[p, 0], fdev)
-        send(ref, ref, wz.at[p, 2], vz.at[p, 2], ndev)
-        send(ref, ref, wy.at[p, 1], vy.at[p, 1], ydev)
+        arrive(ref, wz.at[p], vz.at[p, 0], fdev)
+        pass_on(ref, wz.at[p], vz.at[p, 2], ndev)
+        pass_on(ref, wy.at[p], vy.at[p], ydev)
 
     def after_near(p):
         for i, zz in ((1, near), (2, LINE - 1 - near)):
             ref = blocks[p](zz, y, c)
-            arrive(ref, wz.at[p, i], vz.at[p, i], ndev)
-            send(ref, ref, wy.at[p, i + 1], vy.at[p, i + 1], ydev)
-        line = lines[p](y, c)
-        send(line, line, wc.at[p, 0], vc.at[p, 0], cdev)
+            arrive(ref, wz.at[p], vz.at[p, i], ndev)
+            pass_on(ref, wy.at[p], vy.at[p], ydev)
+        pass_on(lines[p](y, c), wc.at[p], vc.at[p], cdev)
 
     def after_y(p):
-        for i, zz in enumerate((z, far, near, LINE - 1 - near)):
-            arrive(blocks[p](zz, 1 - y, c), wy.at[p, i], vy.at[p, i], ydev)
         line = lines[p](1 - y, c)
-        send(line, line, wc.at[p, 1], vc.at[p, 1], cdev)
+        arrive(line, wy.at[p], vy.at[p], ydev)
+        pass_on(line, wc.at[p], vc.at[p], cdev)
 
     def after_c(p):
-        for i, yy in enumerate((y, 1 - y)):
-            arrive(lines[p](yy, 1 - c), wc.at[p, i], vc.at[p, i], cdev)
+        arrive(planes[p](1 - c), wc.at[p], vc.at[p], cdev)
 
     def both(zz, cc):
         return wd.at[zz, :, cc, down_half(1)]
 
     def after_first_y():
-        arrive(blocks[D_1](z, 1 - y, c), wy.at[D_1, 0], vy.at[D_1, 0], ydev)
+        arrive(blocks[D_1](z, 1 - y, c), wy.at[D_1], vy.at[D_1], ydev)
         own = both(z, c)
-        send(own, own, wz.at[D_1, 0], vz.at[D_1, 0], fdev)
-        send(own, own, wz.at[D_1, 1], vz.at[D_1, 1], ndev)
+        pass_on(own, wz.at[D_1], vz.at[D_1, 0], fdev)
+        pass_on(own, wz.at[D_1], vz.at[D_1, 1], ndev)
 
     def after_first_far():
         ref = both(far, c)
-        arrive(ref, wz.at[D_1, 0], vz.at[D_1, 0], fdev)
-        send(ref, ref, wz.at[D_1, 2], vz.at[D_1, 2], ndev)
+        arrive(ref, wz.at[D_1], vz.at[D_1, 0], fdev)
+        pass_on(ref, wz.at[D_1], vz.at[D_1, 2], ndev)
 
     def after_first_near():
         for i, zz in ((1, near), (2, LINE - 1 - near)):
-            arrive(both(zz, c), wz.at[D_1, i], vz.at[D_1, i], ndev)
-        ref = wd.at[:, :, c, down_half(1)]
-        send(ref, ref, wc.at[D_1, 0], vc.at[D_1, 0], cdev)
+            arrive(both(zz, c), wz.at[D_1], vz.at[D_1, i], ndev)
+        pass_on(planes[D_1](c), wc.at[D_1], vc.at[D_1], cdev)
 
     def after_first_c():
-        arrive(wd.at[:, :, 1 - c, down_half(1)], wc.at[D_1, 0], vc.at[D_1, 0], cdev)
+        arrive(planes[D_1](1 - c), wc.at[D_1], vc.at[D_1], cdev)
+
+    def left(ref, send_sem, recv_sem, target):
+        remote(ref, ref, send_sem, recv_sem, target).wait_send()
+
+    def gathered():
+        three = pl.ds(0, LINE - 1)
+        passed = [
+            wq.at[s, three, y, c], wq.at[1 - s, three, y, c], gv.at[three, y, c], wo.at[three, y, c],
+            wu.at[s, three, y, c], wu.at[1 - s, three, y, c], wd.at[three, y, c, down_half(0)],
+            wd.at[three, :, c, down_half(1)],
+        ]
+        for p in range(8):
+            left(passed[p], wz.at[p], vz.at[p, 0], ndev)
+            left(blocks[p](z, y, c) if p == D_1 else lines[p](y, c), wy.at[p], vy.at[p], ydev)
+            left(planes[p](c), wc.at[p], vc.at[p], cdev)
 
     spans = [pl.ds(0, 2 * part), pl.ds(2 * part, 2 * part), None, None]
     spans += [pl.ds(i * part, part) for i in range(4)]
@@ -406,8 +441,7 @@
     def c_end(k):
         ref, own = land_c[k], parts[k](c)
         if k < 2:
-            for t in range(LINE):
-                arrive(ref.at[t], gt.at[k, t], ht.at[k, t], cdev)
+            arrive(ref, gt.at[k], ht.at[k], cdev)
         else:
             arrive(ref, gc.at[k], hc.at[k], cdev)
 
@@ -463,6 +497,8 @@
         arrive(ryb, gy.at[0], hy.at[0], ydev)
         return rzb[0, y].astype(f32) + ryb[...].astype(f32)
 
+    for copy in small_in:
+        copy.wait()
     lane = lax.broadcasted_iota(jnp.int32, (part, model), 1)
     fits = (lax.rem(lane, part) == lax.broadcasted_iota(jnp.int32, (part, model), 0)) & (
         lane // part == s * 4 * LINE + z * 4 + y * 2 + c
@@ -474,8 +510,12 @@
     stv[...] = dot_nn(small.astype(bf16), jnp.where(fits, 1.0, 0.0).astype(bf16)).astype(bf16)
 
     rank = lax.broadcasted_iota(jnp.int32, (1, ranks), 1)
+
+    def count(i):
+        return lax.shift_right_arithmetic(len_ref[:, i : i + 1], 3)
+
     for i in range(2):
-        live[i : i + 1] = jnp.where(rank < len_ref[i] // 8, routed_ref[i : i + 1], -1)
+        live[i : i + 1] = jnp.where(rank < count(i), routed_ref[i : i + 1], -1)
 
     def chooser(i):
         row = live[i : i + 1].astype(f32)
@@ -492,18 +532,18 @@
 
     def live_column(i):
         rank = lax.broadcasted_iota(jnp.int32, (ranks, 1), 0)
-        return jnp.where(rank < len_ref[i] // 8, 1.0, 0.0).astype(f32)
+        return jnp.where(rank < count(i), 1.0, 0.0).astype(f32)
 
     def allowed(i):
         query = lax.broadcasted_iota(jnp.int32, (ranks, ranks), 0)
         key = lax.broadcasted_iota(jnp.int32, (ranks, ranks), 1)
-        return (key <= query) & (key < len_ref[i] // 8)
-
-    greet([xdev, ydev, cdev, ndev, fdev])
-    swap_v = send(stv, rcv, sx.at[0], rx.at[0], xdev)
+        return (key <= query) & (key < count(i))
+
     for copy in stage:
         copy.wait()
+    pl.semaphore_wait(barrier, 5)
     send(stq, wq.at[s, z, y, c], sx.at[1], rx.at[1], xdev)
+    swap_v = send(stv, rcv, sx.at[0], rx.at[0], xdev)
     for copy in own_q:
         copy.wait()
     spread(Q_OWN)
@@ -685,10 +725,8 @@
     d2_swap = [mlp_back(0)]
     cotangent_rows(1)
 
-    c_down = []
-
     def c_tile(t, k):
-        c_down.append(send(gd.at[t, :, 1 - c, spans[k]], land_c[k].at[t], gt.at[k, t], ht.at[k, t], cdev))
+        remote(gd.at[t, :, 1 - c, spans[k]], land_c[k].at[t], gt.at[k], ht.at[k], cdev).start()
 
     for t in range(LINE):
         grad = dot_tn(act[1, :, t * 512 : t * 512 + 512], ds[1])
@@ -780,7 +818,9 @@
     grad_gm += hidden_back(1)
     attend_back(1)
     z_down.append(z_mid(1))
-    for copy in c_down + z_first:
+    for k in range(2):
+        left(parts[k](1 - c), gt.at[k], ht.at[k], cdev)
+    for copy in z_first:
         gone(copy)
     first_end()
     pl.semaphore_signal(free.at[0], inc=1, device_id=cdev, device_id_type=MESH)
@@ -914,6 +954,7 @@
     arrive(vr.at[4], sx.at[18], rx.at[18], xdev)
     v_all[4] = v_all[3] + vr[4]
     put(v_all.at[4], vec_out)
+    gathered()
     waited = x_swap + a_swap + d_swap + d2_swap + m_swap + d1_swap
     for copy in list(sent):
         if not any(copy is other for other in waited):
@@ -946,9 +987,9 @@
     get_vec = pltpu.make_async_copy(vec_hbm, vec_ref, pass_sem.at[0, 5])
     get_live.start()
     for i, t in tasks:
-        for copy in rows[2 * i : 2 * i + 2] if t == 0 else []:
-            copy.start()
         for a in range(2):
+            if t == 0:
+                rows[2 * i + a].start()
             gets[a, i, t] = pltpu.make_async_copy(part_of(whole[0][a], i, t), bases.at[a, i, t], get_sem.at[a, i, t])
             gets[a, i, t].start()
     through = ((fq_hbm, fq, fq_out), (fo_hbm, fo, fo_out), (fu_hbm, fu, fu_out), (fd_hbm, fd, fd_out))
@@ -996,8 +1037,6 @@
     half_q, half_u = w_qkv.shape[1] // 6, w_up.shape[1] // 2
     part, down = w_qkv.shape[0], w_down.shape[0]
     hbm = pl.BlockSpec(memory_space=pl.ANY)
-    vmem = pl.BlockSpec(memory_space=pltpu.VMEM)
-    smem = pl.BlockSpec(memory_space=pltpu.SMEM)
     sds, space, dma = jax.ShapeDtypeStruct, pltpu.VMEM, pltpu.SemaphoreType.DMA
     rows = (slots, ranks, model)
     grid = (LINE, 2, 2)
@@ -1016,7 +1055,7 @@
     upd, dxr, *sums, vec, live = pl.pallas_call(
         block_kernel,
         out_shape=(sds(rows, bf16), sds(rows, bf16)) + grad_shapes + (sds((8, model), f32), sds(routed.shape, jnp.int32)),
-        in_specs=[hbm] * 6 + [vmem] * 4 + [smem],
+        in_specs=[hbm] * 11,
         out_specs=[hbm] * 8,
         scratch_shapes=[
             space(wq_shape, bf16), space(wo_shape, bf16), space(wu_shape, bf16), space(wd_shape, bf16),
@@ -1034,15 +1073,16 @@
             space((part, model), bf16), space((part, half_q), bf16), space((part, half_u), bf16),
             space((part, model), bf16), space((part, half_q), bf16), space((part, half_u), bf16),
             space((8, model), f32), space((5, 8, model), f32), space((5, 8, model), f32), space(routed.shape, jnp.int32),
-            dma((16,)), dma((16,)), dma((8, 3)), dma((8, 3)), dma((8, 4)), dma((8, 4)), dma((8, 2)), dma((8, 2)),
-            dma((19,)), dma((19,)), dma((9,)), dma((9,)), dma((2, LINE)), dma((2, LINE)), dma((9,)), dma((9,)), dma((9, 3)), dma((9, 3)),
+            *[space((1, part), bf16)] * 3, space(routed.shape, jnp.int32), space((1, slots), jnp.int32),
+            dma((19,)), dma((15,)), dma((8,)), dma((8, 3)), dma((8,)), dma((8,)), dma((8,)), dma((8,)),
+            dma((19,)), dma((19,)), dma((9,)), dma((9,)), dma((2,)), dma((2,)), dma((9,)), dma((9,)), dma((9, 3)), dma((9, 3)),
             pltpu.SemaphoreType.REGULAR((2,)),
         ],
         compiler_params=pltpu.CompilerParams(collective_id=1, has_side_effects=True, vmem_limit_bytes=60 << 20),
         name="block",
     )(
         tokens.reshape(blocked), cotangent.reshape(blocked), w_qkv, w_out, w_up, w_down,
-        gain_attn[None], gain_mlp[None], router[None], routed, lengths,
+        gain_attn[None], gain_mlp[None], router[None], routed, lengths[None],
     )
 
     chunks = 2

time: 170 us -> 169 us (level)
    pallas_call x1, Pallas kernels: 162 us -> 160 us  [split_device(): pl.pallas_call(block_kernel, out_shape=(sds(rows, bf16), sds(rows, bf16))...]
where the time goes in v7:
time: 169 us; the launch traced here: 168 us
  Pallas kernels  168 us (99%)
    pallas_call x1, Pallas kernels, split_device(): pl.pallas_call(block_kernel, out_shape=(sds(rows, bf16), sds(rows, bf16))...  160 us
    pallas_call x1, Pallas kernels, split_device(): pl.pallas_call(rows_kernel, out_shape=(sds(tokens.shape, bf16), sds(token...  7.65 us

profile of v7, /device:TPU:0, one launch (start us, length us, event | category | flops | bytes accessed | tf_op | source)
XLA Modules:
  0.0 168.5 jit_solution(6314129292981297184)
XLA Ops:
  0.6 160.0 %block.1 = (bf16[2,256,1024]{2,1,0:T(8,128)(2,1)}, bf16[2,256,1024]{2,1,0:T(8,128)(2,1)}, f32[32,3072]{1,0:T(8,128)}, f32[32,1024]{1,0:T(8,128)}, f32[32,4096]{1...) custom-call(bf16[2,2,2,2,128,1024]{5,4,3,2,1,0:T(8,128)(2,1)} %bitcast.9, ...), custom_call_target="tpu_custom_call" | custom-call | tf_op jit(solution)/shard_map/block/pallas_call | solution.py:1055
  160.6 7.7 %rows.1 = (bf16[2,1024,1024]{2,1,0:T(8,128)(2,1)}, bf16[2,1024,1024]{2,1,0:T(8,128)(2,1)}, f32[32,3072]{1,0:T(8,128)}, f32[32,1024]{1,0:T(8,128)}, f32[32,4096]{...) custom-call(bf16[2,1024,1024]{2,1,0:T(8,128)(2,1)} %tok_hbm.1, ...), custom_call_target="tpu_custom_call" | custom-call | tf_op jit(solution)/shard_map/rows/pallas_call | solution.py:1090

commit v8 on v7

--- a/solution.py
+++ b/solution.py
@@ -499,15 +499,15 @@
 
     for copy in small_in:
         copy.wait()
-    lane = lax.broadcasted_iota(jnp.int32, (part, model), 1)
-    fits = (lax.rem(lane, part) == lax.broadcasted_iota(jnp.int32, (part, model), 0)) & (
-        lane // part == s * 4 * LINE + z * 4 + y * 2 + c
+    fits = lax.broadcasted_iota(jnp.int32, (part, model), 1) == s * part + lax.broadcasted_iota(
+        jnp.int32, (part, model), 0
     )
     line = lax.broadcasted_iota(jnp.int32, (16, part), 0)
     small = jnp.zeros((16, part), f32)
     for j, ref in enumerate((one_ref, two_ref, three_ref)):
         small = jnp.where(line == j, ref[...].astype(f32), small)
-    stv[...] = dot_nn(small.astype(bf16), jnp.where(fits, 1.0, 0.0).astype(bf16)).astype(bf16)
+    gains[...] = dot_nn(small.astype(bf16), jnp.where(fits, 1.0, 0.0).astype(bf16))
+    stv[...] = gains[:, 0:128].astype(bf16)
 
     rank = lax.broadcasted_iota(jnp.int32, (1, ranks), 1)
 
@@ -601,7 +601,14 @@
     spread_y(D_0)
     after_c(Q_SWAP)
 
-    gains[...] = jnp.sum(gv[...].astype(f32).reshape(4 * LINE, 16, model), axis=0)
+    group = lax.broadcasted_iota(jnp.int32, (16, 128), 1) // part
+    for q in range(LINE):
+        for i in range(2):
+            tile = jnp.zeros((16, 128), f32)
+            for j in range(4):
+                moved = pltpu.roll(gv[q, j // 2, j % 2].astype(f32), (j - i) * part % 128, 1)
+                tile = jnp.where(group == j, moved, tile)
+            gains[:, i * half + q * 128 : i * half + (q + 1) * 128] = tile
     gain_one, gain_two, router = gains[0:1], gains[1:2], gains[2:3]
 
     def enter(i):
@@ -859,8 +866,8 @@
     swap_1, sums_1 = inner_back(1)
     d1_swap = [swap_0, swap_1]
     for j in range(2):
-        vs[0:1, j * half : (j + 1) * half] = sums_0[j] + sums_1[j]
-    vs[1:2] = grad_gm
+        gains[8:9, j * half : (j + 1) * half] = sums_0[j] + sums_1[j]
+    gains[9:10] = grad_gm
     pl.semaphore_wait(free.at[1], 4)
     c_start(6)
     c_start(7)
@@ -880,8 +887,10 @@
         logit[i] = slope
         grad_router += jnp.sum(row * slope, axis=0, keepdims=True)
     put(m_s, upd_out)
-    vs[2:3] = 0.5 * grad_router
-    vs[3:8] = jnp.zeros((5, model), f32)
+    gains[10:11] = 0.5 * grad_router
+    for j in range(3):
+        for t in range(model // 128):
+            vs[8 * j + t : 8 * j + t + 1] = gains[8 + j : 9 + j, t * 128 : (t + 1) * 128]
     send(vs, vr.at[0], gc.at[8], hc.at[8], cdev)
     z_mid(3)
     arrive(vr.at[0], gc.at[8], hc.at[8], cdev)
@@ -1016,12 +1025,13 @@
     part = one.shape[1]
     get_vec.wait()
     flat = s * lax.axis_size("batch") + lax.axis_index("batch")
-    lane = lax.broadcasted_iota(jnp.int32, (part, model), 1)
-    row = lax.broadcasted_iota(jnp.int32, (part, model), 0)
-    here = (lane // part == flat) & (lax.rem(lane, part) == row)
+    each = 128 // part
+    lane = lax.broadcasted_iota(jnp.int32, (part, 128), 1)
+    here = lane == lax.rem(flat, each) * part + lax.broadcasted_iota(jnp.int32, (part, 128), 0)
     eye = lax.broadcasted_iota(jnp.int32, (part, part), 0) == lax.broadcasted_iota(jnp.int32, (part, part), 1)
     for j, (ref, dst) in enumerate(((one, one_out), (two, two_out), (three, three_out))):
-        column = jnp.sum(jnp.where(here, vec_ref[j : j + 1], 0.0), axis=1, keepdims=True)
+        line = vec_ref[pl.ds(8 * j + flat // each, 1)]
+        column = jnp.sum(jnp.where(here, line, 0.0), axis=1, keepdims=True)
         ref[...] = jnp.sum(jnp.where(eye, column, 0.0), axis=0, keepdims=True)
         puts.append(pltpu.make_async_copy(ref, dst, pass_sem.at[1, 4 + j]))
         puts[-1].start()
@@ -1054,13 +1064,13 @@
     )
     upd, dxr, *sums, vec, live = pl.pallas_call(
         block_kernel,
-        out_shape=(sds(rows, bf16), sds(rows, bf16)) + grad_shapes + (sds((8, model), f32), sds(routed.shape, jnp.int32)),
+        out_shape=(sds(rows, bf16), sds(rows, bf16)) + grad_shapes + (sds((24, 128), f32), sds(routed.shape, jnp.int32)),
         in_specs=[hbm] * 11,
         out_specs=[hbm] * 8,
         scratch_shapes=[
             space(wq_shape, bf16), space(wo_shape, bf16), space(wu_shape, bf16), space(wd_shape, bf16),
-            space(grid + (16, model), bf16),
-            space((part, 3 * half_q), bf16), space((part, half_u), bf16), space((16, model), bf16), space((16, model), bf16),
+            space(grid + (16, 128), bf16),
+            space((part, 3 * half_q), bf16), space((part, half_u), bf16), space((16, 128), bf16), space((16, 128), bf16),
             *[row_bf16] * 11, space(rows, f32), space(rows, f32),
             space((slots, ranks, 3 * half_q), bf16), space((slots, ranks, half_q), bf16),
             space((slots, ranks, half_u), bf16), space((slots, ranks, half_u), bf16),
@@ -1072,7 +1082,7 @@
             space((2, part, half_u), f32), space((down, model), f32),
             space((part, model), bf16), space((part, half_q), bf16), space((part, half_u), bf16),
             space((part, model), bf16), space((part, half_q), bf16), space((part, half_u), bf16),
-            space((8, model), f32), space((5, 8, model), f32), space((5, 8, model), f32), space(routed.shape, jnp.int32),
+            space((24, 128), f32), space((5, 24, 128), f32), space((5, 24, 128), f32), space(routed.shape, jnp.int32),
             *[space((1, part), bf16)] * 3, space(routed.shape, jnp.int32), space((1, slots), jnp.int32),
             dma((19,)), dma((15,)), dma((8,)), dma((8, 3)), dma((8,)), dma((8,)), dma((8,)), dma((8,)),
             dma((19,)), dma((19,)), dma((9,)), dma((9,)), dma((2,)), dma((2,)), dma((9,)), dma((9,)), dma((9, 3)), dma((9, 3)),
@@ -1095,7 +1105,7 @@
         scratch_shapes=[
             space((2, slots, chunks, local_len // chunks, model), bf16), space((2,) + rows, bf16),
             *[space(g.shape, f32) for g in grad_shapes],
-            space((8, model), f32), space(routed.shape, jnp.int32), *[space((1, part), f32)] * 3,
+            space((24, 128), f32), space(routed.shape, jnp.int32), *[space((1, part), f32)] * 3,
             dma((2, slots, chunks)), dma((2, slots, chunks)), dma((2, slots)), dma((2, 7)),
         ],
         compiler_params=pltpu.CompilerParams(vmem_limit_bytes=60 << 20),

time: 169 us -> 166 us (0.982)
  Pallas kernels: 168 us -> 165 us
    pallas_call x1, Pallas kernels: 160 us -> 158 us  [split_device(): pl.pallas_call(block_kernel, out_shape=(sds(rows, bf16), sds(rows, bf16))...]
where the time goes in v8:
time: 166 us
  Pallas kernels  165 us (99%)
    pallas_call x1, Pallas kernels, split_device(): pl.pallas_call(block_kernel, out_shape=(sds(rows, bf16), sds(rows, bf16))...  158 us
    pallas_call x1, Pallas kernels, split_device(): pl.pallas_call(rows_kernel, out_shape=(sds(tokens.shape, bf16), sds(token...  7.65 us

profile of v8, /device:TPU:0, one launch (start us, length us, event | category | flops | bytes accessed | tf_op | source)
XLA Modules:
  0.0 166.3 jit_solution(3803738928653953882)
XLA Ops:
  0.6 157.8 %block.1 = (bf16[2,256,1024]{2,1,0:T(8,128)(2,1)}, bf16[2,256,1024]{2,1,0:T(8,128)(2,1)}, f32[32,3072]{1,0:T(8,128)}, f32[32,1024]{1,0:T(8,128)}, f32[32,4096]{1...) custom-call(bf16[2,2,2,2,128,1024]{5,4,3,2,1,0:T(8,128)(2,1)} %bitcast.9, ...), custom_call_target="tpu_custom_call" | custom-call | tf_op jit(solution)/shard_map/block/pallas_call | solution.py:1065
  158.4 7.7 %rows.1 = (bf16[2,1024,1024]{2,1,0:T(8,128)(2,1)}, bf16[2,1024,1024]{2,1,0:T(8,128)(2,1)}, f32[32,3072]{1,0:T(8,128)}, f32[32,1024]{1,0:T(8,128)}, f32[32,4096]{...) custom-call(bf16[2,1024,1024]{2,1,0:T(8,128)(2,1)} %tok_hbm.1, ...), custom_call_target="tpu_custom_call" | custom-call | tf_op jit(solution)/shard_map/rows/pallas_call | solution.py:1100

commit v9 on v8

--- a/solution.py
+++ b/solution.py
@@ -451,10 +451,9 @@
 
         lax.fori_loop(0, LINE, add, 0)
         if k == 0:
-            return [
-                send(ref.at[LINE - 1 - near], rzb.at[1], gz.at[k, 1], hz.at[k, 1], ndev),
-                send(ref.at[near], rzb.at[0], gz.at[k, 0], hz.at[k, 0], ndev),
-            ]
+            remote(ref.at[LINE - 1 - near], rzb.at[1], gz.at[k], hz.at[k, 1], ndev).start()
+            remote(ref.at[near], rzb.at[0], gz.at[k], hz.at[k, 0], ndev).start()
+            return []
         return [send(ref.at[:, 1 - y], land_y[k], gy.at[k], hy.at[k], ydev)]
 
     def y_end(k):
@@ -466,30 +465,28 @@
             return carry
 
         lax.fori_loop(0, LINE, add, 0)
-        return [
-            send(ref.at[LINE - 1 - near], land_z[k].at[1], gz.at[k, 1], hz.at[k, 1], ndev),
-            send(ref.at[near], land_z[k].at[0], gz.at[k, 0], hz.at[k, 0], ndev),
-        ]
+        remote(ref.at[LINE - 1 - near], land_z[k].at[1], gz.at[k], hz.at[k, 1], ndev).start()
+        remote(ref.at[near], land_z[k].at[0], gz.at[k], hz.at[k, 0], ndev).start()
 
     def z_mid(k):
         ref = land_z[k].at[1]
-        arrive(ref, gz.at[k, 1], hz.at[k, 1], ndev)
+        arrive(ref, gz.at[k], hz.at[k, 1], ndev)
         ref[...] = (ref[...].astype(f32) + land_y[k][far].astype(f32)).astype(bf16)
-        return send(ref, land_z[k].at[2], gz.at[k, 2], hz.at[k, 2], fdev)
+        remote(ref, land_z[k].at[2], gz.at[k], hz.at[k, 2], fdev).start()
 
     def z_end(k):
-        arrive(land_z[k].at[0], gz.at[k, 0], hz.at[k, 0], ndev)
-        arrive(land_z[k].at[2], gz.at[k, 2], hz.at[k, 2], fdev)
+        arrive(land_z[k].at[0], gz.at[k], hz.at[k, 0], ndev)
+        arrive(land_z[k].at[2], gz.at[k], hz.at[k, 2], fdev)
         return land_y[k][z].astype(f32) + land_z[k][0].astype(f32) + land_z[k][2].astype(f32)
 
     def first_mid():
-        arrive(rzb.at[1], gz.at[0, 1], hz.at[0, 1], ndev)
+        arrive(rzb.at[1], gz.at[0], hz.at[0, 1], ndev)
         rzb[1] = (rzb[1].astype(f32) + land_c[0][far].astype(f32)).astype(bf16)
-        return send(rzb.at[1], rzb.at[2], gz.at[0, 2], hz.at[0, 2], fdev)
+        remote(rzb.at[1], rzb.at[2], gz.at[0], hz.at[0, 2], fdev).start()
 
     def first_end():
-        arrive(rzb.at[0], gz.at[0, 0], hz.at[0, 0], ndev)
-        arrive(rzb.at[2], gz.at[0, 2], hz.at[0, 2], fdev)
+        arrive(rzb.at[0], gz.at[0], hz.at[0, 0], ndev)
+        arrive(rzb.at[2], gz.at[0], hz.at[0, 2], fdev)
         rzb[0] = (land_c[0][z].astype(f32) + rzb[0].astype(f32) + rzb[2].astype(f32)).astype(bf16)
         return send(rzb.at[0, 1 - y], ryb, gy.at[0], hy.at[0], ydev)
 
@@ -742,7 +739,7 @@
     for t in range(LINE):
         c_tile(t, 0)
     y_down = c_end(1)
-    z_first = c_end(0)
+    c_end(0)
     d2_swap.append(mlp_back(1))
     mlp_out(0)
     m_swap = [mlp_send(0)]
@@ -819,16 +816,15 @@
     c_end(2)
     attend_back(0)
     c_end(3)
-    z_first.append(first_mid())
+    first_mid()
     swap_0, sums_0 = inner_back(0)
-    z_down = y_end(1)
+    y_end(1)
     grad_gm += hidden_back(1)
     attend_back(1)
-    z_down.append(z_mid(1))
+    z_mid(1)
     for k in range(2):
         left(parts[k](1 - c), gt.at[k], ht.at[k], cdev)
-    for copy in z_first:
-        gone(copy)
+    left(rzb, gz.at[0], hz.at[0, 0], ndev)
     first_end()
     pl.semaphore_signal(free.at[0], inc=1, device_id=cdev, device_id_type=MESH)
     y_end(2)
@@ -855,8 +851,9 @@
     c_start(5)
     qkv_tile(2)
     fd[2 * part :] = z_end(1)
-    for copy in y_down + z_down:
+    for copy in y_down:
         gone(copy)
+    left(land_z[1], gz.at[1], hz.at[1, 0], ndev)
     for target in (ydev, cdev, ndev, fdev):
         pl.semaphore_signal(free.at[1], inc=1, device_id=target, device_id_type=MESH)
     out_tile(0)
@@ -895,7 +892,7 @@
     z_mid(3)
     arrive(vr.at[0], gc.at[8], hc.at[8], cdev)
     v_all[0] = vs[...] + vr[0]
-    send(v_all.at[0], vr.at[1], gz.at[8, 0], hz.at[8, 0], ndev)
+    send(v_all.at[0], vr.at[1], gz.at[8], hz.at[8, 0], ndev)
     c_end(7)
     fd[0 : 2 * part] = first_sum()
     put(fd, fd_out)
@@ -904,9 +901,9 @@
     suu[...] = fu[1 - s].astype(bf16)
     send(suu, ruu, sx.at[15], rx.at[15], xdev)
     put(fu.at[s], fu_out.at[:, pl.ds(s * half_u, half_u)])
-    arrive(vr.at[1], gz.at[8, 0], hz.at[8, 0], ndev)
+    arrive(vr.at[1], gz.at[8], hz.at[8, 0], ndev)
     v_all[1] = v_all[0] + vr[1]
-    send(v_all.at[1], vr.at[2], gz.at[8, 1], hz.at[8, 1], fdev)
+    send(v_all.at[1], vr.at[2], gz.at[9], hz.at[8, 1], fdev)
     z_mid(4)
     y_end(5)
 
@@ -920,7 +917,7 @@
         put(d2s.at[i], dx_out.at[i])
 
     rows_back(0)
-    arrive(vr.at[2], gz.at[8, 1], hz.at[8, 1], fdev)
+    arrive(vr.at[2], gz.at[9], hz.at[8, 1], fdev)
     v_all[2] = v_all[1] + vr[2]
     send(v_all.at[2], vr.at[3], gy.at[8], hy.at[8], ydev)
     z_mid(5)
@@ -964,6 +961,8 @@
     v_all[4] = v_all[3] + vr[4]
     put(v_all.at[4], vec_out)
     gathered()
+    for k in range(2, 8):
+        left(land_z[k], gz.at[k], hz.at[k, 0], ndev)
     waited = x_swap + a_swap + d_swap + d2_swap + m_swap + d1_swap
     for copy in list(sent):
         if not any(copy is other for other in waited):
@@ -1008,7 +1007,7 @@
         copy.start()
     get_live.wait()
     for n, (i, t) in enumerate(tasks):
-        if n == len(tasks) - 2:
+        if n == len(tasks) - 1:
             for j in range(4):
                 taken[j].wait()
                 passed[j].start()
@@ -1085,7 +1084,7 @@
             space((24, 128), f32), space((5, 24, 128), f32), space((5, 24, 128), f32), space(routed.shape, jnp.int32),
             *[space((1, part), bf16)] * 3, space(routed.shape, jnp.int32), space((1, slots), jnp.int32),
             dma((19,)), dma((15,)), dma((8,)), dma((8, 3)), dma((8,)), dma((8,)), dma((8,)), dma((8,)),
-            dma((19,)), dma((19,)), dma((9,)), dma((9,)), dma((2,)), dma((2,)), dma((9,)), dma((9,)), dma((9, 3)), dma((9, 3)),
+            dma((19,)), dma((19,)), dma((9,)), dma((9,)), dma((2,)), dma((2,)), dma((9,)), dma((9,)), dma((10,)), dma((9, 3)),
             pltpu.SemaphoreType.REGULAR((2,)),
         ],
         compiler_params=pltpu.CompilerParams(collective_id=1, has_side_effects=True, vmem_limit_bytes=60 << 20),

time: 166 us -> 166 us (level)
  no operation moved by 1% of the time
where the time goes in v9:
time: 166 us
  Pallas kernels  165 us (99%)
    pallas_call x1, Pallas kernels, split_device(): pl.pallas_call(block_kernel, out_shape=(sds(rows, bf16), sds(rows, bf16))...  158 us
    pallas_call x1, Pallas kernels, split_device(): pl.pallas_call(rows_kernel, out_shape=(sds(tokens.shape, bf16), sds(token...  7.68 us

profile of v9, /device:TPU:0, one launch (start us, length us, event | category | flops | bytes accessed | tf_op | source)
XLA Modules:
  0.0 166.2 jit_solution(16034827588810460009)
XLA Ops:
  0.6 157.7 %block.1 = (bf16[2,256,1024]{2,1,0:T(8,128)(2,1)}, bf16[2,256,1024]{2,1,0:T(8,128)(2,1)}, f32[32,3072]{1,0:T(8,128)}, f32[32,1024]{1,0:T(8,128)}, f32[32,4096]{1...) custom-call(bf16[2,2,2,2,128,1024]{5,4,3,2,1,0:T(8,128)(2,1)} %bitcast.9, ...), custom_call_target="tpu_custom_call" | custom-call | tf_op jit(solution)/shard_map/block/pallas_call | solution.py:1064
  158.3 7.7 %rows.1 = (bf16[2,1024,1024]{2,1,0:T(8,128)(2,1)}, bf16[2,1024,1024]{2,1,0:T(8,128)(2,1)}, f32[32,3072]{1,0:T(8,128)}, f32[32,1024]{1,0:T(8,128)}, f32[32,4096]{...) custom-call(bf16[2,1024,1024]{2,1,0:T(8,128)(2,1)} %tok_hbm.1, ...), custom_call_target="tpu_custom_call" | custom-call | tf_op jit(solution)/shard_map/rows/pallas_call | solution.py:1099

commit v10 on v9

--- a/solution.py
+++ b/solution.py
@@ -933,11 +933,11 @@
     send(sqk, rqk, sx.at[16], rx.at[16], xdev)
     for j in range(2):
         put(fqk.at[s, :, pl.ds(j * half_q, half_q)], fq_out.at[:, pl.ds(2 * j * half_q + s * half_q, half_q)])
+    z_mid(7)
     fv[...] = z_end(6)
     sv[...] = fv[:, pl.ds((1 - s) * half_q, half_q)].astype(bf16)
     send(sv, rv, sx.at[17], rx.at[17], xdev)
     put(fv.at[:, pl.ds(s * half_q, half_q)], fq_out.at[:, pl.ds(4 * half_q + s * half_q, half_q)])
-    z_mid(7)
     rows_back(1)
     arrive(ruu, sx.at[15], rx.at[15], xdev)
     fu[1 - s] = ruu[...].astype(f32)

time: 166 us -> 166 us (level)
  no operation moved by 1% of the time
where the time goes in v10:
time: 166 us
  Pallas kernels  165 us (99%)
    pallas_call x1, Pallas kernels, split_device(): pl.pallas_call(block_kernel, out_shape=(sds(rows, bf16), sds(rows, bf16))...  158 us
    pallas_call x1, Pallas kernels, split_device(): pl.pallas_call(rows_kernel, out_shape=(sds(tokens.shape, bf16), sds(token...  7.68 us

profile of v10, /device:TPU:0, one launch (start us, length us, event | category | flops | bytes accessed | tf_op | source)
XLA Modules:
  0.0 166.2 jit_solution(10251771487452564602)
XLA Ops:
  0.6 157.7 %block.1 = (bf16[2,256,1024]{2,1,0:T(8,128)(2,1)}, bf16[2,256,1024]{2,1,0:T(8,128)(2,1)}, f32[32,3072]{1,0:T(8,128)}, f32[32,1024]{1,0:T(8,128)}, f32[32,4096]{1...) custom-call(bf16[2,2,2,2,128,1024]{5,4,3,2,1,0:T(8,128)(2,1)} %bitcast.9, ...), custom_call_target="tpu_custom_call" | custom-call | tf_op jit(solution)/shard_map/block/pallas_call | solution.py:1064
  158.3 7.7 %rows.1 = (bf16[2,1024,1024]{2,1,0:T(8,128)(2,1)}, bf16[2,1024,1024]{2,1,0:T(8,128)(2,1)}, f32[32,3072]{1,0:T(8,128)}, f32[32,1024]{1,0:T(8,128)}, f32[32,4096]{...) custom-call(bf16[2,1024,1024]{2,1,0:T(8,128)(2,1)} %tok_hbm.1, ...), custom_call_target="tpu_custom_call" | custom-call | tf_op jit(solution)/shard_map/rows/pallas_call | solution.py:1099
